TPU v7x, 32 devices: a whole 2x2x4 slice. The times are simulated.
32 devices in a mesh: group: 4 (over x, core), dp: 2 (over y), mp: 4 (over z).
Axes of the slice: x: 2, y: 2, z: 4, core: 2. Of those that a mesh axis runs over, the one named last changes fastest.
Arguments:
- hidden_in: bfloat16 [8, 2048, 768], P(('group', 'dp'), 'mp'), may hold values from -6 to 6
- doc_ids: int32 [8, 2048], P(('group', 'dp'), 'mp'), may hold values from 0 to 2, as said below
- out_cotangent: bfloat16 [8, 2048, 768], P(('group', 'dp'), 'mp'), may hold values from -6 to 6
- entry_weight: float32 [4, 768, 3840], P('group', 'dp', 'mp')
- entry_first: float32 [4, 768, 3840], P('group', 'dp', 'mp')
- entry_second: float32 [4, 768, 3840], P('group', 'dp', 'mp'), as said below
- entry_anchor: float32 [768, 3840], P('dp', 'mp')
- entry_velocity: float32 [768, 3840], P('dp', 'mp')
- exit_weight: float32 [4, 3840, 768], P('group', 'mp', 'dp')
- exit_first: float32 [4, 3840, 768], P('group', 'mp', 'dp')
- exit_second: float32 [4, 3840, 768], P('group', 'mp', 'dp'), as said below
- exit_anchor: float32 [3840, 768], P('mp', 'dp')
- exit_velocity: float32 [3840, 768], P('mp', 'dp')
- shared_weight: float32 [4, 768, 128], P('group', ('dp', 'mp')), may hold values from -0.21875 to 0.21875
- shared_first: float32 [4, 768, 128], P('group', ('dp', 'mp'))
- shared_second: float32 [4, 768, 128], P('group', ('dp', 'mp')), as said below
- shared_anchor: float32 [768, 128], P(('dp', 'mp')), may hold values from -0.21875 to 0.21875
- shared_velocity: float32 [768, 128], P(('dp', 'mp'))
- vector_weight: float32 [4, 8576], P('group')
- vector_first: float32 [4, 8576], P('group')
- vector_second: float32 [4, 8576], P('group'), as said below
- vector_anchor: float32 [8576], replicated
- vector_velocity: float32 [8576], replicated
Outputs:
- block_output: float32 [8, 2048, 768], P(('group', 'dp'), 'mp')
- input_grad: float32 [8, 2048, 768], P(('group', 'dp'), 'mp')
- entry_moment: float32 [4, 768, 3840], P('group', 'dp', 'mp')
- entry_square: float32 [4, 768, 3840], P('group', 'dp', 'mp')
- entry_local: float32 [4, 768, 3840], P('group', 'dp', 'mp')
- entry_change: float32 [768, 3840], P('dp', 'mp')
- entry_momentum: float32 [768, 3840], P('dp', 'mp')
- entry_global: float32 [768, 3840], P('dp', 'mp')
- exit_moment: float32 [4, 3840, 768], P('group', 'mp', 'dp')
- exit_square: float32 [4, 3840, 768], P('group', 'mp', 'dp')
- exit_local: float32 [4, 3840, 768], P('group', 'mp', 'dp')
- exit_change: float32 [3840, 768], P('mp', 'dp')
- exit_momentum: float32 [3840, 768], P('mp', 'dp')
- exit_global: float32 [3840, 768], P('mp', 'dp')
- shared_moment: float32 [4, 768, 128], P('group', ('dp', 'mp'))
- shared_square: float32 [4, 768, 128], P('group', ('dp', 'mp'))
- shared_local: float32 [4, 768, 128], P('group', ('dp', 'mp'))
- shared_change: float32 [768, 128], P(('dp', 'mp'))
- shared_momentum: float32 [768, 128], P(('dp', 'mp'))
- shared_global: float32 [768, 128], P(('dp', 'mp'))
- vector_moment: float32 [4, 8576], P('group')
- vector_square: float32 [4, 8576], P('group')
- vector_local: float32 [4, 8576], P('group')
- vector_change: float32 [8576], replicated
- vector_momentum: float32 [8576], replicated
- vector_global: float32 [8576], replicated
Inputs may be any that keep to these rules, and one draw needn't show every extreme that they name: `doc_ids`: each row's ids do not fall, start at 0 and end at 2; document 1 begins before position 256 and its last position is at or after 7 * 256. `entry_second`: second moments are positive. `exit_second`: second moments are positive. `shared_second`: second moments are positive. `vector_second`: second moments are positive.
All inputs are finite; a program needn't handle non-finite values.
Results may differ from a plain program's by a relative error of at most 0.004.
The roundings to bfloat16 on the way count: a program that leaves them out, or rounds other values in their place, can miss the bound.
Values may be sent and summed in bfloat16 or wider, within the bound.
A program may use at most 192 MiB of HBM per device.

v0:
```python
import math

import jax
import jax.numpy as jnp
from jax import lax
from jax.sharding import PartitionSpec as P

D = 768
HEADS = 12
HS = 64
ROT = 16
STEP = 5
IN_COLS = 3840


NORM_EPS = 1e-05
BETA_ONE = 0.9
BETA_TWO = 0.95
ADAM_EPS = 1e-08
MATRIX_RATE = 0.03
MATRIX_DECAY = 0.1
VECTOR_RATE = 0.3
OUTER_RATE = 0.7
OUTER_BETA = 0.9


def layer_norm(inputs, gain, shift):
    centered = inputs - jnp.mean(inputs, -1, keepdims=True)
    spread = jnp.mean(centered * centered, -1, keepdims=True)
    return centered * lax.rsqrt(spread + NORM_EPS) * gain + shift


def rotation_tables(length):
    half_width = ROT // 2
    positions = jnp.arange(length).astype(jnp.float32)
    frequency = 10000.0 ** (-(jnp.arange(half_width).astype(jnp.float32) * 2.0 / ROT))
    angles = positions[:, None] * frequency[None, :]
    cosine_table = jnp.concatenate([jnp.cos(angles), jnp.cos(angles)], -1)[:, None, :]
    sine_table = jnp.concatenate([jnp.sin(angles), jnp.sin(angles)], -1)[:, None, :]
    return (cosine_table, sine_table)


def rotate(tensor, cosine_table, sine_table):
    half_width = ROT // 2
    leading = tensor[..., :ROT]
    turned = jnp.concatenate([-leading[..., half_width:], leading[..., :half_width]], -1)
    return jnp.concatenate([leading * cosine_table + turned * sine_table, tensor[..., ROT:]], -1)


def masked_scores(query_rows, rotated_keys, query_ids, key_ids, offset):
    block_rows = query_rows.shape[0]
    length = rotated_keys.shape[0]
    scores = jnp.einsum("qhd,kd->hqk", query_rows, rotated_keys, preferred_element_type=jnp.float32)
    scores = scores * (1.0 / math.sqrt(HS))
    query_pos = offset + jnp.arange(block_rows)
    key_pos = jnp.arange(length)
    allowed = (key_pos[None, :] <= query_pos[:, None]) & (query_ids[:, None] == key_ids[None, :])
    return jnp.where(allowed[None], scores, -1000000000.0)


def attend_forward(record):
    rotated_queries, rotated_keys, values, key_ids = record
    length = rotated_keys.shape[0]
    block_rows = min(512, length)
    number = length // block_rows

    def one_block(position):
        offset = position * block_rows
        query_rows = lax.dynamic_slice_in_dim(rotated_queries, offset, block_rows, 0)
        query_ids = lax.dynamic_slice_in_dim(key_ids, offset, block_rows, 0)
        scores = masked_scores(query_rows, rotated_keys, query_ids, key_ids, offset)
        highest = jnp.max(scores, -1, keepdims=True)
        exponent = jnp.exp(scores - highest)
        total = jnp.sum(exponent, -1, keepdims=True)
        softmax = (exponent / total).astype(jnp.bfloat16)
        mixed = jnp.einsum("hqk,kd->qhd", softmax, values, preferred_element_type=jnp.float32)
        return (mixed.astype(jnp.bfloat16), (highest + jnp.log(total))[..., 0])

    mixed, log_total = lax.map(one_block, jnp.arange(number))
    return (mixed.reshape(length, mixed.shape[2], HS), log_total)


def attend_backward(record):
    rotated_queries, rotated_keys, values, key_ids, log_total, mixed_grad = record
    length = rotated_keys.shape[0]
    block_rows = min(512, length)
    number = length // block_rows
    score_scale = 1.0 / math.sqrt(HS)

    def one_step(running, position):
        key_grad, value_grad = running
        offset = position * block_rows
        query_rows = lax.dynamic_slice_in_dim(rotated_queries, offset, block_rows, 0)
        grad_rows = lax.dynamic_slice_in_dim(mixed_grad, offset, block_rows, 0)
        query_ids = lax.dynamic_slice_in_dim(key_ids, offset, block_rows, 0)
        scores = masked_scores(query_rows, rotated_keys, query_ids, key_ids, offset)
        softmax = jnp.exp(scores - log_total[position][..., None])
        prob_grad = jnp.einsum("qhd,kd->hqk", grad_rows, values, preferred_element_type=jnp.float32)
        inner = jnp.sum(softmax * prob_grad, -1, keepdims=True)
        score_grad = (softmax * (prob_grad - inner) * score_scale).astype(jnp.bfloat16)
        query_grad = jnp.einsum(
            "hqk,kd->qhd", score_grad, rotated_keys, preferred_element_type=jnp.float32
        )
        key_grad = key_grad + jnp.einsum(
            "hqk,qhd->kd", score_grad, query_rows, preferred_element_type=jnp.float32
        )
        value_grad = value_grad + jnp.einsum(
            "hqk,qhd->kd",
            softmax.astype(jnp.bfloat16),
            grad_rows,
            preferred_element_type=jnp.float32,
        )
        return ((key_grad, value_grad), query_grad)

    blank_grads = jnp.zeros((length, HS), jnp.float32)
    (key_grad, value_grad), query_grad = lax.scan(
        one_step, (blank_grads, blank_grads), jnp.arange(number)
    )
    return (query_grad.reshape(length, query_grad.shape[2], HS), key_grad, value_grad)


def adamw_update(weight, first, second, gradient, step_rate, decay):
    first_new = BETA_ONE * first + (1.0 - BETA_ONE) * gradient
    second_new = BETA_TWO * second + (1.0 - BETA_TWO) * gradient * gradient
    fix_first = 1.0 - BETA_ONE**STEP
    fix_second = 1.0 - BETA_TWO**STEP
    update = first_new / fix_first / (jnp.sqrt(second_new / fix_second) + ADAM_EPS)
    return (first_new, second_new, weight - step_rate * (update + decay * weight))


def shards(
    hidden_in,
    doc_ids,
    out_cotangent,
    entry_weight,
    entry_first,
    entry_second,
    entry_anchor,
    entry_velocity,
    exit_weight,
    exit_first,
    exit_second,
    exit_anchor,
    exit_velocity,
    shared_weight,
    shared_first,
    shared_second,
    shared_anchor,
    shared_velocity,
    vector_weight,
    vector_first,
    vector_second,
    vector_anchor,
    vector_velocity,
):
    batch = hidden_in.shape[0]
    local_len = hidden_in.shape[1]
    model_parts = lax.axis_size("mp")
    rank = lax.axis_index("mp")
    length = local_len * model_parts
    part_width = entry_weight.shape[2]
    query_width = HEADS * HS // model_parts
    vector = vector_weight[0]
    gain_one, shift_one = (vector[0:D], vector[D : 2 * D])
    gain_two, shift_two = (vector[2 * D : 3 * D], vector[3 * D : 4 * D])
    out_bias = vector[4 * D : 5 * D] + vector[5 * D : 6 * D]
    pair_bias = vector[6 * D : 6 * D + 2 * HS]
    in_bias = lax.dynamic_slice_in_dim(vector, 6 * D + 2 * HS + rank * part_width, part_width, 0)
    query_bias = in_bias[:query_width]
    up_bias = in_bias[query_width:]
    entry_rows, exit_rows = (
        lax.all_gather(entry_weight[0].astype(jnp.bfloat16), "dp", axis=0, tiled=True),
        lax.all_gather(exit_weight[0].astype(jnp.bfloat16), "dp", axis=1, tiled=True),
    )
    pair_weight = lax.all_gather(
        shared_weight[0].astype(jnp.bfloat16), ("dp", "mp"), axis=0, tiled=True
    )
    query_weight = entry_rows[:, :query_width]
    up_weight = entry_rows[:, query_width:]
    attend_weight = exit_rows[:query_width]
    down_weight = exit_rows[query_width:]
    cosine_table, sine_table = rotation_tables(length)
    local_inputs = hidden_in.astype(jnp.float32)
    attn_local = layer_norm(local_inputs, gain_one, shift_one).astype(jnp.bfloat16)
    ffn_local = layer_norm(local_inputs, gain_two, shift_two).astype(jnp.bfloat16)
    attn_input, ffn_input, key_ids = (
        lax.all_gather(attn_local, "mp", axis=1, tiled=True),
        lax.all_gather(ffn_local, "mp", axis=1, tiled=True),
        lax.all_gather(doc_ids, "mp", axis=1, tiled=True),
    )
    queries = (
        jnp.einsum("bsd,dq->bsq", attn_input, query_weight, preferred_element_type=jnp.float32)
        + query_bias
    )
    queries = queries.reshape(batch, length, query_width // HS, HS)
    rotated_queries = rotate(queries, cosine_table, sine_table).astype(jnp.bfloat16)
    pairs = (
        jnp.einsum("bsd,dc->bsc", attn_input, pair_weight, preferred_element_type=jnp.float32)
        + pair_bias
    )
    rotated_keys = rotate(pairs[:, :, None, :HS], cosine_table, sine_table)[:, :, 0].astype(
        jnp.bfloat16
    )
    values = pairs[:, :, HS:].astype(jnp.bfloat16)
    hidden_pre = (
        jnp.einsum("bsd,df->bsf", ffn_input, up_weight, preferred_element_type=jnp.float32)
        + up_bias
    )
    hidden = jax.nn.gelu(hidden_pre, approximate=False).astype(jnp.bfloat16)
    attended, log_total = lax.map(attend_forward, (rotated_queries, rotated_keys, values, key_ids))
    attended = attended.reshape(batch, length, query_width)
    partial_sum = jnp.einsum(
        "bsq,qd->bsd", attended, attend_weight, preferred_element_type=jnp.float32
    )
    partial_sum = partial_sum + jnp.einsum(
        "bsf,fd->bsd", hidden, down_weight, preferred_element_type=jnp.float32
    )
    branch_total = lax.psum_scatter(partial_sum, "mp", scatter_dimension=1, tiled=True)
    block_output = local_inputs + branch_total + out_bias
    local_cots = out_cotangent.astype(jnp.float32)
    cot_rows = lax.all_gather(out_cotangent, "mp", axis=1, tiled=True)
    grad_attend = jnp.einsum("bsq,bsd->qd", attended, cot_rows, preferred_element_type=jnp.float32)
    grad_down = jnp.einsum("bsf,bsd->fd", hidden, cot_rows, preferred_element_type=jnp.float32)
    mixed_grad = jnp.einsum(
        "bsd,qd->bsq", cot_rows, attend_weight, preferred_element_type=jnp.float32
    )
    mixed_grad = mixed_grad.astype(jnp.bfloat16).reshape(batch, length, query_width // HS, HS)
    hidden_grad = jnp.einsum(
        "bsd,fd->bsf", cot_rows, down_weight, preferred_element_type=jnp.float32
    )
    _, gelu_pull = jax.vjp(lambda v: jax.nn.gelu(v, approximate=False), hidden_pre)
    pre_grad = gelu_pull(hidden_grad)[0].astype(jnp.bfloat16)
    grad_up = jnp.einsum("bsd,bsf->df", ffn_input, pre_grad, preferred_element_type=jnp.float32)
    ffn_input_grad = jnp.einsum(
        "bsf,df->bsd", pre_grad, up_weight, preferred_element_type=jnp.float32
    )
    up_bias_grad = jnp.sum(pre_grad.astype(jnp.float32), (0, 1))
    query_rot_grad, key_rot_grad, value_grad = lax.map(
        attend_backward, (rotated_queries, rotated_keys, values, key_ids, log_total, mixed_grad)
    )
    query_grad = rotate(query_rot_grad, cosine_table, -sine_table).astype(jnp.bfloat16)
    query_grad = query_grad.reshape(batch, length, query_width)
    key_grad = rotate(key_rot_grad[:, :, None, :], cosine_table, -sine_table)[:, :, 0]
    pair_partial = jnp.concatenate([key_grad, value_grad], -1)
    grad_query = jnp.einsum(
        "bsd,bsq->dq", attn_input, query_grad, preferred_element_type=jnp.float32
    )
    attn_input_grad = jnp.einsum(
        "bsq,dq->bsd", query_grad, query_weight, preferred_element_type=jnp.float32
    )
    query_bias_grad = jnp.sum(query_grad.astype(jnp.float32), (0, 1))
    attn_sum, ffn_sum, pair_sum = (
        lax.psum_scatter(attn_input_grad, "mp", scatter_dimension=1, tiled=True),
        lax.psum_scatter(ffn_input_grad, "mp", scatter_dimension=1, tiled=True),
        lax.psum_scatter(pair_partial, "mp", scatter_dimension=1, tiled=True),
    )
    pair_low = pair_sum.astype(jnp.bfloat16)
    attn_sum = attn_sum + jnp.einsum(
        "bsc,dc->bsd", pair_low, pair_weight, preferred_element_type=jnp.float32
    )
    _, pull_one = jax.vjp(layer_norm, local_inputs, gain_one, shift_one)
    input_one, gain_one_grad, shift_one_grad = pull_one(attn_sum)
    _, pull_two = jax.vjp(layer_norm, local_inputs, gain_two, shift_two)
    input_two, gain_two_grad, shift_two_grad = pull_two(ffn_sum)
    input_grad = local_cots + input_one + input_two
    grad_pair = jnp.einsum("bsd,bsc->dc", attn_local, pair_low, preferred_element_type=jnp.float32)
    pair_bias_grad = jnp.sum(pair_low.astype(jnp.float32), (0, 1))
    out_bias_grad = jnp.sum(local_cots, (0, 1))
    leading_grads = jnp.concatenate(
        [
            gain_one_grad,
            shift_one_grad,
            gain_two_grad,
            shift_two_grad,
            out_bias_grad,
            out_bias_grad,
            pair_bias_grad,
        ]
    )
    in_bias_grad = jnp.concatenate([query_bias_grad, up_bias_grad])
    bias_tail = lax.dynamic_update_slice(
        jnp.zeros((IN_COLS,), jnp.float32), in_bias_grad, (rank * part_width,)
    )
    vector_grad_local = jnp.concatenate([leading_grads, bias_tail])
    entry_grad_full = jnp.concatenate([grad_query, grad_up], 1)
    exit_grad_full = jnp.concatenate([grad_attend, grad_down], 0)
    entry_grad, exit_grad = (
        lax.psum_scatter(entry_grad_full, "dp", scatter_dimension=0, tiled=True),
        lax.psum_scatter(exit_grad_full, "dp", scatter_dimension=1, tiled=True),
    )
    shared_grad = lax.psum_scatter(grad_pair, ("dp", "mp"), scatter_dimension=0, tiled=True)
    vector_grad = lax.psum(vector_grad_local, ("dp", "mp"))
    entry_m, entry_v, entry_new = adamw_update(
        entry_weight[0], entry_first[0], entry_second[0], entry_grad, MATRIX_RATE, MATRIX_DECAY
    )
    exit_m, exit_v, exit_new = adamw_update(
        exit_weight[0], exit_first[0], exit_second[0], exit_grad, MATRIX_RATE, MATRIX_DECAY
    )
    shared_m, shared_v, shared_new = adamw_update(
        shared_weight[0], shared_first[0], shared_second[0], shared_grad, MATRIX_RATE, MATRIX_DECAY
    )
    vector_m, vector_v, vector_new = adamw_update(
        vector, vector_first[0], vector_second[0], vector_grad, VECTOR_RATE, 0.0
    )
    group_count = lax.axis_size("group")
    summed = lax.psum(
        (
            entry_anchor - entry_new,
            exit_anchor - exit_new,
            shared_anchor - shared_new,
            vector_anchor - vector_new,
        ),
        "group",
    )
    anchors = (entry_anchor, exit_anchor, shared_anchor, vector_anchor)
    velocities = (entry_velocity, exit_velocity, shared_velocity, vector_velocity)
    outer_parts = []
    for position in range(4):
        change = summed[position] / group_count
        momentum = OUTER_BETA * velocities[position] + change
        outer_parts.append(
            (change, momentum, anchors[position] - OUTER_RATE * (change + OUTER_BETA * momentum))
        )
    return (
        (block_output, input_grad, entry_m[None], entry_v[None], entry_new[None])
        + outer_parts[0]
        + (exit_m[None], exit_v[None], exit_new[None])
        + outer_parts[1]
        + (shared_m[None], shared_v[None], shared_new[None])
        + outer_parts[2]
        + (vector_m[None], vector_v[None], vector_new[None])
        + outer_parts[3]
    )


def solution(mesh):
    in_specs = (
        P(("group", "dp"), "mp", None),
        P(("group", "dp"), "mp"),
        P(("group", "dp"), "mp", None),
        P("group", "dp", "mp"),
        P("group", "dp", "mp"),
        P("group", "dp", "mp"),
        P("dp", "mp"),
        P("dp", "mp"),
        P("group", "mp", "dp"),
        P("group", "mp", "dp"),
        P("group", "mp", "dp"),
        P("mp", "dp"),
        P("mp", "dp"),
        P("group", ("dp", "mp"), None),
        P("group", ("dp", "mp"), None),
        P("group", ("dp", "mp"), None),
        P(("dp", "mp"), None),
        P(("dp", "mp"), None),
        P("group", None),
        P("group", None),
        P("group", None),
        P(),
        P(),
    )
    out_specs = (
        P(("group", "dp"), "mp", None),
        P(("group", "dp"), "mp", None),
        P("group", "dp", "mp"),
        P("group", "dp", "mp"),
        P("group", "dp", "mp"),
        P("dp", "mp"),
        P("dp", "mp"),
        P("dp", "mp"),
        P("group", "mp", "dp"),
        P("group", "mp", "dp"),
        P("group", "mp", "dp"),
        P("mp", "dp"),
        P("mp", "dp"),
        P("mp", "dp"),
        P("group", ("dp", "mp"), None),
        P("group", ("dp", "mp"), None),
        P("group", ("dp", "mp"), None),
        P(("dp", "mp"), None),
        P(("dp", "mp"), None),
        P(("dp", "mp"), None),
        P("group", None),
        P("group", None),
        P("group", None),
        P(),
        P(),
        P(),
    )
    return jax.shard_map(shards, mesh=mesh, in_specs=in_specs, out_specs=out_specs, check_vma=False)
```

profile of v0, /device:TPU:1, one launch (start us, length us, event | category | flops | bytes accessed | tf_op | source)
XLA Modules:
  0.0 1190.2 jit_solution(6112329701793278091)
XLA Ops:
  17.9 26.4 %all_gather.24 = bf16[768,128]{1,0:T(8,128)(2,1)S(1)} all-gather(bf16[96,128]{1,0:T(8,128)(2,1)S(1)} %bitcast_convert_fusion.2), channel_id=1, replica_groups=mesh['group'=4,'dp'=2,'mp'=4] {'dp','mp'}, dimensions={0}, use_global_device_ids=true | all-gather | bytes 221184 | tf_op jit(solution)/shard_map/all_gather | solution.py:175
  44.2 9.6 all_gather.21
  54.8 50.4 %all-gather.6.cloned.1.call-done = bf16[1,2048,768]{2,1,0:T(8,128)(2,1)} async-done(((bf16[1,512,768]{2,1,0:T(8,128)(2,1)}), bf16[1,2048,768]{2,1,0:T(8,128)(2,1)}) %all-gather.6.cloned.1.call-update) | async-done | bytes 3145744 | tf_op jit(solution)/shard_map/all_gather | solution.py:187
  110.2 87.7 %while.47 = (s32[]{:T(128)}, bf16[4,512,3,64]{1,3,2,0:T(8,128)(2,1)S(1)}, f32[4,3,512]{2,1,0:T(4,128)S(1)}, s32[4]{0:T(128)S(1)}, s32[2048]{0:T(1024)S(1)}, /*in...) while((s32[]{:T(128)}, ...), condition=%wide.region_5.6_spmd, body=%wide.region_2.5_spmd.sunk | while | flops 846298112 | bytes 42938564 | solution.py:79
  118.5 6.8 fusion.203
  125.3 6.7 fusion.204
  140.3 7.2 fusion.203
  147.5 6.8 fusion.204
  162.6 6.8 fusion.203
  169.4 6.7 fusion.204
  184.4 6.8 fusion.203
  191.2 6.7 fusion.204
  201.3 309.5 %while.48 = (s32[]{:T(128)}, f32[2048,64]{0,1:T(8,128)}, f32[2048,64]{0,1:T(8,128)}, f32[4,512,3,64]{1,0,3,2:T(4,128)}, s32[4]{0:T(128)S(1)}, /*index=5*/s32[204...) while((s32[]{:T(128)}, f32[2048,64]{0,1:T(8,128)}, ...), condition=%wide.region_9.10_spmd.clone, body=%wide.region_7.9_spmd.clone.sunk | while | flops 2098732544 | bytes 130478424 | solution.py:116
  204.1 6.4 fusion.214
  218.7 20.3 %fusion.218 = f32[1,512,3,64]{1,3,2,0:T(8,128)S(1)} fusion(f32[512,3,2048]{2,0,1:T(8,128)} %fusion.213, f32[512,3,2048]{2,0,1:T(8,128)} %fusion.214, f32[3,512]{1,0:T(4,128)S(1)} %dynamic-slice_bitcast_fusion.2, pred[512,2048]{1,0:T(8,128)(4,1)S(1)} %fusion.215, bf16[2048,64]{0,1:T(8,128)(2,1)S(1)} %get-tuple-element.536), kind=kOutput, calls=%fused_computation.40.clone.1 | convolution fusion | flops 437259776 | bytes 26875904 | tf_op jit(solution)/shard_map/while/body/eval_jaxpr/while/body/eval_jaxpr/hqk,kd->qhd/dot_general | solution.py:101
  239.4 8.6 dynamic_update_slice.39
  248.0 21.4 %fusion.216 = f32[2048,64]{0,1:T(8,128)} fusion(f32[512,3,2048]{2,0,1:T(8,128)} %fusion.213, f32[512,3,2048]{2,0,1:T(8,128)} %fusion.214, f32[3,512]{1,0:T(4,128)S(1)} %dynamic-slice_bitcast_fusion.2, pred[512,2048]{1,0:T(8,128)(4,1)S(1)} %fusion.215, f32[2048,64]{0,1:T(8,128)} %get-tuple-element.514, pred[]{:T(512)S(6)} %compare.3, ...), kind=kOutput, calls=%fused_computation.36.clone.1 | convolution fusion | flops 437521920 | bytes 53690372 | tf_op jit(solution)/shard_map/while/body/eval_jaxpr/while/body/eval_jaxpr/hqk,qhd->kd/dot_general | solution.py:104
  269.4 7.2 fusion.217
  279.1 6.4 fusion.214
  285.4 6.3 fusion.213
  293.7 20.1 %fusion.218 = f32[1,512,3,64]{1,3,2,0:T(8,128)S(1)} fusion(f32[512,3,2048]{2,0,1:T(8,128)} %fusion.213, f32[512,3,2048]{2,0,1:T(8,128)} %fusion.214, f32[3,512]{1,0:T(4,128)S(1)} %dynamic-slice_bitcast_fusion.2, pred[512,2048]{1,0:T(8,128)(4,1)S(1)} %fusion.215, bf16[2048,64]{0,1:T(8,128)(2,1)S(1)} %get-tuple-element.536), kind=kOutput, calls=%fused_computation.40.clone.1 | convolution fusion | flops 437259776 | bytes 26875904 | tf_op jit(solution)/shard_map/while/body/eval_jaxpr/while/body/eval_jaxpr/hqk,kd->qhd/dot_general | solution.py:101
  314.2 8.6 dynamic_update_slice.39
  322.8 21.5 %fusion.216 = f32[2048,64]{0,1:T(8,128)} fusion(f32[512,3,2048]{2,0,1:T(8,128)} %fusion.213, f32[512,3,2048]{2,0,1:T(8,128)} %fusion.214, f32[3,512]{1,0:T(4,128)S(1)} %dynamic-slice_bitcast_fusion.2, pred[512,2048]{1,0:T(8,128)(4,1)S(1)} %fusion.215, f32[2048,64]{0,1:T(8,128)} %get-tuple-element.514, pred[]{:T(512)S(6)} %compare.3, ...), kind=kOutput, calls=%fused_computation.36.clone.1 | convolution fusion | flops 437521920 | bytes 53690372 | tf_op jit(solution)/shard_map/while/body/eval_jaxpr/while/body/eval_jaxpr/hqk,qhd->kd/dot_general | solution.py:104
  344.4 7.4 fusion.217
  354.2 6.4 fusion.214
  360.5 6.3 fusion.213
  368.8 20.1 %fusion.218 = f32[1,512,3,64]{1,3,2,0:T(8,128)S(1)} fusion(f32[512,3,2048]{2,0,1:T(8,128)} %fusion.213, f32[512,3,2048]{2,0,1:T(8,128)} %fusion.214, f32[3,512]{1,0:T(4,128)S(1)} %dynamic-slice_bitcast_fusion.2, pred[512,2048]{1,0:T(8,128)(4,1)S(1)} %fusion.215, bf16[2048,64]{0,1:T(8,128)(2,1)S(1)} %get-tuple-element.536), kind=kOutput, calls=%fused_computation.40.clone.1 | convolution fusion | flops 437259776 | bytes 26875904 | tf_op jit(solution)/shard_map/while/body/eval_jaxpr/while/body/eval_jaxpr/hqk,kd->qhd/dot_general | solution.py:101
  389.3 8.6 dynamic_update_slice.39
  397.9 21.5 %fusion.216 = f32[2048,64]{0,1:T(8,128)} fusion(f32[512,3,2048]{2,0,1:T(8,128)} %fusion.213, f32[512,3,2048]{2,0,1:T(8,128)} %fusion.214, f32[3,512]{1,0:T(4,128)S(1)} %dynamic-slice_bitcast_fusion.2, pred[512,2048]{1,0:T(8,128)(4,1)S(1)} %fusion.215, f32[2048,64]{0,1:T(8,128)} %get-tuple-element.514, pred[]{:T(512)S(6)} %compare.3, ...), kind=kOutput, calls=%fused_computation.36.clone.1 | convolution fusion | flops 437521920 | bytes 53690372 | tf_op jit(solution)/shard_map/while/body/eval_jaxpr/while/body/eval_jaxpr/hqk,qhd->kd/dot_general | solution.py:104
  419.5 7.4 fusion.217
  429.3 6.4 fusion.214
  443.9 20.1 %fusion.218 = f32[1,512,3,64]{1,3,2,0:T(8,128)S(1)} fusion(f32[512,3,2048]{2,0,1:T(8,128)} %fusion.213, f32[512,3,2048]{2,0,1:T(8,128)} %fusion.214, f32[3,512]{1,0:T(4,128)S(1)} %dynamic-slice_bitcast_fusion.2, pred[512,2048]{1,0:T(8,128)(4,1)S(1)} %fusion.215, bf16[2048,64]{0,1:T(8,128)(2,1)S(1)} %get-tuple-element.536), kind=kOutput, calls=%fused_computation.40.clone.1 | convolution fusion | flops 437259776 | bytes 26875904 | tf_op jit(solution)/shard_map/while/body/eval_jaxpr/while/body/eval_jaxpr/hqk,kd->qhd/dot_general | solution.py:101
  464.4 8.6 dynamic_update_slice.39
  473.0 21.5 %fusion.216 = f32[2048,64]{0,1:T(8,128)} fusion(f32[512,3,2048]{2,0,1:T(8,128)} %fusion.213, f32[512,3,2048]{2,0,1:T(8,128)} %fusion.214, f32[3,512]{1,0:T(4,128)S(1)} %dynamic-slice_bitcast_fusion.2, pred[512,2048]{1,0:T(8,128)(4,1)S(1)} %fusion.215, f32[2048,64]{0,1:T(8,128)} %get-tuple-element.514, pred[]{:T(512)S(6)} %compare.3, ...), kind=kOutput, calls=%fused_computation.36.clone.1 | convolution fusion | flops 437521920 | bytes 53690372 | tf_op jit(solution)/shard_map/while/body/eval_jaxpr/while/body/eval_jaxpr/hqk,qhd->kd/dot_general | solution.py:104
  494.6 7.4 fusion.217
  524.7 18.2 %multiply_convert_fusion = (bf16[2048,768]{1,0:T(8,128)(2,1)}, f32[2048,768]{1,0:T(8,128)S(1)}, f32[2048,768]{1,0:T(8,128)S(1)}) fusion(f32[768]{0:T(1024)S(1)} %copy-done.56, bf16[768,960]{0,1:T(8,128)(2,1)} %all-gather.8.cloned.1.call-done, bf16[1,2048,768]{2,1,0:T(8,128)(2,1)} %all-gather.12.cloned.1.call-done), kind=kOutput, calls=%fused_computation.69 | convolution fusion | flops 2519728128 | bytes 20057088 | tf_op jit(solution)/shard_map/bsd,df->bsf/dot_general | solution.py:206
  564.6 29.6 %reduce-scatter.16.cloned.1.call-done = f32[384,960]{0,1:T(8,128)} async-done(((f32[768,960]{0,1:T(8,128)}), f32[384,960]{0,1:T(8,128)}) %reduce-scatter.16.cloned.1.call-update) | async-done | bytes 1474576 | tf_op jit(solution)/shard_map/reduce_scatter | solution.py:288
  594.2 6.4 fusion.171
  600.6 37.1 %reduce-scatter.18.cloned.1.call-done = f32[960,384]{1,0:T(8,128)} async-done(((f32[960,768]{1,0:T(8,128)}), f32[960,384]{1,0:T(8,128)}) %reduce-scatter.18.cloned.1.call-update) | async-done | bytes 1474576 | tf_op jit(solution)/shard_map/reduce_scatter | solution.py:289
  637.6 6.8 fusion.170
  650.1 7.1 convolution_bitcast_fusion.2
  668.3 33.1 %reduce-scatter.20.cloned.1.call-done = f32[96,128]{1,0:T(8,128)} async-done(((f32[768,128]{1,0:T(8,128)}), f32[96,128]{1,0:T(8,128)}) %reduce-scatter.20.cloned.1.call-update) | async-done | bytes 49168 | tf_op jit(solution)/shard_map/reduce_scatter | solution.py:291
  702.9 67.7 %all-reduce.7.cloned.1.call-done = (f32[384,960]{0,1:T(8,128)}, f32[960,384]{1,0:T(8,128)}) async-done(((f32[384,960]{0,1:T(8,128)}, f32[960,384]{1,0:T(8,128)}), (f32[384,960]{0,1:T(8,128)}, f32[960,384]{1,0:T(8,128)})) %all-reduce.7.cloned.1.call-update) | async-done | bytes 2949136 | tf_op jit(solution)/shard_map/psum | solution.py:306
  775.0 109.0 %reduce-scatter.10.cloned.1.call-done = f32[1,512,768]{2,1,0:T(8,128)} async-done(((f32[1,2048,768]{2,1,0:T(8,128)}), f32[1,512,768]{2,1,0:T(8,128)}) %reduce-scatter.10.cloned.1.call-update) | async-done | bytes 1572880 | tf_op jit(solution)/shard_map/reduce_scatter | solution.py:253
  884.0 113.5 %reduce-scatter.14.cloned.1.call-done = f32[1,512,768]{2,1,0:T(8,128)} async-done(((f32[1,2048,768]{2,1,0:T(8,128)}), f32[1,512,768]{2,1,0:T(8,128)}) %reduce-scatter.14.cloned.1.call-update) | async-done | bytes 1572880 | tf_op jit(solution)/shard_map/reduce_scatter | solution.py:254
  1003.0 108.0 %reduce-scatter.8.cloned.1.call-done = f32[1,512,768]{2,1,0:T(8,128)} async-done(((f32[1,2048,768]{2,1,0:T(8,128)}), f32[1,512,768]{2,1,0:T(8,128)}) %reduce-scatter.8.cloned.1.call-update) | async-done | bytes 1572880 | tf_op jit(solution)/shard_map/reduce_scatter | solution.py:218
  1114.9 30.1 %psum.38 = f32[8576]{0:T(1024)S(1)} all-reduce(f32[8576]{0:T(1024)S(1)} %constant_dynamic-update-slice_fusion), channel_id=1, replica_groups=mesh['group'=4,'dp'=2,'mp'=4] {'dp','mp'}, use_global_device_ids=true, to_apply=%region_31.32 | all-reduce | flops 8576 | bytes 68608 | tf_op jit(solution)/shard_map/psum | solution.py:292
  1152.4 28.0 %all-reduce.5.cloned.1.call-done = (f32[96,128]{1,0:T(8,128)}, f32[8576]{0:T(1024)}) async-done(((f32[96,128]{1,0:T(8,128)}, f32[8576]{0:T(1024)}), (f32[96,128]{1,0:T(8,128)}, f32[8576]{0:T(1024)})) %all-reduce.5.cloned.1.call-update) | async-done | bytes 83472 | tf_op jit(solution)/shard_map/psum | solution.py:306
  (305 shorter events, 148.6 us)
Async XLA Ops:
  7.2 47.6 %all-gather.8.cloned.1.call-start = ((), (), s32[]{:S(2)}) async-start(), calls=%async_computation.8 | async-start | bytes 2211840 | tf_op jit(solution)/shard_map/all_gather | solution.py:172
  9.7 95.6 %all-gather.6.cloned.1.call-start = ((), (), s32[]{:S(2)}) async-start(), calls=%async_computation.7 | async-start | bytes 3932160 | tf_op jit(solution)/shard_map/all_gather | solution.py:187
  14.1 30.1 %copy-start.57 = (s32[1,512]{1,0:T(1,128)S(1)}, s32[1,512]{1,0:T(1,128)}, u32[]{:S(2)}) copy-start(s32[1,512]{1,0:T(1,128)} %param.28) | copy-start | bytes 6148
  14.1 183.8 %all-gather.10.cloned.1.call-start = ((), (), s32[]{:S(2)}) async-start(), calls=%async_computation.9 | async-start | bytes 2211840 | tf_op jit(solution)/shard_map/all_gather | solution.py:173
  15.2 182.8 %all-gather.14.cloned.1.call-start = ((), (), s32[]{:S(2)}) async-start(), calls=%async_computation.12 | async-start | bytes 3932160 | tf_op jit(solution)/shard_map/all_gather | solution.py:221
  15.8 509.0 %all-gather.12.cloned.1.call-start = ((), (), s32[]{:S(2)}) async-start(), calls=%async_computation.10 | async-start | bytes 3932160 | tf_op jit(solution)/shard_map/all_gather | solution.py:188
  16.3 545.9 %reduce-scatter.12.cloned.1.call-start = ((), (), s32[]{:S(2)}) async-start(), calls=%async_computation.14 | async-start | bytes 1310720 | tf_op jit(solution)/shard_map/reduce_scatter | solution.py:255
  44.2 64.4 %copy-start.18 = (bf16[768,128]{1,0:T(8,128)(2,1)}, bf16[768,128]{1,0:T(8,128)(2,1)S(1)}, u32[]{:S(2)}) copy-start(bf16[768,128]{1,0:T(8,128)(2,1)S(1)} %all_gather.24) | copy-start | bytes 589828
  54.1 56.0 %copy-start.24 = (f32[2048,8]{0,1:T(8,128)}, f32[2048,8]{0,1:T(8,128)S(1)}, u32[]{:S(2)}) copy-start(f32[2048,8]{0,1:T(8,128)S(1)} %get-tuple-element.331) | copy-start | bytes 196612
  54.1 56.0 %copy-start.29 = (f32[1,2048,1,8]{1,3,2,0:T(8,128)}, f32[1,2048,1,8]{1,3,2,0:T(8,128)S(1)}, u32[]{:S(2)}) copy-start(f32[1,2048,1,8]{1,3,2,0:T(8,128)S(1)} %get-tuple-element.329) | copy-start | bytes 196612
  54.8 55.1 %copy-start.22 = (f32[2048,16]{0,1:T(8,128)}, f32[2048,16]{0,1:T(8,128)S(1)}, u32[]{:S(2)}) copy-start(f32[2048,16]{0,1:T(8,128)S(1)} %get-tuple-element.338) | copy-start | bytes 393220
  201.6 8.8 copy-start.20
  248.0 21.4 %copy-start.21 = (bf16[2048,3,64]{0,2,1:T(8,128)(2,1)S(1)}, bf16[2048,3,64]{0,2,1:T(8,128)(2,1)}, u32[]{:S(2)}) copy-start(bf16[2048,3,64]{0,2,1:T(8,128)(2,1)} %copy-done.20) | copy-start | bytes 2359300 | tf_op jit(solution)/shard_map/while/body/eval_jaxpr/while
  276.6 8.8 copy-start.20
  322.8 21.5 %copy-start.21 = (bf16[2048,3,64]{0,2,1:T(8,128)(2,1)S(1)}, bf16[2048,3,64]{0,2,1:T(8,128)(2,1)}, u32[]{:S(2)}) copy-start(bf16[2048,3,64]{0,2,1:T(8,128)(2,1)} %copy-done.20) | copy-start | bytes 2359300 | tf_op jit(solution)/shard_map/while/body/eval_jaxpr/while
  351.7 8.8 copy-start.20
  397.9 21.5 %copy-start.21 = (bf16[2048,3,64]{0,2,1:T(8,128)(2,1)S(1)}, bf16[2048,3,64]{0,2,1:T(8,128)(2,1)}, u32[]{:S(2)}) copy-start(bf16[2048,3,64]{0,2,1:T(8,128)(2,1)} %copy-done.20) | copy-start | bytes 2359300 | tf_op jit(solution)/shard_map/while/body/eval_jaxpr/while
  426.8 8.8 copy-start.20
  473.0 21.5 %copy-start.21 = (bf16[2048,3,64]{0,2,1:T(8,128)(2,1)S(1)}, bf16[2048,3,64]{0,2,1:T(8,128)(2,1)}, u32[]{:S(2)}) copy-start(bf16[2048,3,64]{0,2,1:T(8,128)(2,1)} %copy-done.20) | copy-start | bytes 2359300 | tf_op jit(solution)/shard_map/while/body/eval_jaxpr/while
  515.7 7.4 copy-start.1
  519.7 74.4 %reduce-scatter.16.cloned.1.call-start = ((), (), s32[]{:S(2)}) async-start(), calls=%async_computation.16 | async-start | bytes 4423680 | tf_op jit(solution)/shard_map/reduce_scatter | solution.py:288
  524.7 18.2 %copy-start.14 = (bf16[1,2048,768]{2,1,0:T(8,128)(2,1)S(1)}, bf16[1,2048,768]{2,1,0:T(8,128)(2,1)}, u32[]{:S(2)}) copy-start(bf16[1,2048,768]{2,1,0:T(8,128)(2,1)} %all-gather.14.cloned.1.call-done) | copy-start | bytes 9437188
  524.7 18.2 %copy-start.43 = (bf16[960,768]{1,0:T(8,128)(2,1)S(1)}, bf16[960,768]{1,0:T(8,128)(2,1)}, u32[]{:S(2)}) copy-start(bf16[960,768]{1,0:T(8,128)(2,1)} %all-gather.10.cloned.1.call-done) | copy-start | bytes 4423684
  553.6 84.0 %reduce-scatter.18.cloned.1.call-start = ((), (), s32[]{:S(2)}) async-start(), calls=%async_computation.17 | async-start | bytes 4423680 | tf_op jit(solution)/shard_map/reduce_scatter | solution.py:289
  562.2 32.0 %copy-start.9 = (f32[1,384,960]{1,2,0:T(8,128)S(1)}, f32[1,384,960]{1,2,0:T(8,128)}, u32[]{:S(2)}) copy-start(f32[1,384,960]{1,2,0:T(8,128)} %param.30) | copy-start | bytes 4423684
  562.2 139.2 %reduce-scatter.20.cloned.1.call-start = ((), (), s32[]{:S(2)}) async-start(), calls=%async_computation.18 | async-start | bytes 442368 | tf_op jit(solution)/shard_map/reduce_scatter | solution.py:291
  564.5 206.1 %all-reduce.7.cloned.1.call-start = ((), (), s32[]{:S(2)}) async-start(), calls=%async_computation.20 | async-start | bytes 5898240 | tf_op jit(solution)/shard_map/psum | solution.py:306
  644.5 239.5 %reduce-scatter.10.cloned.1.call-start = ((), (), s32[]{:S(2)}) async-start(), calls=%async_computation.13 | async-start | bytes 7864320 | tf_op jit(solution)/shard_map/reduce_scatter | solution.py:253
  649.8 347.6 %reduce-scatter.14.cloned.1.call-start = ((), (), s32[]{:S(2)}) async-start(), calls=%async_computation.15 | async-start | bytes 7864320 | tf_op jit(solution)/shard_map/reduce_scatter | solution.py:254
  657.3 453.8 %reduce-scatter.8.cloned.1.call-start = ((), (), s32[]{:S(2)}) async-start(), calls=%async_computation.11 | async-start | bytes 7864320 | tf_op jit(solution)/shard_map/reduce_scatter | solution.py:218
  666.9 34.5 %copy-start.32 = (f32[96,128]{1,0:T(8,128)S(1)}, f32[96,128]{1,0:T(8,128)}, u32[]{:S(2)}) copy-start(f32[96,128]{1,0:T(8,128)} %param.43) | copy-start | bytes 147460
  666.9 34.5 %copy-start.34 = (f32[1,96,128]{2,1,0:T(8,128)S(1)}, f32[1,96,128]{2,1,0:T(8,128)}, u32[]{:S(2)}) copy-start(f32[1,96,128]{2,1,0:T(8,128)} %param.40) | copy-start | bytes 147460
  666.9 34.5 %copy-start.45 = (f32[1,96,128]{2,1,0:T(8,128)S(1)}, f32[1,96,128]{2,1,0:T(8,128)}, u32[]{:S(2)}) copy-start(f32[1,96,128]{2,1,0:T(8,128)} %param.42) | copy-start | bytes 147460
  666.9 34.5 %copy-start.46 = (f32[1,96,128]{2,1,0:T(8,128)S(1)}, f32[1,96,128]{2,1,0:T(8,128)}, u32[]{:S(2)}) copy-start(f32[1,96,128]{2,1,0:T(8,128)} %param.41) | copy-start | bytes 147460
  667.0 103.7 %copy-start.11 = (f32[960,384]{1,0:T(8,128)S(1)}, f32[960,384]{1,0:T(8,128)}, u32[]{:S(2)}) copy-start(f32[960,384]{1,0:T(8,128)} %param.38) | copy-start | bytes 4423684
  667.0 513.4 %all-reduce.5.cloned.1.call-start = ((), (), s32[]{:S(2)}) async-start(), calls=%async_computation.19 | async-start | bytes 172032 | tf_op jit(solution)/shard_map/psum | solution.py:306
  770.7 226.8 %copy-start.3 = (bf16[1,512,768]{2,1,0:T(8,128)(2,1)S(1)}, bf16[1,512,768]{2,1,0:T(8,128)(2,1)}, u32[]{:S(2)}) copy-start(bf16[1,512,768]{2,1,0:T(8,128)(2,1)} %param.27) | copy-start | bytes 2359300
  770.7 226.8 %copy-start.19 = (bf16[768,128]{1,0:T(8,128)(2,1)S(1)}, bf16[768,128]{1,0:T(8,128)(2,1)}, u32[]{:S(2)}) copy-start(bf16[768,128]{1,0:T(8,128)(2,1)} %copy-done.18) | copy-start | bytes 589828
  770.7 226.8 %copy-start.37 = (f32[768]{0:T(1024)S(1)}, f32[768]{0:T(1024)}, u32[]{:S(2)}) copy-start(f32[768]{0:T(1024)} %copy-done.36) | copy-start | bytes 9220
  770.7 226.8 %copy-start.39 = (f32[768]{0:T(1024)S(1)}, f32[768]{0:T(1024)}, u32[]{:S(2)}) copy-start(f32[768]{0:T(1024)} %copy-done.38) | copy-start | bytes 9220
  770.7 226.8 %copy-start.42 = (f32[512]{0:T(512)S(1)}, f32[512]{0:T(512)}, u32[]{:S(2)}) copy-start(f32[512]{0:T(512)} %copy-done.41) | copy-start | bytes 6148
  775.0 225.4 %copy-start.54 = (f32[512]{0:T(512)S(1)}, f32[512]{0:T(512)}, u32[]{:S(2)}) copy-start(f32[512]{0:T(512)} %copy-done.53) | copy-start | bytes 6148
  775.0 226.5 %copy-start.52 = (f32[512]{0:T(512)S(1)}, f32[512]{0:T(512)}, u32[]{:S(2)}) copy-start(f32[512]{0:T(512)} %copy-done.51) | copy-start | bytes 6148
  1000.4 110.7 %copy-start.13 = (bf16[1,512,768]{2,1,0:T(8,128)(2,1)S(1)}, bf16[1,512,768]{2,1,0:T(8,128)(2,1)}, u32[]{:S(2)}) copy-start(bf16[1,512,768]{2,1,0:T(8,128)(2,1)} %param.29) | copy-start | bytes 2359300
  1000.4 110.7 %copy-start.55 = (f32[768]{0:T(1024)S(1)}, f32[768]{0:T(1024)}, u32[]{:S(2)}) copy-start(f32[768]{0:T(1024)} %get-tuple-element.230) | copy-start | bytes 9220
  1111.1 34.0 %copy-start.35 = (f32[8576]{0:T(1024)S(1)}, f32[8576]{0:T(1024)}, u32[]{:S(2)}) copy-start(f32[8576]{0:T(1024)} %param.48) | copy-start | bytes 102916
  1145.7 34.6 %copy-start.47 = (f32[96,128]{1,0:T(8,128)S(1)}, f32[96,128]{1,0:T(8,128)}, u32[]{:S(2)}) copy-start(f32[96,128]{1,0:T(8,128)} %param.44) | copy-start | bytes 147460
  1145.8 36.1 %copy-start.48 = (f32[8576]{0:T(1024)S(1)}, f32[8576]{0:T(1024)}, u32[]{:S(2)}) copy-start(f32[8576]{0:T(1024)} %param.49) | copy-start | bytes 102916
  (33 other events, 89.2 us)
Sparse Core Ops, SparseCore 0:
  10.2 29.2 all-gather.7
  41.6 63.6 all-gather.5
  107.4 24.7 all-gather.9
  133.7 63.4 all-gather.13
  199.1 62.1 all-gather.11
  519.8 26.0 reduce-scatter.11
  553.8 40.3 reduce-scatter.15
  596.4 41.1 reduce-scatter.17
  641.8 59.5 reduce-scatter.19
  704.3 66.2 all-reduce.6
  773.0 110.9 reduce-scatter.9
  886.1 111.2 reduce-scatter.13
  999.8 111.2 reduce-scatter.7
  1145.9 34.4 all-reduce.4
where the time goes:
time: 1200 us; the launch traced here: 1190 us
  waiting for transfers between devices  578 us (48%)
  matrix products  363 us (30%)
  other arithmetic  87.1 us (7%)
  blocking collectives  66.1 us (6%)
  local copies, waits for them, and re-layouts  57.2 us (5%)
  loops' own time  22.5 us (2%)
  between operations  15.3 us (1%)
    reduce_scatter x1, waiting for transfers between devices, shards(): lax.psum_scatter(ffn_input_grad, 'mp', scatter_dimension=1, tiled=True)  113 us
    reduce_scatter x1, waiting for transfers between devices, shards(): lax.psum_scatter(attn_input_grad, 'mp', scatter_dimension=1, tiled=True)  109 us
    reduce_scatter x1, waiting for transfers between devices, shards(): lax.psum_scatter(partial_sum, 'mp', scatter_dimension=1, tiled=True)  108 us
    psum x2, waiting for transfers between devices, shards(): lax.psum((entry_anchor - entry_new, exit_anchor - exit_new, shared_anchor...  95.7 us
    dot_general x4, matrix products, one_step(): jnp.einsum('hqk,qhd->kd', score_grad, query_rows, preferred_element_type=...  86 us
    dot_general x4, matrix products, one_step(): jnp.einsum('hqk,kd->qhd', score_grad, rotated_keys, preferred_element_typ...  80.5 us
    all_gather x1, waiting for transfers between devices, shards(): lax.all_gather(attn_local, 'mp', axis=1, tiled=True)  50.4 us
    dot_general x8, matrix products, masked_scores(): jnp.einsum('qhd,kd->hqk', query_rows, rotated_keys, preferred_element_typ...  49.2 us
  transfers between devices with their start and end apart: 14, of which 9 were waited for; matrix products, arithmetic and copies ran while one was open for 41% of the time, Pallas kernels for 0%

commit v1 on v0

v1 whole, which is shorter than its diff:
```python
import math

import jax
import jax.numpy as jnp
from jax import lax
from jax.experimental import pallas as pl
from jax.experimental.pallas import tpu as pltpu
from jax.sharding import PartitionSpec as P

D = 768
HEADS = 12
HS = 64
ROT = 16
STEP = 5
IN_COLS = 3840


NORM_EPS = 1e-05
BETA_ONE = 0.9
BETA_TWO = 0.95
ADAM_EPS = 1e-08
MATRIX_RATE = 0.03
MATRIX_DECAY = 0.1
VECTOR_RATE = 0.3
OUTER_RATE = 0.7
OUTER_BETA = 0.9

TILE = 256
F32 = jnp.float32
BF = jnp.bfloat16


def dot(left, right):
    return jnp.dot(left, right, preferred_element_type=F32)


def dot_nt(left, right):
    return lax.dot_general(left, right, (((1,), (1,)), ((), ())), preferred_element_type=F32)


def dot_tn(left, right):
    return lax.dot_general(left, right, (((0,), (0,)), ((), ())), preferred_element_type=F32)


def tile_at(rank, tile, per):
    return pl.multiple_of((jnp.bitwise_xor(tile // per, rank) * per + tile % per) * TILE, TILE)


def masked(scores, key_tile, query_tile, tiles, key_ids, query_ids):
    edge = key_tile == 0 or query_tile == tiles - 1
    if key_tile == query_tile:
        rows = lax.broadcasted_iota(jnp.int32, (TILE, TILE), 0)
        columns = lax.broadcasted_iota(jnp.int32, (TILE, TILE), 1)
        allowed = rows <= columns
        if edge:
            allowed = allowed & (key_ids == query_ids)
        return jnp.where(allowed, scores, -1e9)
    if edge:
        return jnp.where(key_ids == query_ids, scores, -1e9)
    return scores


def forward_kernel(rank_ref, q_ref, k_ref, vt_ref, row_ids, col_ids, o_ref, l_ref, s_ref):
    tiles = q_ref.shape[1] // TILE
    per = tiles // 4
    rank = rank_ref[0]
    for query in range(tiles):
        at_q = tile_at(rank, query, per)
        q = q_ref[:, pl.ds(at_q, TILE)]
        query_ids = row_ids[:, pl.ds(at_q, TILE)]
        highest = jnp.full((1, TILE), -jnp.inf, F32)
        for key in range(query + 1):
            at_k = tile_at(rank, key, per)
            scores = dot(k_ref[pl.ds(at_k, TILE), :], q)
            scores = masked(scores, key, query, tiles, col_ids[pl.ds(at_k, TILE), :], query_ids)
            s_ref[pl.ds(key * TILE, TILE), :] = scores
            highest = jnp.maximum(highest, jnp.max(scores, 0, keepdims=True))
        total = jnp.zeros((1, TILE), F32)
        for key in range(query + 1):
            exponent = jnp.exp(s_ref[pl.ds(key * TILE, TILE), :] - highest)
            s_ref[pl.ds(key * TILE, TILE), :] = exponent
            total = total + jnp.sum(exponent, 0, keepdims=True)
        inverse = 1.0 / total
        mixed = jnp.zeros((HS, TILE), F32)
        for key in range(query + 1):
            at_k = tile_at(rank, key, per)
            softmax = (s_ref[pl.ds(key * TILE, TILE), :] * inverse).astype(BF)
            mixed = mixed + dot(vt_ref[:, pl.ds(at_k, TILE)], softmax)
        o_ref[:, pl.ds(at_q, TILE)] = mixed.astype(BF)
        l_ref[:, :, pl.ds(at_q, TILE)] = jnp.broadcast_to(highest + jnp.log(total), (8, TILE))[None]


def attend_forward(rank, qt, k, vt, ids):
    length = qt.shape[1]
    heads = qt.shape[0] // HS
    by_head = lambda i, r: (i, 0)
    whole = lambda i, r: (0, 0)
    grid_spec = pltpu.PrefetchScalarGridSpec(
        num_scalar_prefetch=1,
        grid=(heads,),
        in_specs=[
            pl.BlockSpec((HS, length), by_head),
            pl.BlockSpec((length, HS), whole),
            pl.BlockSpec((HS, length), whole),
            pl.BlockSpec((1, length), whole),
            pl.BlockSpec((length, 1), whole),
        ],
        out_specs=[
            pl.BlockSpec((HS, length), by_head),
            pl.BlockSpec((1, 8, length), lambda i, r: (i, 0, 0)),
        ],
        scratch_shapes=[pltpu.VMEM((length, TILE), F32)],
    )
    work = heads * length * length * HS
    return pl.pallas_call(
        forward_kernel,
        grid_spec=grid_spec,
        out_shape=[
            jax.ShapeDtypeStruct((heads * HS, length), BF),
            jax.ShapeDtypeStruct((heads, 8, length), F32),
        ],
        compiler_params=pltpu.CompilerParams(vmem_limit_bytes=32 << 20),
        cost_estimate=pl.CostEstimate(
            flops=8 * work, bytes_accessed=4 << 20, transcendentals=heads * length * length // 2
        ),
        name="attend_rows",
    )(rank, qt, k, vt, ids.reshape(1, length), ids.reshape(length, 1))


def backward_kernel(
    rank_ref, q_ref, do_ref, l_ref, k_ref, v_ref, kt_ref, row_ids, col_ids,
    dq_ref, dk_ref, dv_ref, p_ref, d_ref,
):
    tiles = q_ref.shape[1] // TILE
    per = tiles // 4
    rank = rank_ref[0]

    @pl.when(pl.program_id(0) == 0)
    def _():
        dk_ref[...] = jnp.zeros_like(dk_ref)
        dv_ref[...] = jnp.zeros_like(dv_ref)

    for query in range(tiles):
        at_q = tile_at(rank, query, per)
        q = q_ref[:, pl.ds(at_q, TILE)]
        do = do_ref[:, pl.ds(at_q, TILE)]
        scaled = do * jnp.asarray(0.125, BF)
        query_ids = row_ids[:, pl.ds(at_q, TILE)]
        log_total = l_ref[0, 0:1, pl.ds(at_q, TILE)]
        inner = jnp.zeros((1, TILE), F32)
        for key in range(query + 1):
            at_k = tile_at(rank, key, per)
            scores = dot(k_ref[pl.ds(at_k, TILE), :], q)
            scores = masked(scores, key, query, tiles, col_ids[pl.ds(at_k, TILE), :], query_ids)
            softmax = jnp.exp(scores - log_total)
            prob_grad = dot(v_ref[pl.ds(at_k, TILE), :], scaled)
            p_ref[pl.ds(key * TILE, TILE), :] = softmax
            d_ref[pl.ds(key * TILE, TILE), :] = prob_grad
            inner = inner + jnp.sum(softmax * prob_grad, 0, keepdims=True)
        query_grad = jnp.zeros((HS, TILE), F32)
        for key in range(query + 1):
            at_k = tile_at(rank, key, per)
            softmax = p_ref[pl.ds(key * TILE, TILE), :]
            score_grad = (softmax * (d_ref[pl.ds(key * TILE, TILE), :] - inner)).astype(BF)
            query_grad = query_grad + dot(kt_ref[:, pl.ds(at_k, TILE)], score_grad)
            dk_ref[pl.ds(at_k, TILE), :] += dot_nt(score_grad, q)
            dv_ref[pl.ds(at_k, TILE), :] += dot_nt(softmax.astype(BF), do)
        dq_ref[:, pl.ds(at_q, TILE)] = query_grad


def attend_backward(rank, qt, dot_rows, log_total, k, v, kt, ids):
    length = qt.shape[1]
    heads = qt.shape[0] // HS
    by_head = lambda i, r: (i, 0)
    whole = lambda i, r: (0, 0)
    grid_spec = pltpu.PrefetchScalarGridSpec(
        num_scalar_prefetch=1,
        grid=(heads,),
        in_specs=[
            pl.BlockSpec((HS, length), by_head),
            pl.BlockSpec((HS, length), by_head),
            pl.BlockSpec((1, 8, length), lambda i, r: (i, 0, 0)),
            pl.BlockSpec((length, HS), whole),
            pl.BlockSpec((length, HS), whole),
            pl.BlockSpec((HS, length), whole),
            pl.BlockSpec((1, length), whole),
            pl.BlockSpec((length, 1), whole),
        ],
        out_specs=[
            pl.BlockSpec((HS, length), by_head),
            pl.BlockSpec((length, HS), whole),
            pl.BlockSpec((length, HS), whole),
        ],
        scratch_shapes=[pltpu.VMEM((length, TILE), F32), pltpu.VMEM((length, TILE), F32)],
    )
    work = heads * length * length * HS
    return pl.pallas_call(
        backward_kernel,
        grid_spec=grid_spec,
        out_shape=[
            jax.ShapeDtypeStruct((heads * HS, length), F32),
            jax.ShapeDtypeStruct((length, HS), F32),
            jax.ShapeDtypeStruct((length, HS), F32),
        ],
        compiler_params=pltpu.CompilerParams(vmem_limit_bytes=32 << 20),
        cost_estimate=pl.CostEstimate(
            flops=14 * work, bytes_accessed=6 << 20, transcendentals=heads * length * length // 2
        ),
        name="attend_rows_back",
    )(rank, qt, dot_rows, log_total, k, v, kt, ids.reshape(1, length), ids.reshape(length, 1))


def rotate(rows, cosine_table, sine_table):
    half = ROT // 2
    one, two = (rows[..., :half, :], rows[..., half:ROT, :])
    return jnp.concatenate(
        [
            one * cosine_table - two * sine_table,
            two * cosine_table + one * sine_table,
            rows[..., ROT:, :],
        ],
        -2,
    )


def adamw_update(weight, first, second, gradient, step_rate, decay):
    first_new = BETA_ONE * first + (1.0 - BETA_ONE) * gradient
    second_new = BETA_TWO * second + (1.0 - BETA_TWO) * gradient * gradient
    fix_first = 1.0 - BETA_ONE**STEP
    fix_second = 1.0 - BETA_TWO**STEP
    update = first_new / fix_first / (jnp.sqrt(second_new / fix_second) + ADAM_EPS)
    return (first_new, second_new, weight - step_rate * (update + decay * weight))


def pairs_of(size, bit):
    return [(at, at ^ bit) for at in range(size)]


def over_core(array):
    return lax.ppermute(array, "group", pairs_of(lax.axis_size("group"), 1))


def over_half(array):
    return lax.ppermute(array, "group", pairs_of(lax.axis_size("group"), 2))


def over_next(array):
    return lax.ppermute(array, "mp", pairs_of(lax.axis_size("mp"), 1))


def over_dp(array):
    return lax.ppermute(array, "dp", pairs_of(2, 1))


def swapped_parts(array):
    parts = lax.axis_size("mp")
    pairs = []
    for group in range(lax.axis_size("group")):
        for rank in range(parts):
            here = group * parts + rank
            there = (group ^ 1) * parts + (rank ^ 2)
            pairs.append((here, there if group % 2 != rank // 2 else here))
    return lax.ppermute(array, ("group", "mp"), pairs)


def gather_square(own):
    pair = jnp.stack([own, over_next(own)])
    return jnp.concatenate([pair, over_core(pair)], 0)


def scatter_square(slots, send_type):
    pair = slots[:2] + over_core(slots[2:].astype(send_type)).astype(F32)
    return pair[0] + over_next(pair[1].astype(send_type)).astype(F32)


def sum_square(array):
    array = array + over_core(array)
    return array + over_next(array)


def gather_dp(own, axis):
    if lax.axis_size("dp") == 2:
        other = over_dp(own)
        first = lax.axis_index("dp") == 0
        return jnp.concatenate(
            [jnp.where(first, own, other), jnp.where(first, other, own)], axis
        )
    return lax.all_gather(own, "dp", axis=axis, tiled=True)


def scatter_dp(array, axis, send_type):
    if lax.axis_size("dp") == 2:
        size = array.shape[axis] // 2
        mine = lax.axis_index("dp")
        kept = lax.dynamic_slice_in_dim(array, mine * size, size, axis)
        sent = lax.dynamic_slice_in_dim(array, (1 - mine) * size, size, axis)
        return kept + over_dp(sent.astype(send_type)).astype(F32)
    return lax.psum_scatter(array, "dp", scatter_dimension=axis, tiled=True)


def sum_dp(array):
    if lax.axis_size("dp") == 2:
        return array + over_dp(array)
    return lax.psum(array, "dp")


def sum_groups(array, send_type):
    size = array.shape[0] // 2
    core = lax.axis_index("group") % 2
    kept = lax.dynamic_slice_in_dim(array, core * size, size, 0)
    sent = lax.dynamic_slice_in_dim(array, (1 - core) * size, size, 0)
    part = (kept + over_core(sent)).astype(send_type)
    part = part.astype(F32) + over_half(part).astype(F32)
    other = over_core(part)
    low = core == 0
    return jnp.concatenate([jnp.where(low, part, other), jnp.where(low, other, part)], 0)


def shards(
    hidden_in,
    doc_ids,
    out_cotangent,
    entry_weight,
    entry_first,
    entry_second,
    entry_anchor,
    entry_velocity,
    exit_weight,
    exit_first,
    exit_second,
    exit_anchor,
    exit_velocity,
    shared_weight,
    shared_first,
    shared_second,
    shared_anchor,
    shared_velocity,
    vector_weight,
    vector_first,
    vector_second,
    vector_anchor,
    vector_velocity,
):
    batch, local_len = hidden_in.shape[:2]
    parts = lax.axis_size("mp")
    group, rank = (lax.axis_index("group"), lax.axis_index("mp"))
    is_swapped = (group % 2) != (rank // 2)
    rank = jnp.where(is_swapped, jnp.bitwise_xor(rank, 2), rank)
    length = local_len * parts
    part_width = entry_weight.shape[2]
    query_width = HEADS * HS // parts
    heads = query_width // HS

    home_vector = vector_weight[0]
    vector = jnp.where(is_swapped, over_core(home_vector), home_vector)
    gain_one, shift_one = (vector[0:D], vector[D : 2 * D])
    gain_two, shift_two = (vector[2 * D : 3 * D], vector[3 * D : 4 * D])
    home_bias = home_vector[4 * D : 5 * D] + home_vector[5 * D : 6 * D]
    pair_bias = vector[6 * D : 6 * D + 2 * HS]
    in_bias = lax.dynamic_slice_in_dim(vector, 6 * D + 2 * HS + rank * part_width, part_width, 0)
    query_bias = in_bias[:query_width]
    up_bias = in_bias[query_width:]

    inputs = gather_square(swapped_parts(hidden_in[0])).reshape(length, D)
    ids = gather_square(swapped_parts(doc_ids[0])).reshape(length)
    entry_rows = gather_dp(swapped_parts(entry_weight[0].astype(BF)), 0)
    exit_rows = gather_dp(swapped_parts(exit_weight[0].astype(BF)), 1)
    pieces = gather_square(swapped_parts(shared_weight[0].astype(BF)))
    order = jnp.bitwise_xor(jnp.arange(parts), rank)
    pieces = jnp.take(pieces, order, axis=0)
    pair_weight = gather_dp(pieces.reshape(-1, 2 * HS), 0)
    cots = gather_square(swapped_parts(out_cotangent[0])).reshape(length, D)

    query_weight = entry_rows[:, :query_width]
    up_weight = entry_rows[:, query_width:]
    attend_weight = exit_rows[:query_width]
    down_weight = exit_rows[query_width:]

    half = ROT // 2
    positions = (order[:, None] * local_len + jnp.arange(local_len)[None, :]).reshape(length)
    frequency = 10000.0 ** (-(jnp.arange(half).astype(F32) * 2.0 / ROT))
    angles = frequency[:, None] * positions.astype(F32)[None, :]
    cosine_table, sine_table = (jnp.cos(angles), jnp.sin(angles))

    wide = inputs.astype(F32)
    centered = wide - jnp.mean(wide, -1, keepdims=True)
    normal = centered * lax.rsqrt(jnp.mean(centered * centered, -1, keepdims=True) + NORM_EPS)
    attn_input = (normal * gain_one + shift_one).astype(BF)
    ffn_input = (normal * gain_two + shift_two).astype(BF)

    queries = lax.dot_general(
        query_weight, attn_input, (((0,), (1,)), ((), ())), preferred_element_type=F32
    )
    queries = (queries + query_bias[:, None]).reshape(heads, HS, length)
    rotated_queries = rotate(queries, cosine_table, sine_table).astype(BF) * jnp.asarray(
        1.0 / math.sqrt(HS), BF
    )
    rotated_queries = rotated_queries.reshape(query_width, length)
    pairs = lax.dot_general(
        pair_weight, attn_input, (((0,), (1,)), ((), ())), preferred_element_type=F32
    )
    pairs = pairs + pair_bias[:, None]
    key_rows = rotate(pairs[:HS], cosine_table, sine_table).astype(BF)
    value_rows = pairs[HS:].astype(BF)
    keys, values = (key_rows.T, value_rows.T)
    rank_scalar = rank.reshape(1).astype(jnp.int32)
    attended, log_total = attend_forward(rank_scalar, rotated_queries, keys, value_rows, ids)

    hidden_pre = dot(ffn_input, up_weight) + up_bias
    half_root = math.sqrt(0.5)
    below = 0.5 * (1.0 + lax.erf(hidden_pre * half_root))
    hidden = (hidden_pre * below).astype(BF)
    density = jnp.exp(-0.5 * hidden_pre * hidden_pre) * (1.0 / math.sqrt(2.0 * math.pi))
    slope = below + hidden_pre * density

    partial_sum = dot_tn(attended, attend_weight) + dot(hidden, down_weight)
    branch = scatter_square(partial_sum.reshape(parts, local_len, D), BF)
    block_output = (
        hidden_in[0].astype(F32) + swapped_parts(branch.astype(BF)).astype(F32) + home_bias
    )

    grad_attend = dot(attended, cots)
    grad_down = dot_tn(hidden, cots)
    mixed_grad = dot_nt(attend_weight, cots).astype(BF)
    pre_grad = (dot_nt(cots, down_weight) * slope).astype(BF)
    grad_up = dot_tn(ffn_input, pre_grad)
    ffn_input_grad = dot_nt(pre_grad, up_weight)
    up_bias_grad = jnp.sum(pre_grad.astype(F32), 0)
    query_rot_grad, key_rot_grad, value_grad = attend_backward(
        rank_scalar, rotated_queries, mixed_grad, log_total, keys, values, key_rows, ids
    )
    query_grad = rotate(query_rot_grad.reshape(heads, HS, length), cosine_table, -sine_table)
    query_grad = query_grad.astype(BF).reshape(query_width, length)
    key_grad = rotate(key_rot_grad.T * math.sqrt(HS), cosine_table, -sine_table).T
    pair_partial = jnp.concatenate([key_grad, value_grad], -1)
    grad_query = dot(query_grad, attn_input).T
    attn_input_grad = lax.dot_general(
        query_grad, query_weight, (((0,), (1,)), ((), ())), preferred_element_type=F32
    )
    query_bias_grad = jnp.sum(query_grad.astype(F32), 1)
    joined = attn_input_grad * gain_one + ffn_input_grad * gain_two
    joined_own = scatter_square(joined.reshape(parts, local_len, D), BF)
    pair_low = scatter_square(pair_partial.reshape(parts, local_len, 2 * HS), F32).astype(BF)
    pair_input_grad = dot_nt(pair_low, pair_weight)
    joined_own = joined_own + pair_input_grad * gain_one
    joined_home = swapped_parts(joined_own.astype(BF)).astype(F32)
    home_wide = hidden_in[0].astype(F32)
    home_centered = home_wide - jnp.mean(home_wide, -1, keepdims=True)
    home_scale = lax.rsqrt(jnp.mean(home_centered * home_centered, -1, keepdims=True) + NORM_EPS)
    home_normal = home_centered * home_scale
    input_grad = out_cotangent[0].astype(F32) + home_scale * (
        joined_home
        - jnp.mean(joined_home, -1, keepdims=True)
        - home_normal * jnp.mean(joined_home * home_normal, -1, keepdims=True)
    )

    own_normal = normal[:local_len]
    own_attn = attn_input[:local_len]
    grad_pair = dot_tn(own_attn, pair_low)
    out_bias_grad = jnp.sum(cots[:local_len].astype(F32), 0)
    leading_grads = jnp.concatenate(
        [
            jnp.sum(attn_input_grad * normal, 0) + jnp.sum(pair_input_grad * own_normal, 0),
            jnp.sum(attn_input_grad, 0) + jnp.sum(pair_input_grad, 0),
            jnp.sum(ffn_input_grad * normal, 0),
            jnp.sum(ffn_input_grad, 0),
            out_bias_grad,
            out_bias_grad,
            jnp.sum(pair_low.astype(F32), 0),
        ]
    )
    bias_tail = lax.dynamic_update_slice(
        jnp.zeros((IN_COLS,), F32),
        jnp.concatenate([query_bias_grad, up_bias_grad]),
        (rank * part_width,),
    )
    vector_grad = swapped_parts(
        sum_dp(sum_square(jnp.concatenate([leading_grads, bias_tail])))
    )
    entry_grad = scatter_dp(jnp.concatenate([grad_query, grad_up], 1), 0, BF)
    exit_grad = scatter_dp(jnp.concatenate([grad_attend, grad_down], 0), 1, BF)
    entry_grad = jnp.where(
        is_swapped, swapped_parts(entry_grad.astype(BF)).astype(F32), entry_grad
    )
    exit_grad = jnp.where(is_swapped, swapped_parts(exit_grad.astype(BF)).astype(F32), exit_grad)
    grad_pieces = grad_pair.reshape(lax.axis_size("dp"), parts, -1, 2 * HS)
    grad_pieces = jnp.take(grad_pieces, order, axis=1).swapaxes(0, 1)
    shared_grad = scatter_dp(scatter_square(grad_pieces, F32), 0, F32)
    shared_grad = swapped_parts(shared_grad.reshape(-1, 2 * HS))

    entry_m, entry_v, entry_new = adamw_update(
        entry_weight[0], entry_first[0], entry_second[0], entry_grad, MATRIX_RATE, MATRIX_DECAY
    )
    exit_m, exit_v, exit_new = adamw_update(
        exit_weight[0], exit_first[0], exit_second[0], exit_grad, MATRIX_RATE, MATRIX_DECAY
    )
    shared_m, shared_v, shared_new = adamw_update(
        shared_weight[0], shared_first[0], shared_second[0], shared_grad, MATRIX_RATE, MATRIX_DECAY
    )
    vector_m, vector_v, vector_new = adamw_update(
        home_vector, vector_first[0], vector_second[0], vector_grad, VECTOR_RATE, 0.0
    )
    group_count = lax.axis_size("group")
    vector_gap = vector_anchor - vector_new
    vector_gap = vector_gap + over_core(vector_gap)
    summed = (
        sum_groups(entry_anchor - entry_new, BF),
        sum_groups(exit_anchor - exit_new, BF),
        sum_groups(shared_anchor - shared_new, F32),
        vector_gap + over_half(vector_gap),
    )
    anchors = (entry_anchor, exit_anchor, shared_anchor, vector_anchor)
    velocities = (entry_velocity, exit_velocity, shared_velocity, vector_velocity)
    outer_parts = []
    for position in range(4):
        change = summed[position] / group_count
        momentum = OUTER_BETA * velocities[position] + change
        outer_parts.append(
            (change, momentum, anchors[position] - OUTER_RATE * (change + OUTER_BETA * momentum))
        )
    return (
        (block_output[None], input_grad[None], entry_m[None], entry_v[None], entry_new[None])
        + outer_parts[0]
        + (exit_m[None], exit_v[None], exit_new[None])
        + outer_parts[1]
        + (shared_m[None], shared_v[None], shared_new[None])
        + outer_parts[2]
        + (vector_m[None], vector_v[None], vector_new[None])
        + outer_parts[3]
    )


def solution(mesh):
    in_specs = (
        P(("group", "dp"), "mp", None),
        P(("group", "dp"), "mp"),
        P(("group", "dp"), "mp", None),
        P("group", "dp", "mp"),
        P("group", "dp", "mp"),
        P("group", "dp", "mp"),
        P("dp", "mp"),
        P("dp", "mp"),
        P("group", "mp", "dp"),
        P("group", "mp", "dp"),
        P("group", "mp", "dp"),
        P("mp", "dp"),
        P("mp", "dp"),
        P("group", ("dp", "mp"), None),
        P("group", ("dp", "mp"), None),
        P("group", ("dp", "mp"), None),
        P(("dp", "mp"), None),
        P(("dp", "mp"), None),
        P("group", None),
        P("group", None),
        P("group", None),
        P(),
        P(),
    )
    out_specs = (
        P(("group", "dp"), "mp", None),
        P(("group", "dp"), "mp", None),
        P("group", "dp", "mp"),
        P("group", "dp", "mp"),
        P("group", "dp", "mp"),
        P("dp", "mp"),
        P("dp", "mp"),
        P("dp", "mp"),
        P("group", "mp", "dp"),
        P("group", "mp", "dp"),
        P("group", "mp", "dp"),
        P("mp", "dp"),
        P("mp", "dp"),
        P("mp", "dp"),
        P("group", ("dp", "mp"), None),
        P("group", ("dp", "mp"), None),
        P("group", ("dp", "mp"), None),
        P(("dp", "mp"), None),
        P(("dp", "mp"), None),
        P(("dp", "mp"), None),
        P("group", None),
        P("group", None),
        P("group", None),
        P(),
        P(),
        P(),
    )
    return jax.shard_map(shards, mesh=mesh, in_specs=in_specs, out_specs=out_specs, check_vma=False)
```

time: 1200 us -> 439 us (0.37)
  waiting for transfers between devices: 578 us -> 134 us
  matrix products: 363 us -> 59 us
  starting transfers between devices: 0.83 us -> 79.2 us
  blocking collectives: 66.1 us -> 0 us
  Pallas kernels: 0 us -> 40.1 us
  loops' own time: 22.5 us -> 0 us
  local copies, waits for them, and re-layouts: 57.2 us -> 40.1 us
  between operations: 15.3 us -> 2.64 us
    reduce_scatter x7 -> x0, waiting for transfers between devices: 430 us -> none  [the longest x1 113 us: shards(): lax.psum_scatter(ffn_input_grad, 'mp', scatter_dimension=1, tiled=True)]
    dot_general x43 -> x15, matrix products: 363 us -> 59 us  [the longest x4 21.3 us: dot_nt(): lax.dot_general(left, right, (((1,), (1,)), ((), ())), preferred_element_...]
    ppermute x0 -> x49, waiting for transfers between devices: none -> 134 us  [the longest x12 52.8 us: swapped_parts(): return lax.ppermute(array, ('group', 'mp'), pairs)]
    psum x2 -> x0, waiting for transfers between devices: 95.7 us -> none  [shards(): lax.psum((entry_anchor - entry_new, exit_anchor - exit_new, shared_anchor...]
    ppermute x0 -> x49, starting transfers between devices: none -> 79.2 us  [the longest x12 46.6 us: swapped_parts(): return lax.ppermute(array, ('group', 'mp'), pairs)]
    all_gather x5 -> x0, waiting for transfers between devices: 50.5 us -> none  [the longest x1 50.4 us: shards(): lax.all_gather(attn_local, 'mp', axis=1, tiled=True)]
    pallas_call x0 -> x2, Pallas kernels: none -> 40.1 us  [the longest x1 24.7 us: attend_backward(): pl.pallas_call(backward_kernel, grid_spec=grid_spec, out_shape=[jax.Shape...]
    dynamic_update_slice x8 -> x0, local copies, waits for them, and re-layouts: 36.1 us -> none  [attend_backward(): lax.scan(one_step, (blank_grads, blank_grads), jnp.arange(number))]
  transfers between devices with their start and end apart: 14 -> 49, of which waited for: 9 -> 15; matrix products, arithmetic and copies ran while one was open for 41% -> 29% of each run, Pallas kernels for 0% -> 0%
where the time goes in v1:
time: 439 us; the launch traced here: 432 us
  waiting for transfers between devices  134 us (31%)
  starting transfers between devices  79.2 us (18%)
  other arithmetic  76.5 us (17%)
  matrix products  59 us (13%)
  local copies, waits for them, and re-layouts  40.1 us (9%)
  Pallas kernels  40.1 us (9%)
    ppermute x12, waiting for transfers between devices, swapped_parts(): return lax.ppermute(array, ('group', 'mp'), pairs)  52.8 us
    ppermute x9, waiting for transfers between devices, over_next(): return lax.ppermute(array, 'mp', pairs_of(lax.axis_size('mp'), 1))  52.1 us
    ppermute x12, starting transfers between devices, swapped_parts(): return lax.ppermute(array, ('group', 'mp'), pairs)  46.6 us
    ppermute x7, waiting for transfers between devices, over_dp(): return lax.ppermute(array, 'dp', pairs_of(2, 1))  25.9 us
    pallas_call x1, Pallas kernels, attend_backward(): pl.pallas_call(backward_kernel, grid_spec=grid_spec, out_shape=[jax.Shape...  24.7 us
    dot_general x4, matrix products, dot_nt(): lax.dot_general(left, right, (((1,), (1,)), ((), ())), preferred_element_...  21.3 us
    ppermute x17, starting transfers between devices, over_core(): return lax.ppermute(array, 'group', pairs_of(lax.axis_size('group'), 1))  18.4 us
    dot_general x4, matrix products, dot(): return jnp.dot(left, right, preferred_element_type=F32)  16 us
  transfers between devices with their start and end apart: 49, of which 15 were waited for; matrix products, arithmetic and copies ran while one was open for 29% of the time, Pallas kernels for 0%

profile of v1, /device:TPU:1, one launch (start us, length us, event | category | flops | bytes accessed | tf_op | source)
XLA Modules:
  0.0 431.6 jit_solution(15032093299631348724)
XLA Ops:
  0.7 5.7 %collective-permute-start.10 = (s32[512]{0:T(512)}, s32[512]{0:T(512)S(1)}, u32[]{:S(2)}, u32[]{:S(2)}) collective-permute-start(s32[512]{0:T(512)} %bitcast.287), channel_id=1, source_target_pairs={{0,0},{1,1},{2,8},{3,9},{8,2},{9,3},{10,10},{11,11},{16,16},{17,17... | collective-permute-start | bytes 6152 | tf_op jit(solution)/shard_map/ppermute | solution.py:263
  10.1 2.3 bitcast_convert_fusion
  12.4 4.5 %collective-permute-start.13 = (bf16[960,384]{1,0:T(8,128)(2,1)}, bf16[960,384]{1,0:T(8,128)(2,1)}, u32[]{:S(2)}, u32[]{:S(2)}) collective-permute-start(bf16[960,384]{1,0:T(8,128)(2,1)} %bitcast_convert_fusion), channel_id=1, source_target_pairs={{0,0},{1,1},{2,8},{3,9},{8,2},{9,3},{10,10},{11,11},{16,16},{17,17... | collective-permute-start | bytes 2211848 | tf_op jit(solution)/shard_map/ppermute | solution.py:263
  21.5 2.3 bitcast_convert_fusion.1
  26.0 8.1 %collective-permute-done.11 = s32[512]{0:T(512)S(1)} collective-permute-done((s32[512]{0:T(512)S(1)}, s32[512]{0:T(512)S(1)}, u32[]{:S(2)}, u32[]{:S(2)}) %collective-permute-start.11) | collective-permute-done | bytes 2080 | tf_op jit(solution)/shard_map/ppermute | solution.py:248
  36.0 4.6 %collective-permute-start = (bf16[384,960]{0,1:T(8,128)(2,1)}, bf16[384,960]{0,1:T(8,128)(2,1)}, u32[]{:S(2)}, u32[]{:S(2)}) collective-permute-start(bf16[384,960]{0,1:T(8,128)(2,1)} %bitcast_convert_fusion.1), channel_id=1, source_target_pairs={{0,0},{1,1},{2,8},{3,9},{8,2},{9,3},{10,10},{11,11},{16,16},{17,17... | collective-permute-start | bytes 2211848 | tf_op jit(solution)/shard_map/ppermute | solution.py:263
  41.1 8.6 %collective-permute-done.7 = bf16[96,128]{1,0:T(8,128)(2,1)S(1)} collective-permute-done((bf16[96,128]{1,0:T(8,128)(2,1)S(1)}, bf16[96,128]{1,0:T(8,128)(2,1)S(1)}, u32[]{:S(2)}, u32[]{:S(2)}) %collective-permute-start.7) | collective-permute-done | bytes 24608 | tf_op jit(solution)/shard_map/ppermute | solution.py:248
  49.7 5.1 %collective-permute-start.18 = (bf16[512,768]{1,0:T(8,128)(2,1)}, bf16[512,768]{1,0:T(8,128)(2,1)S(1)}, u32[]{:S(2)}, u32[]{:S(2)}) collective-permute-start(bf16[512,768]{1,0:T(8,128)(2,1)} %bitcast.270), channel_id=1, source_target_pairs={{0,0},{1,1},{2,8},{3,9},{8,2},{9,3},{10,10},{11,11},{16,16},{17,17... | collective-permute-start | bytes 2359304 | tf_op jit(solution)/shard_map/ppermute | solution.py:263
  55.0 5.6 %collective-permute-done.2 = bf16[512,768]{1,0:T(8,128)(2,1)S(1)} collective-permute-done((bf16[512,768]{1,0:T(8,128)(2,1)S(1)}, bf16[512,768]{1,0:T(8,128)(2,1)S(1)}, u32[]{:S(2)}, u32[]{:S(2)}) %collective-permute-start.2) | collective-permute-done | bytes 786464 | tf_op jit(solution)/shard_map/ppermute | solution.py:263
  67.7 24.9 %collective-permute-done.3 = bf16[512,768]{1,0:T(8,128)(2,1)S(1)} collective-permute-done((bf16[512,768]{1,0:T(8,128)(2,1)S(1)}, bf16[512,768]{1,0:T(8,128)(2,1)S(1)}, u32[]{:S(2)}, u32[]{:S(2)}) %collective-permute-start.3) | collective-permute-done | bytes 786464 | tf_op jit(solution)/shard_map/ppermute | solution.py:248
  98.5 13.0 %collective-permute-done.1 = bf16[384,960]{0,1:T(8,128)(2,1)S(1)} collective-permute-done((bf16[384,960]{0,1:T(8,128)(2,1)}, bf16[384,960]{0,1:T(8,128)(2,1)S(1)}, u32[]{:S(2)}, u32[]{:S(2)}) %collective-permute-start.1) | collective-permute-done | bytes 737312 | tf_op jit(solution)/shard_map/ppermute | solution.py:252
  119.5 4.1 add_convert_fusion.2
  136.0 15.4 %attend_rows.1 = (bf16[192,2048]{1,0:T(8,128)(2,1)S(1)}, f32[3,8,2048]{2,1,0:T(8,128)S(1)}) custom-call(s32[1]{0:T(128)} %bitcast.1.rank_ref, bf16[192,2048]{1,0:T(8,128)(2,1)S(1)} %bitcast.231, bf16[2048,64]{1,0:T(8,128)(2,1)S(1)} %copy.63.k_ref, bf16[64,2048]{1,0:T(8,128)(2,1)S(1)} %get-tuple-element.108.vt_ref, s32[1,2048]{1,0:T(1,128)S(1)} %bitcast.236, ...), custom_call_target="tpu_custom_call" | custom-call | flops 6442450944 | bytes 4194304 | tf_op jit(solution)/shard_map/attend_rows/pallas_call | solution.py:115
  153.7 24.7 %attend_rows_back.1 = (f32[192,2048]{1,0:T(8,128)S(1)}, f32[2048,64]{1,0:T(8,128)S(1)}, f32[2048,64]{1,0:T(8,128)S(1)}) custom-call(s32[1]{0:T(128)} %bitcast.1.rank_ref, bf16[192,2048]{1,0:T(8,128)(2,1)S(1)} %bitcast.232, bf16[192,2048]{1,0:T(8,128)(2,1)S(1)} %convolution_convert_fusion.do_ref, f32[3,8,2048]{2,1,0:T(8,128)S(1)} %get-tuple-element.32.l_ref, ...), custom_call_target="tpu_custom_call" | custom-call | flops 11274289152 | bytes 6291456 | tf_op jit(solution)/shard_map/attend_rows_back/pallas_call | solution.py:197
  182.8 6.9 %multiply_convert_fusion = (bf16[2048,768]{1,0:T(8,128)(2,1)S(1)}, f32[2048,768]{1,0:T(8,128)}) fusion(f32[768]{0:T(1024)S(1)} %copy-done.106, bf16[2048,768]{1,0:T(8,128)(2,1)} %get-tuple-element.83, bf16[384,960]{0,1:T(8,128)(2,1)S(1)} %copy-done.43, bf16[384,960]{0,1:T(8,128)(2,1)S(1)} %copy-done.40), kind=kOutput, calls=%fused_computation.16 | convolution fusion | flops 2427715584 | bytes 14060544 | tf_op jit(solution)/shard_map/dot_general | solution.py:34
  189.7 4.1 fusion.103
  193.8 4.7 %fusion.44 = f32[2048,768]{1,0:T(8,128)} fusion(bf16[2048,768]{1,0:T(8,128)(2,1)S(1)} %get-tuple-element.130, bf16[960,384]{1,0:T(8,128)(2,1)S(1)} %copy-done.48, bf16[960,384]{1,0:T(8,128)(2,1)S(1)} %copy-done.46), kind=kOutput, calls=%fused_computation.125 | convolution fusion | flops 2418278400 | bytes 10911744 | tf_op jit(solution)/shard_map/dot_general | solution.py:34
  205.4 7.9 %convert_reduce_fusion = (f32[768]{0:T(1024)}, bf16[2048,768]{1,0:T(8,128)(2,1)S(1)}) fusion(f32[2048,768]{1,0:T(8,128)} %get-tuple-element.131, f32[768]{0:T(1024)S(1)} %copy-done.107, bf16[2048,768]{1,0:T(8,128)(2,1)} %bitcast.239, bf16[960,384]{1,0:T(8,128)(2,1)S(1)} %copy-done.48, bf16[960,384]{1,0:T(8,128)(2,1)S(1)} %copy-done.46), kind=kOutput, calls=%fused_computation.11 | convolution fusion | flops 2438724864 | bytes 14063616 | tf_op jit(solution)/shard_map/dot_general | solution.py:38
  213.3 4.2 fusion.101
  217.5 3.9 convolution_add_fusion
  222.6 3.8 fusion.100
  228.4 2.4 slice.198
  230.8 3.9 add_convert_fusion
  238.4 5.8 %collective-permute-done.24 = f32[512,128]{0,1:T(8,128)S(1)} collective-permute-done((f32[512,128]{0,1:T(8,128)S(1)}, f32[512,128]{0,1:T(8,128)S(1)}, u32[]{:S(2)}, u32[]{:S(2)}) %collective-permute-start.24) | collective-permute-done | bytes 262176 | tf_op jit(solution)/shard_map/ppermute | solution.py:248
  244.2 2.4 fusion.40
  249.9 2.8 fusion.104
  254.2 3.0 collective-permute-done.37
  259.0 12.9 %collective-permute-done.38 = f32[1,96,128]{2,1,0:T(8,128)S(1)} collective-permute-done((f32[1,96,128]{2,1,0:T(8,128)S(1)}, f32[1,96,128]{2,1,0:T(8,128)S(1)}, u32[]{:S(2)}, u32[]{:S(2)}) %collective-permute-start.38) | collective-permute-done | bytes 49184 | tf_op jit(solution)/shard_map/ppermute | solution.py:252
  271.9 6.9 %collective-permute-start.39 = (f32[96,128]{1,0:T(8,128)S(1)}, f32[96,128]{1,0:T(8,128)S(1)}, u32[]{:S(2)}, u32[]{:S(2)}) collective-permute-start(f32[96,128]{1,0:T(8,128)S(1)} %add_bitcast_fusion), channel_id=1, source_target_pairs={{0,0},{1,1},{2,8},{3,9},{8,2},{9,3},{10,10},{11,11},{16,16},{17,17... | collective-permute-start | bytes 147464 | tf_op jit(solution)/shard_map/ppermute | solution.py:263
  278.9 8.6 %fusion.84 = (f32[768]{0:T(1024)S(1)}, f32[768]{0:T(1024)S(1)}, f32[2048,768]{1,0:T(8,128)S(1)}, f32[768]{0:T(1024)S(1)}, f32[768]{0:T(1024)S(1)}, /*index=5*/f32[2048,768]{1,0:T(8,128)}) fusion(f32[2048]{0:T(1024)S(1)} %bitcast.282, f32[2048]{0:T(1024)S(1)} %bitcast.280, bf16[2,512,768]{2,1,0:T(8,128)(2,1)S(1)} %copy-done.12, ...), kind=kOutput, calls=%fused_computation.245 | convolution fusion | flops 2440295424 | bytes 26675200 | tf_op jit(solution)/shard_map/dot_general | solution.py:38
  289.5 3.2 collective-permute-done.40
  297.8 5.6 %collective-permute-start.42 = (f32[48,128]{1,0:T(8,128)S(1)}, f32[48,128]{1,0:T(8,128)S(1)}, u32[]{:S(2)}, u32[]{:S(2)}) collective-permute-start(f32[48,128]{1,0:T(8,128)S(1)} %add.450), channel_id=1, source_target_pairs={{0,8},{8,0},{16,24},{24,16},{1,9},{9,1},{17,25},{25,17},{2,10},{10... | collective-permute-start | bytes 73736 | tf_op jit(solution)/shard_map/ppermute | solution.py:240
  307.8 25.2 %collective-permute-done.27 = bf16[384,960]{0,1:T(8,128)(2,1)S(1)} collective-permute-done((bf16[384,960]{0,1:T(8,128)(2,1)S(1)}, bf16[384,960]{0,1:T(8,128)(2,1)S(1)}, u32[]{:S(2)}, u32[]{:S(2)}) %collective-permute-start.27) | collective-permute-done | bytes 737312 | tf_op jit(solution)/shard_map/ppermute | solution.py:263
  333.0 3.0 fusion.94
  338.3 2.4 copy.71
  340.8 5.9 %fusion.91 = (f32[960,384]{1,0:T(8,128)S(1)}, f32[960,384]{1,0:T(8,128)}, f32[1,960,384]{2,1,0:T(8,128)}, f32[1,960,384]{2,1,0:T(8,128)}) fusion(f32[960,384]{1,0:T(8,128)} %param.34, f32[1,960,384]{2,1,0:T(8,128)} %param.33, f32[960,384]{1,0:T(8,128)} %get-tuple-element.66, bf16[960,384]{1,0:T(8,128)(2,1)} %collective-permute-done.32, pred[]{:T(512)S(6)} %ne.26, ...), kind=kLoop, calls=%fused_computation.250 | loop fusion | flops 6635520 | bytes 14008321 | tf_op jit(solution)/shard_map/sub | solution.py:508
  346.7 3.6 fusion.86
  357.9 2.4 copy.72
  360.4 3.8 collective-permute-start.46
  366.3 8.3 %collective-permute-done.46 = f32[8576]{0:T(1024)S(1)} collective-permute-done((f32[8576]{0:T(1024)S(1)}, f32[8576]{0:T(1024)S(1)}, u32[]{:S(2)}, u32[]{:S(2)}) %collective-permute-start.46) | collective-permute-done | bytes 34336 | tf_op jit(solution)/shard_map/ppermute | solution.py:263
  376.4 5.6 %collective-permute-start.25 = (bf16[512,768]{1,0:T(8,128)(2,1)}, bf16[512,768]{1,0:T(8,128)(2,1)}, u32[]{:S(2)}, u32[]{:S(2)}) collective-permute-start(bf16[512,768]{1,0:T(8,128)(2,1)} %get-tuple-element.90), channel_id=1, source_target_pairs={{0,0},{1,1},{2,8},{3,9},{8,2},{9,3},{10,10},{11,11},{16,16},{17,17... | collective-permute-start | bytes 2359304 | tf_op jit(solution)/shard_map/ppermute | solution.py:263
  385.4 2.2 collective-permute-start.17
  391.5 8.1 %collective-permute-start.30 = (f32[192,960]{1,0:T(8,128)S(1)}, f32[192,960]{1,0:T(8,128)}, u32[]{:S(2)}, u32[]{:S(2)}) collective-permute-start(f32[192,960]{1,0:T(8,128)S(1)} %copy.73), channel_id=1, source_target_pairs={{0,8},{8,0},{16,24},{24,16},{1,9},{9,1},{17,25},{25,17},{2,10},{10... | collective-permute-start | bytes 2211848 | tf_op jit(solution)/shard_map/ppermute | solution.py:240
  401.6 7.2 %collective-permute-done.25 = bf16[512,768]{1,0:T(8,128)(2,1)} collective-permute-done((bf16[512,768]{1,0:T(8,128)(2,1)}, bf16[512,768]{1,0:T(8,128)(2,1)}, u32[]{:S(2)}, u32[]{:S(2)}) %collective-permute-start.25) | collective-permute-done | bytes 786464 | tf_op jit(solution)/shard_map/ppermute | solution.py:263
  410.7 6.5 %collective-permute-done.17 = bf16[512,768]{1,0:T(8,128)(2,1)} collective-permute-done((bf16[512,768]{1,0:T(8,128)(2,1)}, bf16[512,768]{1,0:T(8,128)(2,1)}, u32[]{:S(2)}, u32[]{:S(2)}) %collective-permute-start.17) | collective-permute-done | bytes 786464 | tf_op jit(solution)/shard_map/ppermute | solution.py:263
  417.2 3.7 fusion.13
  424.3 2.6 multiply_subtract_fusion.1
  429.0 2.4 multiply_subtract_fusion
  (441 shorter events, 114.1 us)
Async XLA Ops:
  0.7 23.9 %collective-permute-start.10 = (s32[512]{0:T(512)}, s32[512]{0:T(512)S(1)}, u32[]{:S(2)}, u32[]{:S(2)}) collective-permute-start(s32[512]{0:T(512)} %bitcast.287), channel_id=1, source_target_pairs={{0,0},{1,1},{2,8},{3,9},{8,2},{9,3},{10,10},{11,11},{16,16},{17,17... | collective-permute-start | bytes 6152 | tf_op jit(solution)/shard_map/ppermute | solution.py:263
  7.2 33.3 %collective-permute-start.6 = (bf16[96,128]{1,0:T(8,128)(2,1)S(1)}, bf16[96,128]{1,0:T(8,128)(2,1)S(1)}, u32[]{:S(2)}, u32[]{:S(2)}) collective-permute-start(bf16[96,128]{1,0:T(8,128)(2,1)S(1)} %bitcast_convert_fusion.2), channel_id=1, source_target_pairs={{0,0},{1,1},{2,8},{3,9},{8,2},{9,3},{10,10},{11,11},{16,16},{17,17... | collective-permute-start | bytes 73736 | tf_op jit(solution)/shard_map/ppermute | solution.py:263
  10.0 44.9 %collective-permute-start.5 = (f32[8576]{0:T(1024)S(1)}, f32[8576]{0:T(1024)S(1)}, u32[]{:S(2)}, u32[]{:S(2)}) collective-permute-start(f32[8576]{0:T(1024)S(1)} %reduce.3), channel_id=1, source_target_pairs={{0,8},{8,0},{16,24},{24,16},{1,9},{9,1},{17,25},{25,17},{2,10},{10... | collective-permute-start | bytes 102920 | tf_op jit(solution)/shard_map/ppermute | solution.py:240
  12.4 55.1 %collective-permute-start.13 = (bf16[960,384]{1,0:T(8,128)(2,1)}, bf16[960,384]{1,0:T(8,128)(2,1)}, u32[]{:S(2)}, u32[]{:S(2)}) collective-permute-start(bf16[960,384]{1,0:T(8,128)(2,1)} %bitcast_convert_fusion), channel_id=1, source_target_pairs={{0,0},{1,1},{2,8},{3,9},{8,2},{9,3},{10,10},{11,11},{16,16},{17,17... | collective-permute-start | bytes 2211848 | tf_op jit(solution)/shard_map/ppermute | solution.py:263
  17.0 43.6 %collective-permute-start.2 = (bf16[512,768]{1,0:T(8,128)(2,1)S(1)}, bf16[512,768]{1,0:T(8,128)(2,1)S(1)}, u32[]{:S(2)}, u32[]{:S(2)}) collective-permute-start(bf16[512,768]{1,0:T(8,128)(2,1)S(1)} %bitcast.257), channel_id=1, source_target_pairs={{0,0},{1,1},{2,8},{3,9},{8,2},{9,3},{10,10},{11,11},{16,16},{17,17... | collective-permute-start | bytes 2359304 | tf_op jit(solution)/shard_map/ppermute | solution.py:263
  24.6 9.4 %collective-permute-start.11 = (s32[512]{0:T(512)S(1)}, s32[512]{0:T(512)S(1)}, u32[]{:S(2)}, u32[]{:S(2)}) collective-permute-start(s32[512]{0:T(512)S(1)} %collective-permute-done.10), channel_id=1, source_target_pairs={{0,1},{1,0},{2,3},{3,2},{4,5},{5,4},{6,7},{7,6},{8,9},{9,8},{10,11... | collective-permute-start | bytes 6152 | tf_op jit(solution)/shard_map/ppermute | solution.py:248
  36.0 57.8 %collective-permute-start = (bf16[384,960]{0,1:T(8,128)(2,1)}, bf16[384,960]{0,1:T(8,128)(2,1)}, u32[]{:S(2)}, u32[]{:S(2)}) collective-permute-start(bf16[384,960]{0,1:T(8,128)(2,1)} %bitcast_convert_fusion.1), channel_id=1, source_target_pairs={{0,0},{1,1},{2,8},{3,9},{8,2},{9,3},{10,10},{11,11},{16,16},{17,17... | collective-permute-start | bytes 2211848 | tf_op jit(solution)/shard_map/ppermute | solution.py:263
  40.6 9.1 %collective-permute-start.7 = (bf16[96,128]{1,0:T(8,128)(2,1)S(1)}, bf16[96,128]{1,0:T(8,128)(2,1)S(1)}, u32[]{:S(2)}, u32[]{:S(2)}) collective-permute-start(bf16[96,128]{1,0:T(8,128)(2,1)S(1)} %collective-permute-done.6), channel_id=1, source_target_pairs={{0,1},{1,0},{2,3},{3,2},{4,5},{5,4},{6,7},{7,6},{8,9},{9,8},{10,11... | collective-permute-start | bytes 73736 | tf_op jit(solution)/shard_map/ppermute | solution.py:248
  49.7 45.4 %collective-permute-start.18 = (bf16[512,768]{1,0:T(8,128)(2,1)}, bf16[512,768]{1,0:T(8,128)(2,1)S(1)}, u32[]{:S(2)}, u32[]{:S(2)}) collective-permute-start(bf16[512,768]{1,0:T(8,128)(2,1)} %bitcast.270), channel_id=1, source_target_pairs={{0,0},{1,1},{2,8},{3,9},{8,2},{9,3},{10,10},{11,11},{16,16},{17,17... | collective-permute-start | bytes 2359304 | tf_op jit(solution)/shard_map/ppermute | solution.py:263
  54.9 8.4 %collective-permute-start.8 = (bf16[2,96,128]{2,1,0:T(8,128)(2,1)S(1)}, bf16[2,96,128]{2,1,0:T(8,128)(2,1)S(1)}, u32[]{:S(2)}, u32[]{:S(2)}) collective-permute-start(bf16[2,96,128]{2,1,0:T(8,128)(2,1)S(1)} %pad_maximum_fusion.18), channel_id=1, source_target_pairs={{0,8},{8,0},{16,24},{24,16},{1,9},{9,1},{17,25},{25,17},{2,10},{10... | collective-permute-start | bytes 147464 | tf_op jit(solution)/shard_map/ppermute | solution.py:240
  60.6 32.1 %collective-permute-start.3 = (bf16[512,768]{1,0:T(8,128)(2,1)S(1)}, bf16[512,768]{1,0:T(8,128)(2,1)S(1)}, u32[]{:S(2)}, u32[]{:S(2)}) collective-permute-start(bf16[512,768]{1,0:T(8,128)(2,1)S(1)} %collective-permute-done.2), channel_id=1, source_target_pairs={{0,1},{1,0},{2,3},{3,2},{4,5},{5,4},{6,7},{7,6},{8,9},{9,8},{10,11... | collective-permute-start | bytes 2359304 | tf_op jit(solution)/shard_map/ppermute | solution.py:248
  66.2 28.8 %collective-permute-start.9 = (bf16[384,128]{1,0:T(8,128)(2,1)S(1)}, bf16[384,128]{1,0:T(8,128)(2,1)S(1)}, u32[]{:S(2)}, u32[]{:S(2)}) collective-permute-start(bf16[384,128]{1,0:T(8,128)(2,1)S(1)} %bitcast_select_fusion), channel_id=1, source_target_pairs={{0,4},{4,0},{1,5},{5,1},{2,6},{6,2},{3,7},{7,3},{8,12},{12,8},{9,1... | collective-permute-start | bytes 294920 | tf_op jit(solution)/shard_map/ppermute | solution.py:252
  67.5 28.5 %collective-permute-start.14 = (bf16[960,384]{1,0:T(8,128)(2,1)}, bf16[960,384]{1,0:T(8,128)(2,1)S(1)}, u32[]{:S(2)}, u32[]{:S(2)}) collective-permute-start(bf16[960,384]{1,0:T(8,128)(2,1)} %collective-permute-done.13), channel_id=1, source_target_pairs={{0,4},{4,0},{1,5},{5,1},{2,6},{6,2},{3,7},{7,3},{8,12},{12,8},{9,1... | collective-permute-start | bytes 2211848 | tf_op jit(solution)/shard_map/ppermute | solution.py:252
  92.8 23.7 %collective-permute-start.4 = (bf16[2,512,768]{2,1,0:T(8,128)(2,1)S(1)}, bf16[2,512,768]{2,1,0:T(8,128)(2,1)S(1)}, u32[]{:S(2)}, u32[]{:S(2)}) collective-permute-start(bf16[2,512,768]{2,1,0:T(8,128)(2,1)S(1)} %pad_maximum_fusion.2), channel_id=1, source_target_pairs={{0,8},{8,0},{16,24},{24,16},{1,9},{9,1},{17,25},{25,17},{2,10},{10... | collective-permute-start | bytes 4718600 | tf_op jit(solution)/shard_map/ppermute | solution.py:240
  93.7 17.8 %collective-permute-start.1 = (bf16[384,960]{0,1:T(8,128)(2,1)}, bf16[384,960]{0,1:T(8,128)(2,1)S(1)}, u32[]{:S(2)}, u32[]{:S(2)}) collective-permute-start(bf16[384,960]{0,1:T(8,128)(2,1)} %collective-permute-done), channel_id=1, source_target_pairs={{0,4},{4,0},{1,5},{5,1},{2,6},{6,2},{3,7},{7,3},{8,12},{12,8},{9,1... | collective-permute-start | bytes 2211848 | tf_op jit(solution)/shard_map/ppermute | solution.py:252
  95.1 18.4 %collective-permute-start.19 = (bf16[512,768]{1,0:T(8,128)(2,1)S(1)}, bf16[512,768]{1,0:T(8,128)(2,1)S(1)}, u32[]{:S(2)}, u32[]{:S(2)}) collective-permute-start(bf16[512,768]{1,0:T(8,128)(2,1)S(1)} %collective-permute-done.18), channel_id=1, source_target_pairs={{0,1},{1,0},{2,3},{3,2},{4,5},{5,4},{6,7},{7,6},{8,9},{9,8},{10,11... | collective-permute-start | bytes 2359304 | tf_op jit(solution)/shard_map/ppermute | solution.py:248
  115.2 15.7 %collective-permute-start.20 = (bf16[2,512,768]{2,1,0:T(8,128)(2,1)}, bf16[2,512,768]{2,1,0:T(8,128)(2,1)}, u32[]{:S(2)}, u32[]{:S(2)}) collective-permute-start(bf16[2,512,768]{2,1,0:T(8,128)(2,1)} %pad_maximum_fusion.3), channel_id=1, source_target_pairs={{0,8},{8,0},{16,24},{24,16},{1,9},{9,1},{17,25},{25,17},{2,10},{10... | collective-permute-start | bytes 4718600 | tf_op jit(solution)/shard_map/ppermute | solution.py:240
  205.4 29.3 %collective-permute-start.23 = (f32[2,512,128]{1,0,2:T(2,128)}, f32[2,512,128]{1,0,2:T(2,128)}, u32[]{:S(2)}, u32[]{:S(2)}) collective-permute-start(f32[2,512,128]{1,0,2:T(2,128)} %slice.200), channel_id=1, source_target_pairs={{0,8},{8,0},{16,24},{24,16},{1,9},{9,1},{17,25},{25,17},{2,10},{10... | collective-permute-start | bytes 1572872 | tf_op jit(solution)/shard_map/ppermute | solution.py:240
  236.7 7.4 %collective-permute-start.24 = (f32[512,128]{0,1:T(8,128)S(1)}, f32[512,128]{0,1:T(8,128)S(1)}, u32[]{:S(2)}, u32[]{:S(2)}) collective-permute-start(f32[512,128]{0,1:T(8,128)S(1)} %bitcast.271), channel_id=1, source_target_pairs={{0,1},{1,0},{2,3},{3,2},{4,5},{5,4},{6,7},{7,6},{8,9},{9,8},{10,11... | collective-permute-start | bytes 786440 | tf_op jit(solution)/shard_map/ppermute | solution.py:248
  248.4 4.2 collective-permute-start.36
  252.7 4.4 %collective-permute-start.37 = (f32[2,96,128]{2,1,0:T(8,128)S(1)}, f32[2,96,128]{2,1,0:T(8,128)S(1)}, u32[]{:S(2)}, u32[]{:S(2)}) collective-permute-start(f32[2,96,128]{2,1,0:T(8,128)S(1)} %slice_bitcast_fusion.2), channel_id=1, source_target_pairs={{0,1},{1,0},{2,3},{3,2},{4,5},{5,4},{6,7},{7,6},{8,9},{9,8},{10,11... | collective-permute-start | bytes 294920 | tf_op jit(solution)/shard_map/ppermute | solution.py:248
  253.0 41.0 %collective-permute-start.31 = (bf16[960,384]{1,0:T(8,128)(2,1)S(1)}, bf16[960,384]{1,0:T(8,128)(2,1)S(1)}, u32[]{:S(2)}, u32[]{:S(2)}) collective-permute-start(bf16[960,384]{1,0:T(8,128)(2,1)S(1)} %fusion.27), channel_id=1, source_target_pairs={{0,4},{4,0},{1,5},{5,1},{2,6},{6,2},{3,7},{7,3},{8,12},{12,8},{9,1... | collective-permute-start | bytes 2211848 | tf_op jit(solution)/shard_map/ppermute | solution.py:252
  257.3 14.6 %collective-permute-start.38 = (f32[1,96,128]{2,1,0:T(8,128)S(1)}, f32[1,96,128]{2,1,0:T(8,128)S(1)}, u32[]{:S(2)}, u32[]{:S(2)}) collective-permute-start(f32[1,96,128]{2,1,0:T(8,128)S(1)} %constant_dynamic-slice_fusion.1), channel_id=1, source_target_pairs={{0,4},{4,0},{1,5},{5,1},{2,6},{6,2},{3,7},{7,3},{8,12},{12,8},{9,1... | collective-permute-start | bytes 147464 | tf_op jit(solution)/shard_map/ppermute | solution.py:252
  258.6 44.7 %collective-permute-start.26 = (bf16[384,960]{0,1:T(8,128)(2,1)S(1)}, bf16[384,960]{0,1:T(8,128)(2,1)S(1)}, u32[]{:S(2)}, u32[]{:S(2)}) collective-permute-start(bf16[384,960]{0,1:T(8,128)(2,1)S(1)} %fusion.31), channel_id=1, source_target_pairs={{0,4},{4,0},{1,5},{5,1},{2,6},{6,2},{3,7},{7,3},{8,12},{12,8},{9,1... | collective-permute-start | bytes 2211848 | tf_op jit(solution)/shard_map/ppermute | solution.py:252
  271.9 16.5 %collective-permute-start.39 = (f32[96,128]{1,0:T(8,128)S(1)}, f32[96,128]{1,0:T(8,128)S(1)}, u32[]{:S(2)}, u32[]{:S(2)}) collective-permute-start(f32[96,128]{1,0:T(8,128)S(1)} %add_bitcast_fusion), channel_id=1, source_target_pairs={{0,0},{1,1},{2,8},{3,9},{8,2},{9,3},{10,10},{11,11},{16,16},{17,17... | collective-permute-start | bytes 147464 | tf_op jit(solution)/shard_map/ppermute | solution.py:263
  287.7 18.6 %collective-permute-start.21 = (bf16[2,512,768]{2,1,0:T(8,128)(2,1)S(1)}, bf16[2,512,768]{2,1,0:T(8,128)(2,1)S(1)}, u32[]{:S(2)}, u32[]{:S(2)}) collective-permute-start(bf16[2,512,768]{2,1,0:T(8,128)(2,1)S(1)} %bitcast.266), channel_id=1, source_target_pairs={{0,8},{8,0},{16,24},{24,16},{1,9},{9,1},{17,25},{25,17},{2,10},{10... | collective-permute-start | bytes 4718600 | tf_op jit(solution)/shard_map/ppermute | solution.py:240
  287.8 64.6 %collective-permute-start.15 = (bf16[2,512,768]{2,1,0:T(8,128)(2,1)}, bf16[2,512,768]{2,1,0:T(8,128)(2,1)}, u32[]{:S(2)}, u32[]{:S(2)}) collective-permute-start(bf16[2,512,768]{2,1,0:T(8,128)(2,1)} %bitcast.19), channel_id=1, source_target_pairs={{0,8},{8,0},{16,24},{24,16},{1,9},{9,1},{17,25},{25,17},{2,10},{10... | collective-permute-start | bytes 4718600 | tf_op jit(solution)/shard_map/ppermute | solution.py:240
  289.1 3.7 collective-permute-start.40
  292.8 5.0 %collective-permute-start.41 = (f32[48,128]{1,0:T(8,128)S(1)}, f32[48,128]{1,0:T(8,128)S(1)}, u32[]{:S(2)}, u32[]{:S(2)}) collective-permute-start(f32[48,128]{1,0:T(8,128)S(1)} %dynamic-slice_add_fusion), channel_id=1, source_target_pairs={{0,16},{8,24},{16,0},{24,8},{1,17},{9,25},{17,1},{25,9},{2,18},{10... | collective-permute-start | bytes 73736 | tf_op jit(solution)/shard_map/ppermute | solution.py:244
  295.5 45.2 %collective-permute-start.32 = (bf16[960,384]{1,0:T(8,128)(2,1)}, bf16[960,384]{1,0:T(8,128)(2,1)}, u32[]{:S(2)}, u32[]{:S(2)}) collective-permute-start(bf16[960,384]{1,0:T(8,128)(2,1)} %get-tuple-element.65), channel_id=1, source_target_pairs={{0,0},{1,1},{2,8},{3,9},{8,2},{9,3},{10,10},{11,11},{16,16},{17,17... | collective-permute-start | bytes 2211848 | tf_op jit(solution)/shard_map/ppermute | solution.py:263
  297.8 7.9 %collective-permute-start.42 = (f32[48,128]{1,0:T(8,128)S(1)}, f32[48,128]{1,0:T(8,128)S(1)}, u32[]{:S(2)}, u32[]{:S(2)}) collective-permute-start(f32[48,128]{1,0:T(8,128)S(1)} %add.450), channel_id=1, source_target_pairs={{0,8},{8,0},{16,24},{24,16},{1,9},{9,1},{17,25},{25,17},{2,10},{10... | collective-permute-start | bytes 73736 | tf_op jit(solution)/shard_map/ppermute | solution.py:240
  303.5 29.4 %collective-permute-start.27 = (bf16[384,960]{0,1:T(8,128)(2,1)S(1)}, bf16[384,960]{0,1:T(8,128)(2,1)S(1)}, u32[]{:S(2)}, u32[]{:S(2)}) collective-permute-start(bf16[384,960]{0,1:T(8,128)(2,1)S(1)} %get-tuple-element.72), channel_id=1, source_target_pairs={{0,0},{1,1},{2,8},{3,9},{8,2},{9,3},{10,10},{11,11},{16,16},{17,17... | collective-permute-start | bytes 2211848 | tf_op jit(solution)/shard_map/ppermute | solution.py:263
  307.8 38.9 %collective-permute-start.22 = (bf16[512,768]{1,0:T(8,128)(2,1)}, bf16[512,768]{1,0:T(8,128)(2,1)}, u32[]{:S(2)}, u32[]{:S(2)}) collective-permute-start(bf16[512,768]{1,0:T(8,128)(2,1)} %fusion.39), channel_id=1, source_target_pairs={{0,1},{1,0},{2,3},{3,2},{4,5},{5,4},{6,7},{7,6},{8,9},{9,8},{10,11... | collective-permute-start | bytes 2359304 | tf_op jit(solution)/shard_map/ppermute | solution.py:248
  340.7 17.2 %collective-permute-start.28 = (f32[192,960]{1,0:T(8,128)}, f32[192,960]{1,0:T(8,128)}, u32[]{:S(2)}, u32[]{:S(2)}) collective-permute-start(f32[192,960]{1,0:T(8,128)} %copy.71), channel_id=1, source_target_pairs={{0,8},{8,0},{16,24},{24,16},{1,9},{9,1},{17,25},{25,17},{2,10},{10... | collective-permute-start | bytes 2211848 | tf_op jit(solution)/shard_map/ppermute | solution.py:240
  350.4 1.9 collective-permute-start.43
  352.3 22.5 %collective-permute-start.33 = (f32[480,384]{1,0:T(8,128)}, f32[480,384]{1,0:T(8,128)}, u32[]{:S(2)}, u32[]{:S(2)}) collective-permute-start(f32[480,384]{1,0:T(8,128)} %constant_dynamic-slice_fusion.2), channel_id=1, source_target_pairs={{0,8},{8,0},{16,24},{24,16},{1,9},{9,1},{17,25},{25,17},{2,10},{10... | collective-permute-start | bytes 2211848 | tf_op jit(solution)/shard_map/ppermute | solution.py:240
  352.3 2.9 collective-permute-start.44
  355.2 5.1 %collective-permute-start.45 = (f32[8576]{0:T(1024)S(1)}, f32[8576]{0:T(1024)S(1)}, u32[]{:S(2)}, u32[]{:S(2)}) collective-permute-start(f32[8576]{0:T(1024)S(1)} %add.457), channel_id=1, source_target_pairs={{0,4},{4,0},{1,5},{5,1},{2,6},{6,2},{3,7},{7,3},{8,12},{12,8},{9,1... | collective-permute-start | bytes 102920 | tf_op jit(solution)/shard_map/ppermute | solution.py:252
  357.4 25.9 %collective-permute-start.16 = (bf16[512,768]{1,0:T(8,128)(2,1)}, bf16[512,768]{1,0:T(8,128)(2,1)}, u32[]{:S(2)}, u32[]{:S(2)}) collective-permute-start(bf16[512,768]{1,0:T(8,128)(2,1)} %fusion.38), channel_id=1, source_target_pairs={{0,1},{1,0},{2,3},{3,2},{4,5},{5,4},{6,7},{7,6},{8,9},{9,8},{10,11... | collective-permute-start | bytes 2359304 | tf_op jit(solution)/shard_map/ppermute | solution.py:248
  360.4 14.3 %collective-permute-start.46 = (f32[8576]{0:T(1024)S(1)}, f32[8576]{0:T(1024)S(1)}, u32[]{:S(2)}, u32[]{:S(2)}) collective-permute-start(f32[8576]{0:T(1024)S(1)} %add.458), channel_id=1, source_target_pairs={{0,0},{1,1},{2,8},{3,9},{8,2},{9,3},{10,10},{11,11},{16,16},{17,17... | collective-permute-start | bytes 102920 | tf_op jit(solution)/shard_map/ppermute | solution.py:263
  366.0 24.2 %collective-permute-start.29 = (bf16[192,960]{0,1:T(8,128)(2,1)S(1)}, bf16[192,960]{0,1:T(8,128)(2,1)S(1)}, u32[]{:S(2)}, u32[]{:S(2)}) collective-permute-start(bf16[192,960]{0,1:T(8,128)(2,1)S(1)} %add_convert_fusion.3), channel_id=1, source_target_pairs={{0,16},{8,24},{16,0},{24,8},{1,17},{9,25},{17,1},{25,9},{2,18},{10... | collective-permute-start | bytes 1105928 | tf_op jit(solution)/shard_map/ppermute | solution.py:244
  374.7 7.2 %collective-permute-start.47 = (f32[8576]{0:T(1024)S(1)}, f32[8576]{0:T(1024)S(1)}, u32[]{:S(2)}, u32[]{:S(2)}) collective-permute-start(f32[8576]{0:T(1024)S(1)} %get-tuple-element.47), channel_id=1, source_target_pairs={{0,8},{8,0},{16,24},{24,16},{1,9},{9,1},{17,25},{25,17},{2,10},{10... | collective-permute-start | bytes 102920 | tf_op jit(solution)/shard_map/ppermute | solution.py:240
  376.0 23.6 %collective-permute-start.34 = (bf16[480,384]{1,0:T(8,128)(2,1)S(1)}, bf16[480,384]{1,0:T(8,128)(2,1)}, u32[]{:S(2)}, u32[]{:S(2)}) collective-permute-start(bf16[480,384]{1,0:T(8,128)(2,1)S(1)} %add_convert_fusion.4), channel_id=1, source_target_pairs={{0,16},{8,24},{16,0},{24,8},{1,17},{9,25},{17,1},{25,9},{2,18},{10... | collective-permute-start | bytes 1105928 | tf_op jit(solution)/shard_map/ppermute | solution.py:244
  376.4 32.4 %collective-permute-start.25 = (bf16[512,768]{1,0:T(8,128)(2,1)}, bf16[512,768]{1,0:T(8,128)(2,1)}, u32[]{:S(2)}, u32[]{:S(2)}) collective-permute-start(bf16[512,768]{1,0:T(8,128)(2,1)} %get-tuple-element.90), channel_id=1, source_target_pairs={{0,0},{1,1},{2,8},{3,9},{8,2},{9,3},{10,10},{11,11},{16,16},{17,17... | collective-permute-start | bytes 2359304 | tf_op jit(solution)/shard_map/ppermute | solution.py:263
  382.0 7.6 %collective-permute-start.48 = (f32[8576]{0:T(1024)S(1)}, f32[8576]{0:T(1024)S(1)}, u32[]{:S(2)}, u32[]{:S(2)}) collective-permute-start(f32[8576]{0:T(1024)S(1)} %add.464), channel_id=1, source_target_pairs={{0,16},{8,24},{16,0},{24,8},{1,17},{9,25},{17,1},{25,9},{2,18},{10... | collective-permute-start | bytes 102920 | tf_op jit(solution)/shard_map/ppermute | solution.py:244
  385.4 31.8 %collective-permute-start.17 = (bf16[512,768]{1,0:T(8,128)(2,1)}, bf16[512,768]{1,0:T(8,128)(2,1)}, u32[]{:S(2)}, u32[]{:S(2)}) collective-permute-start(bf16[512,768]{1,0:T(8,128)(2,1)} %fusion.23), channel_id=1, source_target_pairs={{0,0},{1,1},{2,8},{3,9},{8,2},{9,3},{10,10},{11,11},{16,16},{17,17... | collective-permute-start | bytes 2359304 | tf_op jit(solution)/shard_map/ppermute | solution.py:263
  391.5 29.4 %collective-permute-start.30 = (f32[192,960]{1,0:T(8,128)S(1)}, f32[192,960]{1,0:T(8,128)}, u32[]{:S(2)}, u32[]{:S(2)}) collective-permute-start(f32[192,960]{1,0:T(8,128)S(1)} %copy.73), channel_id=1, source_target_pairs={{0,8},{8,0},{16,24},{24,16},{1,9},{9,1},{17,25},{25,17},{2,10},{10... | collective-permute-start | bytes 2211848 | tf_op jit(solution)/shard_map/ppermute | solution.py:240
  401.5 25.4 %collective-permute-start.35 = (f32[480,384]{1,0:T(8,128)}, f32[480,384]{1,0:T(8,128)}, u32[]{:S(2)}, u32[]{:S(2)}) collective-permute-start(f32[480,384]{1,0:T(8,128)} %convert_add_fusion.4), channel_id=1, source_target_pairs={{0,8},{8,0},{16,24},{24,16},{1,9},{9,1},{17,25},{25,17},{2,10},{10... | collective-permute-start | bytes 2211848 | tf_op jit(solution)/shard_map/ppermute | solution.py:240
  (118 other events, 1237.2 us)

commit v2 on v1

v2 whole, which is shorter than its diff:
```python
import functools
import math

import jax
import jax.numpy as jnp
import numpy as np
from jax import lax
from jax.experimental import pallas as pl
from jax.experimental.pallas import tpu as pltpu
from jax.sharding import PartitionSpec as P

D = 768
HEADS = 12
HS = 64
ROT = 16
STEP = 5
IN_COLS = 3840


NORM_EPS = 1e-05
BETA_ONE = 0.9
BETA_TWO = 0.95
ADAM_EPS = 1e-08
MATRIX_RATE = 0.03
MATRIX_DECAY = 0.1
VECTOR_RATE = 0.3
OUTER_RATE = 0.7
OUTER_BETA = 0.9

TILE = 256
F32 = jnp.float32
BF = jnp.bfloat16


def dot(left, right):
    return jnp.dot(left, right, preferred_element_type=F32)


def dot_nt(left, right):
    return lax.dot_general(left, right, (((1,), (1,)), ((), ())), preferred_element_type=F32)


def dot_tn(left, right):
    return lax.dot_general(left, right, (((0,), (0,)), ((), ())), preferred_element_type=F32)


def adamw_update(weight, first, second, gradient, step_rate, decay):
    first_new = BETA_ONE * first + (1.0 - BETA_ONE) * gradient
    second_new = BETA_TWO * second + (1.0 - BETA_TWO) * gradient * gradient
    fix_first = 1.0 - BETA_ONE**STEP
    fix_second = 1.0 - BETA_TWO**STEP
    update = first_new / fix_first / (jnp.sqrt(second_new / fix_second) + ADAM_EPS)
    return (first_new, second_new, weight - step_rate * (update + decay * weight))


def pairs_of(size, bit):
    return [(at, at ^ bit) for at in range(size)]


def over_core(array):
    return lax.ppermute(array, "group", pairs_of(lax.axis_size("group"), 1))


def over_half(array):
    return lax.ppermute(array, "group", pairs_of(lax.axis_size("group"), 2))


def over_next(array):
    return lax.ppermute(array, "mp", pairs_of(lax.axis_size("mp"), 1))


def over_dp(array):
    return lax.ppermute(array, "dp", pairs_of(2, 1))


def swapped_parts(array):
    parts = lax.axis_size("mp")
    pairs = []
    for group in range(lax.axis_size("group")):
        for rank in range(parts):
            here = group * parts + rank
            there = (group ^ 1) * parts + (rank ^ 2)
            pairs.append((here, there if group % 2 != rank // 2 else here))
    return lax.ppermute(array, ("group", "mp"), pairs)


def gather_square(own):
    pair = jnp.stack([own, over_next(own)])
    return jnp.concatenate([pair, over_core(pair)], 0)


def scatter_square(slots, send_type):
    pair = slots[:2] + over_core(slots[2:].astype(send_type)).astype(F32)
    return pair[0] + over_next(pair[1].astype(send_type)).astype(F32)


def sum_square(array):
    array = array + over_core(array)
    return array + over_next(array)


def gather_dp(own, axis):
    if lax.axis_size("dp") == 2:
        other = over_dp(own)
        first = lax.axis_index("dp") == 0
        return jnp.concatenate(
            [jnp.where(first, own, other), jnp.where(first, other, own)], axis
        )
    return lax.all_gather(own, "dp", axis=axis, tiled=True)


def scatter_dp(array, axis, send_type):
    if lax.axis_size("dp") == 2:
        size = array.shape[axis] // 2
        mine = lax.axis_index("dp")
        kept = lax.dynamic_slice_in_dim(array, mine * size, size, axis)
        sent = lax.dynamic_slice_in_dim(array, (1 - mine) * size, size, axis)
        return kept + over_dp(sent.astype(send_type)).astype(F32)
    return lax.psum_scatter(array, "dp", scatter_dimension=axis, tiled=True)


def sum_dp(array):
    if lax.axis_size("dp") == 2:
        return array + over_dp(array)
    return lax.psum(array, "dp")


def sum_groups(array, send_type):
    size = array.shape[0] // 2
    core = lax.axis_index("group") % 2
    kept = lax.dynamic_slice_in_dim(array, core * size, size, 0)
    sent = lax.dynamic_slice_in_dim(array, (1 - core) * size, size, 0)
    part = (kept + over_core(sent)).astype(send_type)
    part = part.astype(F32) + over_half(part).astype(F32)
    other = over_core(part)
    low = core == 0
    return jnp.concatenate([jnp.where(low, part, other), jnp.where(low, other, part)], 0)


def flip_one(index):
    return index + 1 - 2 * (index % 2)


def flip_two(index):
    return index + 2 - 4 * ((index // 2) % 2)


def at_slot(slot, rank):
    rank = flip_one(rank) if slot % 2 else rank
    return flip_two(rank) if slot // 2 else rank


class Copies:
    def __init__(self, send, receive):
        self.send, self.receive, self.used, self.sends = (send, receive, 0, [])

    def remote(self, source, target, device):
        at = self.used
        self.used += 1
        copy = pltpu.make_async_remote_copy(
            src_ref=source,
            dst_ref=target,
            send_sem=self.send.at[at],
            recv_sem=self.receive.at[at],
            device_id=device,
            device_id_type=pl.DeviceIdType.MESH,
        )
        copy.start()
        self.sends.append(copy)
        return copy

    def swapped(self, source, target, is_swapped, device):
        at = self.used
        self.used += 1
        far = pltpu.make_async_remote_copy(
            src_ref=source,
            dst_ref=target,
            send_sem=self.send.at[at],
            recv_sem=self.receive.at[at],
            device_id=device,
            device_id_type=pl.DeviceIdType.MESH,
        )
        near = pltpu.make_async_copy(source, target, self.receive.at[at])

        @pl.when(is_swapped)
        def _():
            far.start()

        @pl.when(jnp.logical_not(is_swapped))
        def _():
            near.start()

        def wait():
            @pl.when(is_swapped)
            def _():
                far.wait_send()
                far.wait_recv()

            @pl.when(jnp.logical_not(is_swapped))
            def _():
                near.wait()

        return wait

    def finish(self):
        for copy in self.sends:
            copy.wait_send()


class Place:
    def __init__(self, dp_size):
        group, self.dp, home = (lax.axis_index("group"), lax.axis_index("dp"), lax.axis_index("mp"))
        core, upper = (group % 2, home // 2)
        self.is_swapped = core != upper
        self.home = home
        self.rank = jnp.where(self.is_swapped, flip_two(home), home)
        self.swap = {"group": flip_one(group), "mp": flip_two(home)}
        self.core = {"group": flip_one(group)}
        self.next = {"mp": flip_one(home)}
        self.dp_peers = [{"dp": (self.dp + step) % dp_size} for step in range(1, dp_size)]

    def meet(self):
        barrier = pltpu.get_barrier_semaphore()
        peers = [self.core, self.next, self.swap] + self.dp_peers
        for peer in peers:
            pl.semaphore_signal(
                barrier, inc=1, device_id=peer, device_id_type=pl.DeviceIdType.MESH
            )
        pl.semaphore_wait(barrier, len(peers))


def rotate(rows, cosine, sine):
    half = ROT // 2
    one, two = (rows[:half], rows[half:ROT])
    return jnp.concatenate(
        [one * cosine - two * sine, two * cosine + one * sine, rows[ROT:]], 0
    )


def first_kernel(
    dp_size, x_ref, c_ref, small_ref, big_ref, pair_ref, ids_ref, norm_ref, qb_ref, kvb_ref, cos_ref, sin_ref,
    xg, cg, a1, a2, big, small, kvw, ot, dqt, pair_grad,
    smt, kvt, qt, dot_rows, kt, vt, k, v, dk, dv, s_ref, d_ref, idr, send, receive,
):
    place = Place(dp_size)
    rank, dp = (place.rank, place.dp)
    copies = Copies(send, receive)
    local = x_ref.shape[0]
    length = 4 * local
    rows = small_ref.shape[0]
    query_width = small_ref.shape[1] // 2
    heads = query_width // HS
    gathers_pair = pair_ref.shape[0] != D
    place.meet()

    def swapped(source, target):
        return copies.swapped(source, target, place.is_swapped, place.swap)

    def dp_rows(ref, start, size):
        return ref.at[pl.ds(pl.multiple_of(dp * rows + start, 16), size)]

    step = local // 2
    spans = [pl.ds(at * step, step) for at in range(2)]
    x_swaps = [swapped(x_ref.at[s], xg.at[0, s]) for s in spans]
    small_swap = swapped(small_ref, dp_rows(small, 0, rows))
    if gathers_pair:
        pair_swap = swapped(pair_ref, kvw.at[dp, place.home])
    ids_swap = swapped(ids_ref, idr.at[:, pl.ds(0, local)])
    c_swaps = [swapped(c_ref.at[s], cg.at[0, s]) for s in spans]
    chunk = rows // 4 if rows % 64 == 0 else rows
    big_swaps = [
        swapped(big_ref.at[pl.ds(at, chunk)], dp_rows(big, at, chunk)) for at in range(0, rows, chunk)
    ]

    def normalise(slot):
        def body(at, carry):
            span = pl.ds(pl.multiple_of(at * 128, 128), 128)
            wide = xg[slot, span, :].astype(F32)
            centered = wide - jnp.mean(wide, -1, keepdims=True)
            normal = centered * lax.rsqrt(
                jnp.mean(centered * centered, -1, keepdims=True) + NORM_EPS
            )
            a1[slot, span, :] = (normal * norm_ref[0:1, :] + norm_ref[1:2, :]).astype(BF)
            a2[slot, span, :] = (normal * norm_ref[2:3, :] + norm_ref[3:4, :]).astype(BF)
            return carry

        lax.fori_loop(0, local // 128, body, 0)

    def lanes(ref, slot):
        return ref.at[:, pl.ds(slot * local, local)]

    x_next, x_core, x_far = ([], [], [])
    for span, wait in zip(spans, x_swaps):
        wait()
        x_next.append(copies.remote(xg.at[0, span], xg.at[1, span], place.next))
        x_core.append(copies.remote(xg.at[0, span], xg.at[2, span], place.core))
    normalise(0)
    small_swap()
    small_dp = [copies.remote(dp_rows(small, 0, rows), dp_rows(small, 0, rows), peer) for peer in place.dp_peers]
    if gathers_pair:
        pair_swap()
        own_pair = kvw.at[dp, rank]
        pair_next = copies.remote(own_pair, own_pair, place.next)
        pair_core = copies.remote(own_pair, own_pair, place.core)
    ids_swap()
    ids_next = copies.remote(lanes(idr, 0), lanes(idr, 1), place.next)
    ids_core = copies.remote(lanes(idr, 0), lanes(idr, 2), place.core)
    for span, copy in zip(spans, x_next):
        copy.wait_recv()
        x_far.append(copies.remote(xg.at[1, span], xg.at[3, span], place.core))
    if gathers_pair:
        pair_next.wait_recv()
        next_pair = kvw.at[dp, flip_one(rank)]
        pair_far = copies.remote(next_pair, next_pair, place.core)
    ids_next.wait_recv()
    ids_far = copies.remote(lanes(idr, 1), lanes(idr, 3), place.core)
    if gathers_pair:
        pair_core.wait_recv()
        pair_far.wait_recv()
        pair_dp = [copies.remote(kvw.at[dp], kvw.at[dp], peer) for peer in place.dp_peers]
    for copy in x_core:
        copy.wait_recv()
    normalise(2)
    c_next, c_core, c_far = ([], [], [])
    for span, wait in zip(spans, c_swaps):
        wait()
        c_next.append(copies.remote(cg.at[0, span], cg.at[1, span], place.next))
        c_core.append(copies.remote(cg.at[0, span], cg.at[2, span], place.core))
    normalise(1)
    for copy in x_far:
        copy.wait_recv()
    normalise(3)
    for copy in small_dp:
        copy.wait_recv()
    smt[...] = small[...].T
    if gathers_pair:
        for copy in pair_dp:
            copy.wait_recv()
        kvt[...] = kvw[...].reshape(D, 2 * HS).T
    else:
        kvw[...] = pair_ref[...]
        kvt[...] = pair_ref[...].T
    for slot in range(4):
        block = at_slot(slot, rank)
        table = pl.ds(pl.multiple_of(block * local, local), local)
        cosine, sine = (cos_ref[:, table], sin_ref[:, table])
        tokens = pl.ds(slot * local, local)
        queries = dot_nt(smt[0:query_width, :], a1[slot]) + qb_ref[...]
        for head in range(heads):
            turned = rotate(queries[head * HS : (head + 1) * HS], cosine, sine).astype(BF)
            qt[head * HS : (head + 1) * HS, tokens] = turned * jnp.asarray(1.0 / math.sqrt(HS), BF)
        pairs = dot_nt(kvt[...], a1[slot]) + kvb_ref[...]
        turned = rotate(pairs[:HS], cosine, sine).astype(BF)
        kt[:, tokens] = turned
        k[tokens, :] = turned.T
        value = pairs[HS:].astype(BF)
        vt[:, tokens] = value
        v[tokens, :] = value.T
    for span, copy in zip(spans, c_next):
        copy.wait_recv()
        c_far.append(copies.remote(cg.at[1, span], cg.at[3, span], place.core))
    for copy in c_core + c_far:
        copy.wait_recv()
    for slot in range(4):
        tokens = pl.ds(slot * local, local)
        dot_rows[:, tokens] = dot_nt(smt[query_width:, :], cg[slot]).astype(BF)
    big_dp = []

    def big_send(at):
        big_swaps[at]()
        part = dp_rows(big, at * chunk, chunk)
        big_dp.extend(copies.remote(part, part, peer) for peer in place.dp_peers)

    for copy in (ids_core, ids_far):
        copy.wait_recv()
    ids = idr[...].astype(F32)
    first_end = jnp.sum(jnp.where(ids < 0.5, 1.0, 0.0), 1, keepdims=True)
    second_end = jnp.sum(jnp.where(ids < 1.5, 1.0, 0.0), 1, keepdims=True)

    def document(position):
        position = position.astype(F32)
        return jnp.where(position < first_end, 0.0, jnp.where(position < second_end, 1.0, 2.0))

    dk[...] = jnp.zeros_like(dk)
    dv[...] = jnp.zeros_like(dv)
    tiles = length // TILE
    per = tiles // 4

    def tile_at(tile):
        return pl.multiple_of(at_slot(tile // per, rank) * local + (tile % per) * TILE, TILE)

    def masked(scores, key, query):
        edge = key == 0 or query == tiles - 1
        allowed = None
        if key == query:
            down = lax.broadcasted_iota(jnp.int32, (TILE, TILE), 0)
            allowed = down <= lax.broadcasted_iota(jnp.int32, (TILE, TILE), 1)
        if edge:
            down = document(lax.broadcasted_iota(jnp.int32, (TILE, 1), 0) + key * TILE)
            along = document(lax.broadcasted_iota(jnp.int32, (1, TILE), 1) + query * TILE)
            same = down == along
            allowed = same if allowed is None else allowed & same
        return scores if allowed is None else jnp.where(allowed, scores, -1e9)

    def one_head(head, carry):
        own = pl.ds(pl.multiple_of(head * HS, HS), HS)
        for query in range(tiles):
            at_q = pl.ds(tile_at(query), TILE)
            q, do = (qt[own, at_q], dot_rows[own, at_q])
            scaled = do * jnp.asarray(1.0 / math.sqrt(HS), BF)
            highest = jnp.full((1, TILE), -jnp.inf, F32)
            for key in range(query + 1):
                at_k = pl.ds(tile_at(key), TILE)
                at_s = pl.ds(key * TILE, TILE)
                scores = masked(dot(k[at_k, :], q), key, query)
                s_ref[at_s, :] = scores
                highest = jnp.maximum(highest, jnp.max(scores, 0, keepdims=True))
                d_ref[at_s, :] = dot(v[at_k, :], scaled)
            total = jnp.zeros((1, TILE), F32)
            inner = jnp.zeros((1, TILE), F32)
            for key in range(query + 1):
                at_s = pl.ds(key * TILE, TILE)
                exponent = jnp.exp(s_ref[at_s, :] - highest)
                s_ref[at_s, :] = exponent
                total = total + jnp.sum(exponent, 0, keepdims=True)
                inner = inner + jnp.sum(exponent * d_ref[at_s, :], 0, keepdims=True)
            inverse = 1.0 / total
            inner = inner * inverse
            mixed = jnp.zeros((HS, TILE), F32)
            query_grad = jnp.zeros((HS, TILE), F32)
            for key in range(query + 1):
                at_k = pl.ds(tile_at(key), TILE)
                at_s = pl.ds(key * TILE, TILE)
                softmax = s_ref[at_s, :] * inverse
                low = softmax.astype(BF)
                score_grad = (softmax * (d_ref[at_s, :] - inner)).astype(BF)
                mixed = mixed + dot(vt[:, at_k], low)
                query_grad = query_grad + dot(kt[:, at_k], score_grad)
                dk[at_k, :] += dot_nt(score_grad, q)
                dv[at_k, :] += dot_nt(low, do)
            ot[own, at_q] = mixed.astype(BF)
            table = pl.ds(query * TILE, TILE)
            dqt[own, at_q] = rotate(query_grad, cos_ref[:, table], -sin_ref[:, table]).astype(BF)
        return carry

    lax.fori_loop(0, heads, one_head, 0)
    for at in range(len(big_swaps)):
        big_send(at)
    for slot in range(4):
        block = at_slot(slot, rank)
        table = pl.ds(pl.multiple_of(block * local, local), local)
        tokens = pl.ds(slot * local, local)
        key_grad = dk[tokens, :].T * math.sqrt(HS)
        pair_grad[0:HS, tokens] = rotate(key_grad, cos_ref[:, table], -sin_ref[:, table])
        pair_grad[HS:, tokens] = dv[tokens, :].T
    for copy in big_dp:
        copy.wait_recv()
    copies.finish()


def first_pass(dp_size, x, c, small, big, pair, ids, norms, qb, kvb, cosine, sine):
    local = x.shape[0]
    length = 4 * local
    width = small.shape[1]
    query_width = width // 2
    gathers_pair = pair.shape[0] != D
    outs = [
        ((4, local, D), BF),
        ((4, local, D), BF),
        ((4, local, D), BF),
        ((4, local, D), BF),
        ((D, big.shape[1]), BF),
        ((D, width), BF),
        ((dp_size, 4, pair.shape[0], 2 * HS) if gathers_pair else (D, 2 * HS), BF),
        ((query_width, length), BF),
        ((query_width, length), BF),
        ((2 * HS, length), F32),
    ]
    vmem = pl.BlockSpec(memory_space=pltpu.VMEM)
    copies = 40 + 8 * dp_size
    work = query_width * length * length
    return pl.pallas_call(
        functools.partial(first_kernel, dp_size),
        out_shape=[jax.ShapeDtypeStruct(shape, kind) for shape, kind in outs],
        in_specs=[vmem] * 11,
        out_specs=[vmem] * len(outs),
        scratch_shapes=[
            pltpu.VMEM((width, D), BF),
            pltpu.VMEM((2 * HS, D), BF),
            pltpu.VMEM((query_width, length), BF),
            pltpu.VMEM((query_width, length), BF),
            pltpu.VMEM((HS, length), BF),
            pltpu.VMEM((HS, length), BF),
            pltpu.VMEM((length, HS), BF),
            pltpu.VMEM((length, HS), BF),
            pltpu.VMEM((length, HS), F32),
            pltpu.VMEM((length, HS), F32),
            pltpu.VMEM((length, TILE), F32),
            pltpu.VMEM((length, TILE), F32),
            pltpu.VMEM((1, length), jnp.int32),
            pltpu.SemaphoreType.DMA((copies,)),
            pltpu.SemaphoreType.DMA((copies,)),
        ],
        compiler_params=pltpu.CompilerParams(
            collective_id=0, has_side_effects=True, vmem_limit_bytes=52 << 20
        ),
        cost_estimate=pl.CostEstimate(
            flops=40 * work, bytes_accessed=24 << 20, transcendentals=work // HS
        ),
        name="gather_attend",
    )(x, c, small, big, pair, ids, norms, qb, kvb, cosine, sine)

def shards(
    hidden_in,
    doc_ids,
    out_cotangent,
    entry_weight,
    entry_first,
    entry_second,
    entry_anchor,
    entry_velocity,
    exit_weight,
    exit_first,
    exit_second,
    exit_anchor,
    exit_velocity,
    shared_weight,
    shared_first,
    shared_second,
    shared_anchor,
    shared_velocity,
    vector_weight,
    vector_first,
    vector_second,
    vector_anchor,
    vector_velocity,
):
    batch, local_len = hidden_in.shape[:2]
    parts = lax.axis_size("mp")
    group, rank = (lax.axis_index("group"), lax.axis_index("mp"))
    is_swapped = (group % 2) != (rank // 2)
    rank = jnp.where(is_swapped, jnp.bitwise_xor(rank, 2), rank)
    length = local_len * parts
    part_width = entry_weight.shape[2]
    query_width = HEADS * HS // parts
    heads = query_width // HS

    home_vector = vector_weight[0]
    vector = jnp.where(is_swapped, over_core(home_vector), home_vector)
    gain_one, shift_one = (vector[0:D], vector[D : 2 * D])
    gain_two, shift_two = (vector[2 * D : 3 * D], vector[3 * D : 4 * D])
    home_bias = home_vector[4 * D : 5 * D] + home_vector[5 * D : 6 * D]
    pair_bias = vector[6 * D : 6 * D + 2 * HS]
    in_bias = lax.dynamic_slice_in_dim(vector, 6 * D + 2 * HS + rank * part_width, part_width, 0)
    query_bias = in_bias[:query_width]
    up_bias = in_bias[query_width:]

    dp_size = lax.axis_size("dp")
    order = jnp.bitwise_xor(jnp.arange(parts), rank)
    small = jnp.concatenate(
        [entry_weight[0, :, :query_width], exit_weight[0, :query_width].T], 1
    ).astype(BF)
    big = jnp.concatenate(
        [entry_weight[0, :, query_width:], exit_weight[0, query_width:].T], 1
    ).astype(BF)
    pair_piece = shared_weight[0].astype(BF)
    if pair_piece.shape[0] % 16:
        pieces = gather_square(swapped_parts(pair_piece))
        pieces = jnp.take(pieces, order, axis=0)
        pair_piece = gather_dp(pieces.reshape(-1, 2 * HS), 0)
    half = ROT // 2
    frequency = 10000.0 ** (-(np.arange(half) * 2.0 / ROT))
    angles = frequency.astype(np.float32)[:, None] * np.arange(length, dtype=np.float32)[None, :]
    cosine_table = jnp.asarray(np.cos(angles.astype(np.float64)).astype(np.float32))
    sine_table = jnp.asarray(np.sin(angles.astype(np.float64)).astype(np.float32))
    inputs, cots, attn_input, ffn_input, big, small, pair_weight, attended, query_grad, pair_rows = (
        first_pass(
            dp_size,
            hidden_in[0],
            out_cotangent[0],
            small,
            big,
            pair_piece,
            doc_ids,
            vector[: 4 * D].reshape(4, D),
            query_bias[:, None],
            pair_bias[:, None],
            cosine_table,
            sine_table,
        )
    )
    inputs, cots, attn_input, ffn_input = (
        a.reshape(length, D) for a in (inputs, cots, attn_input, ffn_input)
    )
    query_weight, attend_turned = (small[:, :query_width], small[:, query_width:])
    up_weight, down_turned = (big[:, : part_width - query_width], big[:, part_width - query_width :])
    pair_weight = pair_weight.reshape(D, 2 * HS)
    wide = inputs.astype(F32)
    centered = wide - jnp.mean(wide, -1, keepdims=True)
    normal = centered * lax.rsqrt(jnp.mean(centered * centered, -1, keepdims=True) + NORM_EPS)

    hidden_pre = dot(ffn_input, up_weight) + up_bias
    half_root = math.sqrt(0.5)
    below = 0.5 * (1.0 + lax.erf(hidden_pre * half_root))
    hidden = (hidden_pre * below).astype(BF)
    density = jnp.exp(-0.5 * hidden_pre * hidden_pre) * (1.0 / math.sqrt(2.0 * math.pi))
    slope = below + hidden_pre * density

    partial_sum = lax.dot_general(
        attended, attend_turned, (((0,), (1,)), ((), ())), preferred_element_type=F32
    ) + dot_nt(hidden, down_turned)
    branch = scatter_square(partial_sum.reshape(parts, local_len, D), BF)
    block_output = (
        hidden_in[0].astype(F32) + swapped_parts(branch.astype(BF)).astype(F32) + home_bias
    )

    grad_attend = dot(attended, cots)
    grad_down = dot_tn(hidden, cots)
    pre_grad = (dot(cots, down_turned) * slope).astype(BF)
    grad_up = dot_tn(ffn_input, pre_grad)
    ffn_input_grad = dot_nt(pre_grad, up_weight)
    up_bias_grad = jnp.sum(pre_grad.astype(F32), 0)
    pair_partial = pair_rows.T
    grad_query = dot(query_grad, attn_input).T
    attn_input_grad = lax.dot_general(
        query_grad, query_weight, (((0,), (1,)), ((), ())), preferred_element_type=F32
    )
    query_bias_grad = jnp.sum(query_grad.astype(F32), 1)
    joined = attn_input_grad * gain_one + ffn_input_grad * gain_two
    joined_own = scatter_square(joined.reshape(parts, local_len, D), BF)
    pair_low = scatter_square(pair_partial.reshape(parts, local_len, 2 * HS), F32).astype(BF)
    pair_input_grad = dot_nt(pair_low, pair_weight)
    joined_own = joined_own + pair_input_grad * gain_one
    joined_home = swapped_parts(joined_own.astype(BF)).astype(F32)
    home_wide = hidden_in[0].astype(F32)
    home_centered = home_wide - jnp.mean(home_wide, -1, keepdims=True)
    home_scale = lax.rsqrt(jnp.mean(home_centered * home_centered, -1, keepdims=True) + NORM_EPS)
    home_normal = home_centered * home_scale
    input_grad = out_cotangent[0].astype(F32) + home_scale * (
        joined_home
        - jnp.mean(joined_home, -1, keepdims=True)
        - home_normal * jnp.mean(joined_home * home_normal, -1, keepdims=True)
    )

    own_normal = normal[:local_len]
    own_attn = attn_input[:local_len]
    grad_pair = dot_tn(own_attn, pair_low)
    out_bias_grad = jnp.sum(cots[:local_len].astype(F32), 0)
    leading_grads = jnp.concatenate(
        [
            jnp.sum(attn_input_grad * normal, 0) + jnp.sum(pair_input_grad * own_normal, 0),
            jnp.sum(attn_input_grad, 0) + jnp.sum(pair_input_grad, 0),
            jnp.sum(ffn_input_grad * normal, 0),
            jnp.sum(ffn_input_grad, 0),
            out_bias_grad,
            out_bias_grad,
            jnp.sum(pair_low.astype(F32), 0),
        ]
    )
    bias_tail = lax.dynamic_update_slice(
        jnp.zeros((IN_COLS,), F32),
        jnp.concatenate([query_bias_grad, up_bias_grad]),
        (rank * part_width,),
    )
    vector_grad = swapped_parts(
        sum_dp(sum_square(jnp.concatenate([leading_grads, bias_tail])))
    )
    entry_grad = scatter_dp(jnp.concatenate([grad_query, grad_up], 1), 0, BF)
    exit_grad = scatter_dp(jnp.concatenate([grad_attend, grad_down], 0), 1, BF)
    entry_grad = jnp.where(
        is_swapped, swapped_parts(entry_grad.astype(BF)).astype(F32), entry_grad
    )
    exit_grad = jnp.where(is_swapped, swapped_parts(exit_grad.astype(BF)).astype(F32), exit_grad)
    grad_pieces = grad_pair.reshape(lax.axis_size("dp"), parts, -1, 2 * HS)
    grad_pieces = jnp.take(grad_pieces, order, axis=1).swapaxes(0, 1)
    shared_grad = scatter_dp(scatter_square(grad_pieces, F32), 0, F32)
    shared_grad = swapped_parts(shared_grad.reshape(-1, 2 * HS))

    entry_m, entry_v, entry_new = adamw_update(
        entry_weight[0], entry_first[0], entry_second[0], entry_grad, MATRIX_RATE, MATRIX_DECAY
    )
    exit_m, exit_v, exit_new = adamw_update(
        exit_weight[0], exit_first[0], exit_second[0], exit_grad, MATRIX_RATE, MATRIX_DECAY
    )
    shared_m, shared_v, shared_new = adamw_update(
        shared_weight[0], shared_first[0], shared_second[0], shared_grad, MATRIX_RATE, MATRIX_DECAY
    )
    vector_m, vector_v, vector_new = adamw_update(
        home_vector, vector_first[0], vector_second[0], vector_grad, VECTOR_RATE, 0.0
    )
    group_count = lax.axis_size("group")
    vector_gap = vector_anchor - vector_new
    vector_gap = vector_gap + over_core(vector_gap)
    summed = (
        sum_groups(entry_anchor - entry_new, BF),
        sum_groups(exit_anchor - exit_new, BF),
        sum_groups(shared_anchor - shared_new, F32),
        vector_gap + over_half(vector_gap),
    )
    anchors = (entry_anchor, exit_anchor, shared_anchor, vector_anchor)
    velocities = (entry_velocity, exit_velocity, shared_velocity, vector_velocity)
    outer_parts = []
    for position in range(4):
        change = summed[position] / group_count
        momentum = OUTER_BETA * velocities[position] + change
        outer_parts.append(
            (change, momentum, anchors[position] - OUTER_RATE * (change + OUTER_BETA * momentum))
        )
    return (
        (block_output[None], input_grad[None], entry_m[None], entry_v[None], entry_new[None])
        + outer_parts[0]
        + (exit_m[None], exit_v[None], exit_new[None])
        + outer_parts[1]
        + (shared_m[None], shared_v[None], shared_new[None])
        + outer_parts[2]
        + (vector_m[None], vector_v[None], vector_new[None])
        + outer_parts[3]
    )


def solution(mesh):
    in_specs = (
        P(("group", "dp"), "mp", None),
        P(("group", "dp"), "mp"),
        P(("group", "dp"), "mp", None),
        P("group", "dp", "mp"),
        P("group", "dp", "mp"),
        P("group", "dp", "mp"),
        P("dp", "mp"),
        P("dp", "mp"),
        P("group", "mp", "dp"),
        P("group", "mp", "dp"),
        P("group", "mp", "dp"),
        P("mp", "dp"),
        P("mp", "dp"),
        P("group", ("dp", "mp"), None),
        P("group", ("dp", "mp"), None),
        P("group", ("dp", "mp"), None),
        P(("dp", "mp"), None),
        P(("dp", "mp"), None),
        P("group", None),
        P("group", None),
        P("group", None),
        P(),
        P(),
    )
    out_specs = (
        P(("group", "dp"), "mp", None),
        P(("group", "dp"), "mp", None),
        P("group", "dp", "mp"),
        P("group", "dp", "mp"),
        P("group", "dp", "mp"),
        P("dp", "mp"),
        P("dp", "mp"),
        P("dp", "mp"),
        P("group", "mp", "dp"),
        P("group", "mp", "dp"),
        P("group", "mp", "dp"),
        P("mp", "dp"),
        P("mp", "dp"),
        P("mp", "dp"),
        P("group", ("dp", "mp"), None),
        P("group", ("dp", "mp"), None),
        P("group", ("dp", "mp"), None),
        P(("dp", "mp"), None),
        P(("dp", "mp"), None),
        P(("dp", "mp"), None),
        P("group", None),
        P("group", None),
        P("group", None),
        P(),
        P(),
        P(),
    )
    return jax.shard_map(shards, mesh=mesh, in_specs=in_specs, out_specs=out_specs, check_vma=False)
```

time: 439 us -> 408 us (0.929)
  Pallas kernels: 40.1 us -> 161 us
  waiting for transfers between devices: 134 us -> 60.7 us
  other arithmetic: 76.5 us -> 49 us
  starting transfers between devices: 79.2 us -> 52.7 us
  matrix products: 59 us -> 45 us
  local copies, waits for them, and re-layouts: 40.1 us -> 31.1 us
    pallas_call x2 -> x1, Pallas kernels: 40.1 us -> 161 us  [first_pass(): pl.pallas_call(functools.partial(first_kernel, dp_size), out_shape=[jax.S...]
    ppermute x9 -> x5, waiting for transfers between devices: 52.1 us -> 8.56 us  [over_next(): return lax.ppermute(array, 'mp', pairs_of(lax.axis_size('mp'), 1))]
    ppermute x7 -> x4, waiting for transfers between devices: 25.9 us -> 1.33 us  [over_dp(): return lax.ppermute(array, 'dp', pairs_of(2, 1))]
    ppermute x12 -> x6, starting transfers between devices: 46.6 us -> 24.1 us  [swapped_parts(): return lax.ppermute(array, ('group', 'mp'), pairs)]
    convert_element_type x5 -> x1, other arithmetic: 13.5 us -> 0.01 us  [shards(): pair_piece = shared_weight[0].astype(BF)]
    dot_general x4 -> x3, matrix products: 21.3 us -> 15.2 us  [dot_nt(): lax.dot_general(left, right, (((1,), (1,)), ((), ())), preferred_element_...]
    dot_general x4 -> x3, matrix products: 14.5 us -> 8.57 us  [dot_tn(): lax.dot_general(left, right, (((0,), (0,)), ((), ())), preferred_element_...]
    ppermute x12 -> x6, waiting for transfers between devices: 52.8 us -> 47.2 us  [swapped_parts(): return lax.ppermute(array, ('group', 'mp'), pairs)]
  transfers between devices with their start and end apart: 49 -> 32, of which waited for: 15 -> 10; matrix products, arithmetic and copies ran while one was open for 29% -> 22% of each run, Pallas kernels for 0% -> 0%
where the time goes in v2:
time: 408 us; the launch traced here: 401 us
  Pallas kernels  161 us (39%)
  waiting for transfers between devices  60.7 us (15%)
  starting transfers between devices  52.7 us (13%)
  other arithmetic  49 us (12%)
  matrix products  45 us (11%)
  local copies, waits for them, and re-layouts  31.1 us (8%)
    pallas_call x1, Pallas kernels, first_pass(): pl.pallas_call(functools.partial(first_kernel, dp_size), out_shape=[jax.S...  161 us
    ppermute x6, waiting for transfers between devices, swapped_parts(): return lax.ppermute(array, ('group', 'mp'), pairs)  47.2 us
    ppermute x6, starting transfers between devices, swapped_parts(): return lax.ppermute(array, ('group', 'mp'), pairs)  24.1 us
    ppermute x13, starting transfers between devices, over_core(): return lax.ppermute(array, 'group', pairs_of(lax.axis_size('group'), 1))  17.6 us
    dot_general x4, matrix products, dot(): return jnp.dot(left, right, preferred_element_type=F32)  16.2 us
    dot_general x3, matrix products, dot_nt(): lax.dot_general(left, right, (((1,), (1,)), ((), ())), preferred_element_...  15.2 us
    dot_general x3, matrix products, dot_tn(): lax.dot_general(left, right, (((0,), (0,)), ((), ())), preferred_element_...  8.57 us
    ppermute x5, waiting for transfers between devices, over_next(): return lax.ppermute(array, 'mp', pairs_of(lax.axis_size('mp'), 1))  8.56 us
  transfers between devices with their start and end apart: 32, of which 10 were waited for; matrix products, arithmetic and copies ran while one was open for 22% of the time, Pallas kernels for 0%

profile of v2, /device:TPU:1, one launch (start us, length us, event | category | flops | bytes accessed | tf_op | source)
XLA Modules:
  0.0 401.5 jit_solution(11472396859681113831)
XLA Ops:
  1.7 1.3 add_reduce_fusion
  3.0 1.8 copy.64
  11.0 160.6 %gather_attend.1 = (bf16[4,512,768]{2,1,0:T(8,128)(2,1)}, bf16[4,512,768]{2,1,0:T(8,128)(2,1)}, bf16[4,512,768]{2,1,0:T(8,128)(2,1)}, bf16[4,512,768]{2,1,0:T(8,...) custom-call(bf16[512,768]{1,0:T(8,128)(2,1)} %bitcast.207, ...), custom_call_target="tpu_custom_call" | custom-call | flops 32212254720 | bytes 25165824 | tf_op jit(solution)/shard_map/gather_attend/pallas_call | solution.py:482
  171.7 6.8 %multiply_convert_fusion = (bf16[2048,768]{1,0:T(8,128)(2,1)S(1)}, f32[2048,768]{1,0:T(8,128)}) fusion(f32[768]{0:T(1024)S(1)} %slice.142, bf16[2048,768]{1,0:T(8,128)(2,1)} %bitcast.223, bf16[768,1536]{1,0:T(8,128)(2,1)} %get-tuple-element.39), kind=kOutput, calls=%fused_computation.15 | convolution fusion | flops 2425356288 | bytes 13765632 | tf_op jit(solution)/shard_map/dot_general | solution.py:36
  178.5 2.6 fusion.39
  181.2 4.1 %fusion.84 = f32[768,768]{1,0:T(8,128)} fusion(bf16[2048,768]{1,0:T(8,128)(2,1)S(1)} %get-tuple-element.107, bf16[2048,768]{1,0:T(8,128)(2,1)S(1)} %bitcast.210), kind=kOutput, calls=%fused_computation.201 | convolution fusion | flops 2415919104 | bytes 8650752 | tf_op jit(solution)/shard_map/dot_general | solution.py:44
  187.4 1.3 slice.256
  188.7 1.9 slice.181
  191.7 2.5 convert_reduce_fusion.1
  199.4 7.8 %convert_reduce_fusion = (f32[768]{0:T(1024)}, bf16[2048,768]{1,0:T(8,128)(2,1)S(1)}) fusion(f32[2048,768]{1,0:T(8,128)} %get-tuple-element.108, f32[768]{0:T(1024)S(1)} %slice.142, bf16[2048,768]{1,0:T(8,128)(2,1)} %bitcast.209, bf16[768,1536]{1,0:T(8,128)(2,1)} %get-tuple-element.39), kind=kOutput, calls=%fused_computation.10 | convolution fusion | flops 2436365568 | bytes 13768704 | tf_op jit(solution)/shard_map/dot_general | solution.py:36
  207.3 4.1 %fusion.82 = f32[768,768]{0,1:T(8,128)} fusion(bf16[2048,768]{1,0:T(8,128)(2,1)S(1)} %bitcast.224, bf16[2048,768]{1,0:T(8,128)(2,1)S(1)} %get-tuple-element.110), kind=kOutput, calls=%fused_computation.199 | convolution fusion | flops 2415919104 | bytes 8650752 | tf_op jit(solution)/shard_map/dot_general | solution.py:44
  213.9 3.7 fusion.47
  218.8 2.6 collective-permute-start.7
  222.2 5.2 %collective-permute-done.7 = f32[512,128]{1,0:T(8,128)S(1)} collective-permute-done((f32[512,128]{1,0:T(8,128)S(1)}, f32[512,128]{1,0:T(8,128)S(1)}, u32[]{:S(2)}, u32[]{:S(2)}) %collective-permute-start.7) | collective-permute-done | bytes 262176 | tf_op jit(solution)/shard_map/ppermute | solution.py:69
  229.2 1.3 collective-permute-start.19
  231.6 1.5 collective-permute-start.20
  233.3 2.4 collective-permute-done.20
  237.4 1.3 collective-permute-done.21
  238.8 8.1 %collective-permute-start.22 = (f32[96,128]{1,0:T(8,128)S(1)}, f32[96,128]{1,0:T(8,128)S(1)}, u32[]{:S(2)}, u32[]{:S(2)}) collective-permute-start(f32[96,128]{1,0:T(8,128)S(1)} %add_bitcast_fusion), channel_id=1, source_target_pairs={{0,0},{1,1},{2,8},{3,9},{8,2},{9,3},{10,10},{11,11},{16,16},{17,17... | collective-permute-start | bytes 147464 | tf_op jit(solution)/shard_map/ppermute | solution.py:84
  246.9 9.0 %fusion.67 = (f32[768]{0:T(1024)}, f32[768]{0:T(1024)}, f32[2048,768]{1,0:T(8,128)S(1)}, f32[768]{0:T(1024)}, f32[768]{0:T(1024)}, /*index=5*/f32[2048,768]{1,0:T(8,128)}) fusion(f32[2048]{0:T(1024)S(1)} %bitcast.221, f32[2048]{0:T(1024)S(1)} %bitcast.220, bf16[4,512,768]{2,1,0:T(8,128)(2,1)S(1)} %copy-done.4, f32[768]{0:T(1024)S(1)} %get-tuple-element.104, ...), kind=kOutput, calls=%fused_computation.188 | convolution fusion | flops 2434790400 | bytes 26380288 | tf_op jit(solution)/shard_map/dot_general | solution.py:40
  257.9 3.2 collective-permute-done.23
  262.3 2.7 fusion.75
  265.0 2.2 collective-permute-start.15
  267.3 5.5 %collective-permute-start.25 = (f32[48,128]{1,0:T(8,128)S(1)}, f32[48,128]{1,0:T(8,128)S(1)}, u32[]{:S(2)}, u32[]{:S(2)}) collective-permute-start(f32[48,128]{1,0:T(8,128)S(1)} %add.354), channel_id=1, source_target_pairs={{0,8},{8,0},{16,24},{24,16},{1,9},{9,1},{17,25},{25,17},{2,10},{10... | collective-permute-start | bytes 73736 | tf_op jit(solution)/shard_map/ppermute | solution.py:61
  273.0 2.2 collective-permute-start.10
  277.2 25.2 %collective-permute-done.10 = bf16[384,960]{0,1:T(8,128)(2,1)S(1)} collective-permute-done((bf16[384,960]{0,1:T(8,128)(2,1)S(1)}, bf16[384,960]{0,1:T(8,128)(2,1)S(1)}, u32[]{:S(2)}, u32[]{:S(2)}) %collective-permute-start.10) | collective-permute-done | bytes 737312 | tf_op jit(solution)/shard_map/ppermute | solution.py:84
  302.5 3.0 fusion.77
  307.8 2.4 copy.70
  310.2 5.8 %fusion.74 = (f32[960,384]{1,0:T(8,128)S(1)}, f32[960,384]{1,0:T(8,128)}, f32[1,960,384]{2,1,0:T(8,128)}, f32[1,960,384]{2,1,0:T(8,128)}) fusion(f32[960,384]{1,0:T(8,128)} %param.36, f32[1,960,384]{2,1,0:T(8,128)} %param.35, f32[960,384]{1,0:T(8,128)} %get-tuple-element.74, bf16[960,384]{1,0:T(8,128)(2,1)} %collective-permute-done.15, pred[]{:T(512)S(6)} %ne.26, ...), kind=kLoop, calls=%fused_computation.193 | loop fusion | flops 6635520 | bytes 14008321 | tf_op jit(solution)/shard_map/sub | solution.py:696
  316.2 3.6 fusion.69
  322.0 1.8 convert_add_fusion.1
  327.5 2.4 copy.71
  330.0 3.8 collective-permute-start.29
  333.8 1.8 add_convert_fusion
  335.9 8.3 %collective-permute-done.29 = f32[8576]{0:T(1024)S(1)} collective-permute-done((f32[8576]{0:T(1024)S(1)}, f32[8576]{0:T(1024)S(1)}, u32[]{:S(2)}, u32[]{:S(2)}) %collective-permute-start.29) | collective-permute-done | bytes 34336 | tf_op jit(solution)/shard_map/ppermute | solution.py:84
  345.9 5.6 %collective-permute-start.8 = (bf16[512,768]{1,0:T(8,128)(2,1)}, bf16[512,768]{1,0:T(8,128)(2,1)}, u32[]{:S(2)}, u32[]{:S(2)}) collective-permute-start(bf16[512,768]{1,0:T(8,128)(2,1)} %get-tuple-element.92), channel_id=1, source_target_pairs={{0,0},{1,1},{2,8},{3,9},{8,2},{9,3},{10,10},{11,11},{16,16},{17,17... | collective-permute-start | bytes 2359304 | tf_op jit(solution)/shard_map/ppermute | solution.py:84
  352.8 2.2 fusion.23
  355.0 2.2 collective-permute-start.3
  361.1 8.1 %collective-permute-start.13 = (f32[192,960]{1,0:T(8,128)S(1)}, f32[192,960]{1,0:T(8,128)}, u32[]{:S(2)}, u32[]{:S(2)}) collective-permute-start(f32[192,960]{1,0:T(8,128)S(1)} %copy.72), channel_id=1, source_target_pairs={{0,8},{8,0},{16,24},{24,16},{1,9},{9,1},{17,25},{25,17},{2,10},{10... | collective-permute-start | bytes 2211848 | tf_op jit(solution)/shard_map/ppermute | solution.py:61
  369.2 1.9 convert_add_fusion.4
  371.2 7.1 %collective-permute-done.8 = bf16[512,768]{1,0:T(8,128)(2,1)} collective-permute-done((bf16[512,768]{1,0:T(8,128)(2,1)}, bf16[512,768]{1,0:T(8,128)(2,1)}, u32[]{:S(2)}, u32[]{:S(2)}) %collective-permute-start.8) | collective-permute-done | bytes 786464 | tf_op jit(solution)/shard_map/ppermute | solution.py:84
  378.4 1.9 convert_reduce_fusion.2
  380.2 6.5 %collective-permute-done.3 = bf16[512,768]{1,0:T(8,128)(2,1)} collective-permute-done((bf16[512,768]{1,0:T(8,128)(2,1)}, bf16[512,768]{1,0:T(8,128)(2,1)}, u32[]{:S(2)}, u32[]{:S(2)}) %collective-permute-start.3) | collective-permute-done | bytes 786464 | tf_op jit(solution)/shard_map/ppermute | solution.py:84
  386.8 3.7 fusion.13
  390.5 1.5 copy.73
  393.9 2.6 multiply_subtract_fusion.1
  396.5 1.5 broadcast_select_fusion.3
  398.6 2.4 multiply_subtract_fusion
  (274 shorter events, 47.7 us)
Async XLA Ops:
  1.5 8.8 %collective-permute-start = (f32[8576]{0:T(1024)S(1)}, f32[8576]{0:T(1024)S(1)}, u32[]{:S(2)}, u32[]{:S(2)}) collective-permute-start(f32[8576]{0:T(1024)S(1)} %reduce.3), channel_id=1, source_target_pairs={{0,8},{8,0},{16,24},{24,16},{1,9},{9,1},{17,25},{25,17},{2,10},{10... | collective-permute-start | bytes 102920 | tf_op jit(solution)/shard_map/ppermute | solution.py:61
  197.2 20.4 %collective-permute-start.6 = (f32[2,512,128]{2,1,0:T(8,128)}, f32[2,512,128]{2,1,0:T(8,128)}, u32[]{:S(2)}, u32[]{:S(2)}) collective-permute-start(f32[2,512,128]{2,1,0:T(8,128)} %bitcast.24), channel_id=1, source_target_pairs={{0,8},{8,0},{16,24},{24,16},{1,9},{9,1},{17,25},{25,17},{2,10},{10... | collective-permute-start | bytes 1572872 | tf_op jit(solution)/shard_map/ppermute | solution.py:61
  212.3 50.0 %collective-permute-start.14 = (bf16[960,384]{1,0:T(8,128)(2,1)}, bf16[960,384]{1,0:T(8,128)(2,1)}, u32[]{:S(2)}, u32[]{:S(2)}) collective-permute-start(bf16[960,384]{1,0:T(8,128)(2,1)} %fusion.27), channel_id=1, source_target_pairs={{0,4},{4,0},{1,5},{5,1},{2,6},{6,2},{3,7},{7,3},{8,12},{12,8},{9,1... | collective-permute-start | bytes 2211848 | tf_op jit(solution)/shard_map/ppermute | solution.py:73
  218.8 8.6 %collective-permute-start.7 = (f32[512,128]{1,0:T(8,128)S(1)}, f32[512,128]{1,0:T(8,128)S(1)}, u32[]{:S(2)}, u32[]{:S(2)}) collective-permute-start(f32[512,128]{1,0:T(8,128)S(1)} %slice_bitcast_fusion.5), channel_id=1, source_target_pairs={{0,1},{1,0},{2,3},{3,2},{4,5},{5,4},{6,7},{7,6},{8,9},{9,8},{10,11... | collective-permute-start | bytes 786440 | tf_op jit(solution)/shard_map/ppermute | solution.py:69
  229.2 2.4 collective-permute-start.19
  231.2 15.7 %copy-start.55 = (f32[768]{0:T(1024)}, f32[768]{0:T(1024)S(1)}, u32[]{:S(2)}) copy-start(f32[768]{0:T(1024)S(1)} %get-tuple-element.103) | copy-start | bytes 9220
  231.6 4.1 %collective-permute-start.20 = (f32[2,96,128]{2,1,0:T(8,128)S(1)}, f32[2,96,128]{2,1,0:T(8,128)S(1)}, u32[]{:S(2)}, u32[]{:S(2)}) collective-permute-start(f32[2,96,128]{2,1,0:T(8,128)S(1)} %slice_bitcast_fusion.9), channel_id=1, source_target_pairs={{0,1},{1,0},{2,3},{3,2},{4,5},{5,4},{6,7},{7,6},{8,9},{9,8},{10,11... | collective-permute-start | bytes 294920 | tf_op jit(solution)/shard_map/ppermute | solution.py:69
  235.7 3.0 collective-permute-start.21
  237.1 35.8 %collective-permute-start.9 = (bf16[384,960]{0,1:T(8,128)(2,1)S(1)}, bf16[384,960]{0,1:T(8,128)(2,1)S(1)}, u32[]{:S(2)}, u32[]{:S(2)}) collective-permute-start(bf16[384,960]{0,1:T(8,128)(2,1)S(1)} %fusion.31), channel_id=1, source_target_pairs={{0,4},{4,0},{1,5},{5,1},{2,6},{6,2},{3,7},{7,3},{8,12},{12,8},{9,1... | collective-permute-start | bytes 2211848 | tf_op jit(solution)/shard_map/ppermute | solution.py:73
  238.8 17.9 %collective-permute-start.22 = (f32[96,128]{1,0:T(8,128)S(1)}, f32[96,128]{1,0:T(8,128)S(1)}, u32[]{:S(2)}, u32[]{:S(2)}) collective-permute-start(f32[96,128]{1,0:T(8,128)S(1)} %add_bitcast_fusion), channel_id=1, source_target_pairs={{0,0},{1,1},{2,8},{3,9},{8,2},{9,3},{10,10},{11,11},{16,16},{17,17... | collective-permute-start | bytes 147464 | tf_op jit(solution)/shard_map/ppermute | solution.py:84
  256.1 19.8 %collective-permute-start.4 = (bf16[2,512,768]{2,1,0:T(8,128)(2,1)S(1)}, bf16[2,512,768]{2,1,0:T(8,128)(2,1)S(1)}, u32[]{:S(2)}, u32[]{:S(2)}) collective-permute-start(bf16[2,512,768]{2,1,0:T(8,128)(2,1)S(1)} %bitcast.214), channel_id=1, source_target_pairs={{0,8},{8,0},{16,24},{24,16},{1,9},{9,1},{17,25},{25,17},{2,10},{10... | collective-permute-start | bytes 4718600 | tf_op jit(solution)/shard_map/ppermute | solution.py:61
  256.2 65.8 %collective-permute-start.1 = (bf16[2,512,768]{2,1,0:T(8,128)(2,1)}, bf16[2,512,768]{2,1,0:T(8,128)(2,1)}, u32[]{:S(2)}, u32[]{:S(2)}) collective-permute-start(bf16[2,512,768]{2,1,0:T(8,128)(2,1)} %bitcast.13), channel_id=1, source_target_pairs={{0,8},{8,0},{16,24},{24,16},{1,9},{9,1},{17,25},{25,17},{2,10},{10... | collective-permute-start | bytes 4718600 | tf_op jit(solution)/shard_map/ppermute | solution.py:61
  257.5 3.6 collective-permute-start.23
  261.1 6.1 %collective-permute-start.24 = (f32[48,128]{1,0:T(8,128)S(1)}, f32[48,128]{1,0:T(8,128)S(1)}, u32[]{:S(2)}, u32[]{:S(2)}) collective-permute-start(f32[48,128]{1,0:T(8,128)S(1)} %dynamic-slice_add_fusion), channel_id=1, source_target_pairs={{0,16},{8,24},{16,0},{24,8},{1,17},{9,25},{17,1},{25,9},{2,18},{10... | collective-permute-start | bytes 73736 | tf_op jit(solution)/shard_map/ppermute | solution.py:65
  265.0 45.2 %collective-permute-start.15 = (bf16[960,384]{1,0:T(8,128)(2,1)}, bf16[960,384]{1,0:T(8,128)(2,1)}, u32[]{:S(2)}, u32[]{:S(2)}) collective-permute-start(bf16[960,384]{1,0:T(8,128)(2,1)} %get-tuple-element.73), channel_id=1, source_target_pairs={{0,0},{1,1},{2,8},{3,9},{8,2},{9,3},{10,10},{11,11},{16,16},{17,17... | collective-permute-start | bytes 2211848 | tf_op jit(solution)/shard_map/ppermute | solution.py:84
  267.3 7.9 %collective-permute-start.25 = (f32[48,128]{1,0:T(8,128)S(1)}, f32[48,128]{1,0:T(8,128)S(1)}, u32[]{:S(2)}, u32[]{:S(2)}) collective-permute-start(f32[48,128]{1,0:T(8,128)S(1)} %add.354), channel_id=1, source_target_pairs={{0,8},{8,0},{16,24},{24,16},{1,9},{9,1},{17,25},{25,17},{2,10},{10... | collective-permute-start | bytes 73736 | tf_op jit(solution)/shard_map/ppermute | solution.py:61
  273.0 29.4 %collective-permute-start.10 = (bf16[384,960]{0,1:T(8,128)(2,1)S(1)}, bf16[384,960]{0,1:T(8,128)(2,1)S(1)}, u32[]{:S(2)}, u32[]{:S(2)}) collective-permute-start(bf16[384,960]{0,1:T(8,128)(2,1)S(1)} %get-tuple-element.80), channel_id=1, source_target_pairs={{0,0},{1,1},{2,8},{3,9},{8,2},{9,3},{10,10},{11,11},{16,16},{17,17... | collective-permute-start | bytes 2211848 | tf_op jit(solution)/shard_map/ppermute | solution.py:84
  275.9 26.5 %copy-start.15 = (f32[1,384,960]{1,2,0:T(8,128)S(1)}, f32[1,384,960]{1,2,0:T(8,128)}, u32[]{:S(2)}) copy-start(f32[1,384,960]{1,2,0:T(8,128)} %param.28) | copy-start | bytes 4423684
  275.9 26.5 %copy-start.30 = (f32[1,384,960]{1,2,0:T(8,128)S(1)}, f32[1,384,960]{1,2,0:T(8,128)}, u32[]{:S(2)}) copy-start(f32[1,384,960]{1,2,0:T(8,128)} %param.30) | copy-start | bytes 4423684
  275.9 26.5 %copy-start.31 = (f32[1,384,960]{1,2,0:T(8,128)S(1)}, f32[1,384,960]{1,2,0:T(8,128)}, u32[]{:S(2)}) copy-start(f32[1,384,960]{1,2,0:T(8,128)} %param.29) | copy-start | bytes 4423684
  276.2 26.2 %copy-start.13 = (f32[384,960]{0,1:T(8,128)S(1)}, f32[384,960]{0,1:T(8,128)}, u32[]{:S(2)}) copy-start(f32[384,960]{0,1:T(8,128)} %param.31) | copy-start | bytes 4423684
  277.2 38.9 %collective-permute-start.5 = (bf16[512,768]{1,0:T(8,128)(2,1)}, bf16[512,768]{1,0:T(8,128)(2,1)}, u32[]{:S(2)}, u32[]{:S(2)}) collective-permute-start(bf16[512,768]{1,0:T(8,128)(2,1)} %fusion.46), channel_id=1, source_target_pairs={{0,1},{1,0},{2,3},{3,2},{4,5},{5,4},{6,7},{7,6},{8,9},{9,8},{10,11... | collective-permute-start | bytes 2359304 | tf_op jit(solution)/shard_map/ppermute | solution.py:69
  310.2 17.3 %collective-permute-start.11 = (f32[192,960]{1,0:T(8,128)}, f32[192,960]{1,0:T(8,128)}, u32[]{:S(2)}, u32[]{:S(2)}) collective-permute-start(f32[192,960]{1,0:T(8,128)} %copy.70), channel_id=1, source_target_pairs={{0,8},{8,0},{16,24},{24,16},{1,9},{9,1},{17,25},{25,17},{2,10},{10... | collective-permute-start | bytes 2211848 | tf_op jit(solution)/shard_map/ppermute | solution.py:61
  319.9 1.9 collective-permute-start.26
  321.8 22.6 %collective-permute-start.16 = (f32[480,384]{1,0:T(8,128)}, f32[480,384]{1,0:T(8,128)}, u32[]{:S(2)}, u32[]{:S(2)}) collective-permute-start(f32[480,384]{1,0:T(8,128)} %constant_dynamic-slice_fusion.2), channel_id=1, source_target_pairs={{0,8},{8,0},{16,24},{24,16},{1,9},{9,1},{17,25},{25,17},{2,10},{10... | collective-permute-start | bytes 2211848 | tf_op jit(solution)/shard_map/ppermute | solution.py:61
  321.9 2.9 collective-permute-start.27
  324.7 5.2 %collective-permute-start.28 = (f32[8576]{0:T(1024)S(1)}, f32[8576]{0:T(1024)S(1)}, u32[]{:S(2)}, u32[]{:S(2)}) collective-permute-start(f32[8576]{0:T(1024)S(1)} %add.363), channel_id=1, source_target_pairs={{0,4},{4,0},{1,5},{5,1},{2,6},{6,2},{3,7},{7,3},{8,12},{12,8},{9,1... | collective-permute-start | bytes 102920 | tf_op jit(solution)/shard_map/ppermute | solution.py:73
  327.0 25.9 %collective-permute-start.2 = (bf16[512,768]{1,0:T(8,128)(2,1)}, bf16[512,768]{1,0:T(8,128)(2,1)}, u32[]{:S(2)}, u32[]{:S(2)}) collective-permute-start(bf16[512,768]{1,0:T(8,128)(2,1)} %fusion.45), channel_id=1, source_target_pairs={{0,1},{1,0},{2,3},{3,2},{4,5},{5,4},{6,7},{7,6},{8,9},{9,8},{10,11... | collective-permute-start | bytes 2359304 | tf_op jit(solution)/shard_map/ppermute | solution.py:69
  329.9 14.3 %copy-start.36 = (f32[8576]{0:T(1024)S(1)}, f32[8576]{0:T(1024)}, u32[]{:S(2)}) copy-start(f32[8576]{0:T(1024)} %copy-done.35) | copy-start | bytes 102916
  329.9 14.3 %copy-start.40 = (f32[8576]{0:T(1024)S(1)}, f32[8576]{0:T(1024)}, u32[]{:S(2)}) copy-start(f32[8576]{0:T(1024)} %param.46) | copy-start | bytes 102916
  329.9 14.3 %copy-start.41 = (f32[8576]{0:T(1024)S(1)}, f32[8576]{0:T(1024)}, u32[]{:S(2)}) copy-start(f32[8576]{0:T(1024)} %get-tuple-element.113) | copy-start | bytes 102916
  329.9 14.3 %copy-start.42 = (f32[8576]{0:T(1024)S(1)}, f32[8576]{0:T(1024)}, u32[]{:S(2)}) copy-start(f32[8576]{0:T(1024)} %get-tuple-element.114) | copy-start | bytes 102916
  329.9 14.5 %copy-start.19 = (f32[960,384]{1,0:T(8,128)S(1)}, f32[960,384]{1,0:T(8,128)}, u32[]{:S(2)}) copy-start(f32[960,384]{1,0:T(8,128)} %copy-done.18) | copy-start | bytes 4423684
  330.0 14.3 %collective-permute-start.29 = (f32[8576]{0:T(1024)S(1)}, f32[8576]{0:T(1024)S(1)}, u32[]{:S(2)}, u32[]{:S(2)}) collective-permute-start(f32[8576]{0:T(1024)S(1)} %add.364), channel_id=1, source_target_pairs={{0,0},{1,1},{2,8},{3,9},{8,2},{9,3},{10,10},{11,11},{16,16},{17,17... | collective-permute-start | bytes 102920 | tf_op jit(solution)/shard_map/ppermute | solution.py:84
  335.6 24.2 %copy-start.22 = (bf16[192,960]{0,1:T(8,128)(2,1)}, bf16[192,960]{0,1:T(8,128)(2,1)S(1)}, u32[]{:S(2)}) copy-start(bf16[192,960]{0,1:T(8,128)(2,1)S(1)} %add_convert_fusion) | copy-start | bytes 1105924
  335.6 24.2 %collective-permute-start.12 = (bf16[192,960]{0,1:T(8,128)(2,1)S(1)}, bf16[192,960]{0,1:T(8,128)(2,1)S(1)}, u32[]{:S(2)}, u32[]{:S(2)}) collective-permute-start(bf16[192,960]{0,1:T(8,128)(2,1)S(1)} %add_convert_fusion), channel_id=1, source_target_pairs={{0,16},{8,24},{16,0},{24,8},{1,17},{9,25},{17,1},{25,9},{2,18},{10... | collective-permute-start | bytes 1105928 | tf_op jit(solution)/shard_map/ppermute | solution.py:65
  344.3 7.2 %collective-permute-start.30 = (f32[8576]{0:T(1024)S(1)}, f32[8576]{0:T(1024)S(1)}, u32[]{:S(2)}, u32[]{:S(2)}) collective-permute-start(f32[8576]{0:T(1024)S(1)} %get-tuple-element.57), channel_id=1, source_target_pairs={{0,8},{8,0},{16,24},{24,16},{1,9},{9,1},{17,25},{25,17},{2,10},{10... | collective-permute-start | bytes 102920 | tf_op jit(solution)/shard_map/ppermute | solution.py:61
  345.6 23.6 %collective-permute-start.17 = (bf16[480,384]{1,0:T(8,128)(2,1)S(1)}, bf16[480,384]{1,0:T(8,128)(2,1)}, u32[]{:S(2)}, u32[]{:S(2)}) collective-permute-start(bf16[480,384]{1,0:T(8,128)(2,1)S(1)} %add_convert_fusion.1), channel_id=1, source_target_pairs={{0,16},{8,24},{16,0},{24,8},{1,17},{9,25},{17,1},{25,9},{2,18},{10... | collective-permute-start | bytes 1105928 | tf_op jit(solution)/shard_map/ppermute | solution.py:65
  345.9 32.4 %collective-permute-start.8 = (bf16[512,768]{1,0:T(8,128)(2,1)}, bf16[512,768]{1,0:T(8,128)(2,1)}, u32[]{:S(2)}, u32[]{:S(2)}) collective-permute-start(bf16[512,768]{1,0:T(8,128)(2,1)} %get-tuple-element.92), channel_id=1, source_target_pairs={{0,0},{1,1},{2,8},{3,9},{8,2},{9,3},{10,10},{11,11},{16,16},{17,17... | collective-permute-start | bytes 2359304 | tf_op jit(solution)/shard_map/ppermute | solution.py:84
  351.6 7.6 %collective-permute-start.31 = (f32[8576]{0:T(1024)S(1)}, f32[8576]{0:T(1024)S(1)}, u32[]{:S(2)}, u32[]{:S(2)}) collective-permute-start(f32[8576]{0:T(1024)S(1)} %add.370), channel_id=1, source_target_pairs={{0,16},{8,24},{16,0},{24,8},{1,17},{9,25},{17,1},{25,9},{2,18},{10... | collective-permute-start | bytes 102920 | tf_op jit(solution)/shard_map/ppermute | solution.py:65
  355.0 31.8 %collective-permute-start.3 = (bf16[512,768]{1,0:T(8,128)(2,1)}, bf16[512,768]{1,0:T(8,128)(2,1)}, u32[]{:S(2)}, u32[]{:S(2)}) collective-permute-start(bf16[512,768]{1,0:T(8,128)(2,1)} %fusion.23), channel_id=1, source_target_pairs={{0,0},{1,1},{2,8},{3,9},{8,2},{9,3},{10,10},{11,11},{16,16},{17,17... | collective-permute-start | bytes 2359304 | tf_op jit(solution)/shard_map/ppermute | solution.py:84
  360.7 17.7 %copy-start.7 = (bf16[1,512,768]{2,1,0:T(8,128)(2,1)S(1)}, bf16[1,512,768]{2,1,0:T(8,128)(2,1)}, u32[]{:S(2)}) copy-start(bf16[1,512,768]{2,1,0:T(8,128)(2,1)} %param.25) | copy-start | bytes 2359300
  360.7 17.7 %copy-start.52 = (f32[512]{0:T(512)S(1)}, f32[512]{0:T(512)}, u32[]{:S(2)}) copy-start(f32[512]{0:T(512)} %copy-done.51) | copy-start | bytes 6148
  360.7 17.7 %copy-start.53 = (f32[512]{0:T(512)S(1)}, f32[512]{0:T(512)}, u32[]{:S(2)}) copy-start(f32[512]{0:T(512)} %add_rsqrt_fusion) | copy-start | bytes 6148
  361.0 25.7 %copy-start.34 = (bf16[1,512,768]{2,1,0:T(8,128)(2,1)S(1)}, bf16[1,512,768]{2,1,0:T(8,128)(2,1)}, u32[]{:S(2)}) copy-start(bf16[1,512,768]{2,1,0:T(8,128)(2,1)} %param.27) | copy-start | bytes 2359300
  361.0 25.7 %copy-start.54 = (f32[768]{0:T(1024)S(1)}, f32[768]{0:T(1024)}, u32[]{:S(2)}) copy-start(f32[768]{0:T(1024)} %add_reduce_fusion) | copy-start | bytes 9220
  361.1 29.4 %collective-permute-start.13 = (f32[192,960]{1,0:T(8,128)S(1)}, f32[192,960]{1,0:T(8,128)}, u32[]{:S(2)}, u32[]{:S(2)}) collective-permute-start(f32[192,960]{1,0:T(8,128)S(1)} %copy.72), channel_id=1, source_target_pairs={{0,8},{8,0},{16,24},{24,16},{1,9},{9,1},{17,25},{25,17},{2,10},{10... | collective-permute-start | bytes 2211848 | tf_op jit(solution)/shard_map/ppermute | solution.py:61
  371.1 25.4 %collective-permute-start.18 = (f32[480,384]{1,0:T(8,128)}, f32[480,384]{1,0:T(8,128)}, u32[]{:S(2)}, u32[]{:S(2)}) collective-permute-start(f32[480,384]{1,0:T(8,128)} %convert_add_fusion.4), channel_id=1, source_target_pairs={{0,8},{8,0},{16,24},{24,16},{1,9},{9,1},{17,25},{25,17},{2,10},{10... | collective-permute-start | bytes 2211848 | tf_op jit(solution)/shard_map/ppermute | solution.py:61
  (51 other events, 185.5 us)

commit v3 on v2

v3 whole, which is shorter than its diff:
```python
import functools
import math

import jax
import jax.numpy as jnp
import numpy as np
from jax import lax
from jax.experimental import pallas as pl
from jax.experimental.pallas import tpu as pltpu
from jax.sharding import PartitionSpec as P

D = 768
HEADS = 12
HS = 64
ROT = 16
STEP = 5
IN_COLS = 3840


NORM_EPS = 1e-05
BETA_ONE = 0.9
BETA_TWO = 0.95
ADAM_EPS = 1e-08
MATRIX_RATE = 0.03
MATRIX_DECAY = 0.1
VECTOR_RATE = 0.3
OUTER_RATE = 0.7
OUTER_BETA = 0.9

TILE = 256
F32 = jnp.float32
BF = jnp.bfloat16


def dot(left, right):
    return jnp.dot(left, right, preferred_element_type=F32)


def dot_nt(left, right):
    return lax.dot_general(left, right, (((1,), (1,)), ((), ())), preferred_element_type=F32)


def dot_tn(left, right):
    return lax.dot_general(left, right, (((0,), (0,)), ((), ())), preferred_element_type=F32)


def adamw_update(weight, first, second, gradient, step_rate, decay):
    first_new = BETA_ONE * first + (1.0 - BETA_ONE) * gradient
    second_new = BETA_TWO * second + (1.0 - BETA_TWO) * gradient * gradient
    fix_first = 1.0 - BETA_ONE**STEP
    fix_second = 1.0 - BETA_TWO**STEP
    update = first_new / fix_first / (jnp.sqrt(second_new / fix_second) + ADAM_EPS)
    return (first_new, second_new, weight - step_rate * (update + decay * weight))


def pairs_of(size, bit):
    return [(at, at ^ bit) for at in range(size)]


def over_core(array):
    return lax.ppermute(array, "group", pairs_of(lax.axis_size("group"), 1))


def over_half(array):
    return lax.ppermute(array, "group", pairs_of(lax.axis_size("group"), 2))


def over_next(array):
    return lax.ppermute(array, "mp", pairs_of(lax.axis_size("mp"), 1))


def over_dp(array):
    return lax.ppermute(array, "dp", pairs_of(2, 1))


def swapped_parts(array):
    parts = lax.axis_size("mp")
    pairs = []
    for group in range(lax.axis_size("group")):
        for rank in range(parts):
            here = group * parts + rank
            there = (group ^ 1) * parts + (rank ^ 2)
            pairs.append((here, there if group % 2 != rank // 2 else here))
    return lax.ppermute(array, ("group", "mp"), pairs)


def gather_square(own):
    pair = jnp.stack([own, over_next(own)])
    return jnp.concatenate([pair, over_core(pair)], 0)


def scatter_square(slots, send_type):
    pair = slots[:2] + over_core(slots[2:].astype(send_type)).astype(F32)
    return pair[0] + over_next(pair[1].astype(send_type)).astype(F32)


def sum_square(array):
    array = array + over_core(array)
    return array + over_next(array)


def gather_dp(own, axis):
    if lax.axis_size("dp") == 2:
        other = over_dp(own)
        first = lax.axis_index("dp") == 0
        return jnp.concatenate(
            [jnp.where(first, own, other), jnp.where(first, other, own)], axis
        )
    return lax.all_gather(own, "dp", axis=axis, tiled=True)


def scatter_dp(array, axis, send_type):
    if lax.axis_size("dp") == 2:
        size = array.shape[axis] // 2
        mine = lax.axis_index("dp")
        kept = lax.dynamic_slice_in_dim(array, mine * size, size, axis)
        sent = lax.dynamic_slice_in_dim(array, (1 - mine) * size, size, axis)
        return kept + over_dp(sent.astype(send_type)).astype(F32)
    return lax.psum_scatter(array, "dp", scatter_dimension=axis, tiled=True)


def sum_dp(array):
    if lax.axis_size("dp") == 2:
        return array + over_dp(array)
    return lax.psum(array, "dp")


def sum_groups(array, send_type):
    size = array.shape[0] // 2
    core = lax.axis_index("group") % 2
    kept = lax.dynamic_slice_in_dim(array, core * size, size, 0)
    sent = lax.dynamic_slice_in_dim(array, (1 - core) * size, size, 0)
    part = (kept + over_core(sent)).astype(send_type)
    part = part.astype(F32) + over_half(part).astype(F32)
    other = over_core(part)
    low = core == 0
    return jnp.concatenate([jnp.where(low, part, other), jnp.where(low, other, part)], 0)


def flip_one(index):
    return index + 1 - 2 * (index % 2)


def flip_two(index):
    return index + 2 - 4 * ((index // 2) % 2)


def at_slot(slot, rank):
    rank = flip_one(rank) if slot % 2 else rank
    return flip_two(rank) if slot // 2 else rank


class Copies:
    def __init__(self, send, receive):
        self.send, self.receive, self.used, self.sends = (send, receive, 0, [])

    def remote(self, source, target, device, starts=True):
        at = self.used
        self.used += 1
        copy = pltpu.make_async_remote_copy(
            src_ref=source,
            dst_ref=target,
            send_sem=self.send.at[at],
            recv_sem=self.receive.at[at],
            device_id=device,
            device_id_type=pl.DeviceIdType.MESH,
        )
        if starts:
            copy.start()
        self.sends.append(copy)
        return copy

    def swapped(self, source, target, is_swapped, device):
        at = self.used
        self.used += 1
        far = pltpu.make_async_remote_copy(
            src_ref=source,
            dst_ref=target,
            send_sem=self.send.at[at],
            recv_sem=self.receive.at[at],
            device_id=device,
            device_id_type=pl.DeviceIdType.MESH,
        )
        near = pltpu.make_async_copy(source, target, self.receive.at[at])

        def start():
            @pl.when(is_swapped)
            def _():
                far.start()

            @pl.when(jnp.logical_not(is_swapped))
            def _():
                near.start()

        def wait():
            @pl.when(is_swapped)
            def _():
                far.wait_send()
                far.wait_recv()

            @pl.when(jnp.logical_not(is_swapped))
            def _():
                near.wait()

        return (start, wait)

    def homeward(self, source, target, device):
        at = self.used
        self.used += 1
        return pltpu.make_async_remote_copy(
            src_ref=source,
            dst_ref=target,
            send_sem=self.send.at[at],
            recv_sem=self.receive.at[at],
            device_id=device,
            device_id_type=pl.DeviceIdType.MESH,
        )

    def sent(self, copy):
        copy.wait_send()
        self.sends = [other for other in self.sends if other is not copy]

    def finish(self):
        for copy in self.sends:
            copy.wait_send()


class Place:
    def __init__(self, dp_size):
        group, self.dp, home = (lax.axis_index("group"), lax.axis_index("dp"), lax.axis_index("mp"))
        core, upper = (group % 2, home // 2)
        self.is_swapped = core != upper
        self.home = home
        self.rank = jnp.where(self.is_swapped, flip_two(home), home)
        self.swap = {"group": flip_one(group), "mp": flip_two(home)}
        self.core = {"group": flip_one(group)}
        self.next = {"mp": flip_one(home)}
        self.dp_peers = [{"dp": (self.dp + step) % dp_size} for step in range(1, dp_size)]

    def meet(self):
        barrier = pltpu.get_barrier_semaphore()
        peers = [self.core, self.next, self.swap] + self.dp_peers
        for peer in peers:
            pl.semaphore_signal(
                barrier, inc=1, device_id=peer, device_id_type=pl.DeviceIdType.MESH
            )
        pl.semaphore_wait(barrier, len(peers))


def column_of(row):
    size = row.shape[1]
    down = lax.broadcasted_iota(jnp.int32, (size, size), 0)
    along = lax.broadcasted_iota(jnp.int32, (size, size), 1)
    return jnp.sum(jnp.where(down == along, row, 0.0), 1, keepdims=True)


def rotate(rows, cosine, sine):
    half = ROT // 2
    one, two = (rows[:half], rows[half:ROT])
    return jnp.concatenate(
        [one * cosine - two * sine, two * cosine + one * sine, rows[ROT:]], 0
    )


def first_kernel(
    dp_size, x_ref, c_ref, entry_ref, exit_ref, shared_ref, ids_ref, vector_ref, cos_ref, sin_ref,
    xg, cg, a1, h, dh, big, small, kvw, ot, dqt, pair_grad, norm_ref, ub_grad, big_own,
    small_ref, big_ref, pair_ref, vector_other, qb_ref, kvb_ref, big_land, a2, smt, kvt, qt, dot_rows, kt, vt, k, v, dk, dv, s_ref, d_ref, l_ref, idr,
    g_send, g_recv, g_swap, send, receive,
):
    place = Place(dp_size)
    rank, dp = (place.rank, place.dp)
    copies = Copies(send, receive)
    local = x_ref.shape[0]
    length = 4 * local
    rows = entry_ref.shape[0]
    query_width = small_ref.shape[1] // 2
    heads = query_width // HS
    gathers_pair = shared_ref.shape[0] != D
    place.meet()
    vector_core = copies.remote(vector_ref, vector_other, place.core)

    def swapped(source, target):
        return copies.swapped(source, target, place.is_swapped, place.swap)

    def dp_rows(ref, start, size):
        return ref.at[pl.ds(pl.multiple_of(dp * rows + start, 16), size)]

    step = local // 2
    spans = [pl.ds(at * step, step) for at in range(2)]
    x_swaps = [swapped(x_ref.at[s], xg.at[0, s]) for s in spans]
    c_swaps = [swapped(c_ref.at[s], cg.at[0, s]) for s in spans]
    small_swap = swapped(small_ref, dp_rows(small, 0, rows))
    ids_swap = swapped(ids_ref, idr.at[:, pl.ds(0, local)])
    chunk = rows // 8 if rows % 128 == 0 else rows
    big_swaps = [
        swapped(big_ref.at[pl.ds(at, chunk)], dp_rows(big, at, chunk)) for at in range(0, rows, chunk)
    ]
    first = [ids_swap]
    if gathers_pair:
        pair_swap = swapped(pair_ref, kvw.at[dp, place.home])
        first.append(pair_swap)
    queue = iter([start for start, _ in x_swaps + [small_swap] + c_swaps])

    def start_next():
        start = next(queue, None)
        if start is not None:
            start()

    start_next()
    start_next()
    if gathers_pair:
        pair_ref[...] = shared_ref[...].astype(BF)
    for start, _ in first:
        start()
    small_ref[:, :query_width] = entry_ref[:, :query_width].astype(BF)
    small_ref[:, query_width:] = exit_ref[:query_width, :].T.astype(BF)
    wide = big_ref.shape[1] // 2
    big_ref[:, :wide] = entry_ref[:, query_width:].astype(BF)
    big_ref[:, wide:] = exit_ref[query_width:, :].T.astype(BF)
    vector_core.wait_recv()

    def role_vector(start, size):
        span = slice(start, start + size)
        return jnp.where(place.is_swapped, vector_other[:, span], vector_ref[:, span])

    for at in range(4):
        norm_ref[at : at + 1, :] = role_vector(at * D, D)
    kvb_ref[...] = column_of(role_vector(6 * D, 2 * HS))
    part = query_width + wide
    tail = 6 * D + 2 * HS
    in_bias = role_vector(tail, part)
    for at in range(1, 4):
        in_bias = jnp.where(rank == at, role_vector(tail + at * part, part), in_bias)
    qb_ref[...] = column_of(in_bias[:, :query_width])
    norm_ref[4:5, :] = in_bias[:, query_width:]

    def normalise(slot):
        def body(at, carry):
            span = pl.ds(pl.multiple_of(at * 128, 128), 128)
            wide = xg[slot, span, :].astype(F32)
            centered = wide - jnp.mean(wide, -1, keepdims=True)
            normal = centered * lax.rsqrt(
                jnp.mean(centered * centered, -1, keepdims=True) + NORM_EPS
            )
            a1[slot, span, :] = (normal * norm_ref[0:1, :] + norm_ref[1:2, :]).astype(BF)
            a2[slot, span, :] = (normal * norm_ref[2:3, :] + norm_ref[3:4, :]).astype(BF)
            return carry

        lax.fori_loop(0, local // 128, body, 0)

    def lanes(ref, slot):
        return ref.at[:, pl.ds(slot * local, local)]

    x_next, x_core, x_far = ([], [], [])
    for span, (_, wait) in zip(spans, x_swaps):
        wait()
        start_next()
        x_next.append(copies.remote(xg.at[0, span], xg.at[1, span], place.next))
        x_core.append(copies.remote(xg.at[0, span], xg.at[2, span], place.core))
    small_swap[1]()
    start_next()
    small_dp = [copies.remote(dp_rows(small, 0, rows), dp_rows(small, 0, rows), peer) for peer in place.dp_peers]
    ids_swap[1]()
    ids_next = copies.remote(lanes(idr, 0), lanes(idr, 1), place.next)
    ids_core = copies.remote(lanes(idr, 0), lanes(idr, 2), place.core)
    if gathers_pair:
        pair_swap[1]()
        own_pair = kvw.at[dp, rank]
        pair_next = copies.remote(own_pair, own_pair, place.next)
        pair_core = copies.remote(own_pair, own_pair, place.core)
    normalise(0)
    for span, copy in zip(spans, x_next):
        copy.wait_recv()
        x_far.append(copies.remote(xg.at[1, span], xg.at[3, span], place.core))
    ids_next.wait_recv()
    ids_far = copies.remote(lanes(idr, 1), lanes(idr, 3), place.core)
    if gathers_pair:
        pair_next.wait_recv()
        next_pair = kvw.at[dp, flip_one(rank)]
        pair_far = copies.remote(next_pair, next_pair, place.core)
        pair_core.wait_recv()
        pair_far.wait_recv()
        pair_dp = [copies.remote(kvw.at[dp], kvw.at[dp], peer) for peer in place.dp_peers]
    c_next, c_core, c_far, big_dp = ([], [], [], [])
    for span in spans:
        c_next.append(copies.remote(cg.at[0, span], cg.at[1, span], place.next, starts=False))
        c_core.append(copies.remote(cg.at[0, span], cg.at[2, span], place.core, starts=False))
        c_far.append(copies.remote(cg.at[1, span], cg.at[3, span], place.core, starts=False))
    for at in range(0, rows, chunk):
        part = dp_rows(big, at, chunk)
        big_dp.append([copies.remote(part, part, peer, starts=False) for peer in place.dp_peers])

    def c_arrives(at):
        c_swaps[at][1]()
        if at < len(big_swaps):
            big_swaps[at][0]()
        c_next[at].start()
        c_core[at].start()

    def c_passes(at):
        c_next[at].wait_recv()
        c_far[at].start()

    def big_arrives(at):
        big_swaps[at][1]()
        if at + 2 < len(big_swaps):
            big_swaps[at + 2][0]()
        for copy in big_dp[at]:
            copy.start()

    events = [functools.partial(big_arrives, at) for at in range(len(big_swaps))]
    events[2:2] = [functools.partial(c_passes, 0)]
    events[5:5] = [functools.partial(c_passes, 1)]
    for copy in x_core:
        copy.wait_recv()
    normalise(2)
    normalise(1)
    for copy in x_far:
        copy.wait_recv()
    normalise(3)
    for copy in small_dp:
        copy.wait_recv()
    smt[...] = small[...].T
    if gathers_pair:
        for copy in pair_dp:
            copy.wait_recv()
        kvt[...] = kvw[...].reshape(D, 2 * HS).T
    else:
        kvw[...] = shared_ref[...]
        kvt[...] = shared_ref[...].T
    c_arrives(0)
    for slot in range(4):
        block = at_slot(slot, rank)
        table = pl.ds(pl.multiple_of(block * local, local), local)
        cosine, sine = (cos_ref[:, table], sin_ref[:, table])
        tokens = pl.ds(slot * local, local)
        queries = dot_nt(smt[0:query_width, :], a1[slot]) + qb_ref[...]
        for head in range(heads):
            turned = rotate(queries[head * HS : (head + 1) * HS], cosine, sine).astype(BF)
            qt[head * HS : (head + 1) * HS, tokens] = turned * jnp.asarray(1.0 / math.sqrt(HS), BF)
        pairs = dot_nt(kvt[...], a1[slot]) + kvb_ref[...]
        turned = rotate(pairs[:HS], cosine, sine).astype(BF)
        kt[:, tokens] = turned
        k[tokens, :] = turned.T
        value = pairs[HS:].astype(BF)
        vt[:, tokens] = value
        v[tokens, :] = value.T
    c_arrives(1)
    for copy in (ids_core, ids_far):
        copy.wait_recv()
    ids = idr[...].astype(F32)
    first_end = jnp.sum(jnp.where(ids < 0.5, 1.0, 0.0), 1, keepdims=True)
    second_end = jnp.sum(jnp.where(ids < 1.5, 1.0, 0.0), 1, keepdims=True)

    def document(position):
        position = position.astype(F32)
        return jnp.where(position < first_end, 0.0, jnp.where(position < second_end, 1.0, 2.0))

    tiles = length // TILE
    per = tiles // 4

    def tile_at(tile):
        return pl.multiple_of(at_slot(tile // per, rank) * local + (tile % per) * TILE, TILE)

    def masked(scores, key, query):
        edge = key == 0 or query == tiles - 1
        allowed = None
        if key == query:
            down = lax.broadcasted_iota(jnp.int32, (TILE, TILE), 0)
            allowed = down <= lax.broadcasted_iota(jnp.int32, (TILE, TILE), 1)
        if edge:
            down = document(lax.broadcasted_iota(jnp.int32, (TILE, 1), 0) + key * TILE)
            along = document(lax.broadcasted_iota(jnp.int32, (1, TILE), 1) + query * TILE)
            same = down == along
            allowed = same if allowed is None else allowed & same
        return scores if allowed is None else jnp.where(allowed, scores, -1e9)

    def hooks(head, query, todo, first):
        for at, event in enumerate(todo):
            if query == first + at % (tiles - first):

                @pl.when(head == at // (tiles - first))
                def _():
                    event()

    def forward_head(head, carry):
        own = pl.ds(pl.multiple_of(head * HS, HS), HS)
        for query in range(tiles):
            hooks(head, query, events, 3)
            at_q = pl.ds(tile_at(query), TILE)
            q = qt[own, at_q]
            highest = jnp.full((1, TILE), -jnp.inf, F32)
            for key in range(query + 1):
                scores = masked(dot(k[pl.ds(tile_at(key), TILE), :], q), key, query)
                s_ref[pl.ds(key * TILE, TILE), :] = scores
                highest = jnp.maximum(highest, jnp.max(scores, 0, keepdims=True))
            total = jnp.zeros((1, TILE), F32)
            for key in range(query + 1):
                exponent = jnp.exp(s_ref[pl.ds(key * TILE, TILE), :] - highest)
                s_ref[pl.ds(key * TILE, TILE), :] = exponent
                total = total + jnp.sum(exponent, 0, keepdims=True)
            inverse = 1.0 / total
            mixed = jnp.zeros((HS, TILE), F32)
            for key in range(query + 1):
                softmax = (s_ref[pl.ds(key * TILE, TILE), :] * inverse).astype(BF)
                mixed = mixed + dot(vt[:, pl.ds(tile_at(key), TILE)], softmax)
            ot[own, at_q] = mixed.astype(BF)
            l_ref[head, :, at_q] = jnp.broadcast_to(highest + jnp.log(total), (8, TILE))
        return carry

    lax.fori_loop(0, heads, forward_head, 0)
    for event in events[heads * (tiles - 3) :]:
        event()

    for copy in c_core + c_far:
        copy.wait_recv()
    for copy in sum(big_dp, []):
        copy.wait_recv()
    ub_grad[...] = jnp.zeros_like(ub_grad)

    def perceptron(slot, carry):
        for at in range(0, local, TILE):
            span = pl.ds(at, TILE)
            pre = dot(a2[slot, span, :], big[:, :wide]) + norm_ref[4:5, :]
            below = 0.5 * (1.0 + lax.erf(pre * math.sqrt(0.5)))
            h[slot, span, :] = (pre * below).astype(BF)
            density = jnp.exp(-0.5 * pre * pre) * (1.0 / math.sqrt(2.0 * math.pi))
            grad = dot(cg[slot, span, :], big[:, wide:]) * (below + pre * density)
            grad = grad.astype(BF)
            dh[slot, span, :] = grad
            ub_grad[0:1, :] += jnp.sum(grad.astype(F32), 0, keepdims=True)
        tokens = pl.ds(pl.multiple_of(slot * local, local), local)
        dot_rows[:, tokens] = dot_nt(smt[query_width:, :], cg[slot]).astype(BF)
        return carry

    lax.fori_loop(0, 4, perceptron, 0)

    def big_grad(at):
        columns = pl.ds(pl.multiple_of(at, 128), 128)
        up, down = (0.0, 0.0)
        for slot in range(4):
            up = up + dot_tn(a2[slot, :, columns], dh[slot])
            down = down + dot_tn(cg[slot, :, columns], h[slot])
        return (up, down)

    shares = dp_size == 2 and rows % 128 == 0
    sums = []
    if shares:
        pieces = rows // 128
        for at in range(pieces):
            up, down = big_grad((1 - dp) * rows + at * 128)
            span = pl.ds(at * 128, 128)
            g_send[span, :wide] = up.astype(BF)
            g_send[span, wide:] = down.astype(BF)
            sums.append(copies.remote(g_send.at[span], g_recv.at[span], place.dp_peers[0]))
        for at in range(pieces):
            up, down = big_grad(dp * rows + at * 128)
            span = pl.ds(at * 128, 128)
            big_own[span, :wide] = up
            big_own[span, wide:] = down
        homes = [
            copies.homeward(g_swap.at[pl.ds(at * 128, 128)], big_land.at[pl.ds(at * 128, 128)], place.swap)
            for at in range(pieces)
        ]

        def sum_arrives(at):
            span = pl.ds(at * 128, 128)
            sums[at].wait_recv()
            total = big_own[span, :] + g_recv[span, :].astype(F32)
            big_own[span, :] = total

            @pl.when(place.is_swapped)
            def _():
                g_swap[span, :] = total.astype(BF)
                homes[at].start()

        later = [functools.partial(sum_arrives, at) for at in range(pieces)]
    else:

        def big_grad_rows(at, carry):
            up, down = big_grad(at * 128)
            span = pl.ds(pl.multiple_of(at * 128, 128), 128)
            big_own[span, :wide] = up
            big_own[span, wide:] = down
            return carry

        lax.fori_loop(0, D // 128, big_grad_rows, 0)
        later, homes = ([], [])

    dk[...] = jnp.zeros_like(dk)
    dv[...] = jnp.zeros_like(dv)

    def backward_head(head, carry):
        own = pl.ds(pl.multiple_of(head * HS, HS), HS)
        for query in range(tiles):
            hooks(head, query, later, 6)
            at_q = pl.ds(tile_at(query), TILE)
            q, do = (qt[own, at_q], dot_rows[own, at_q])
            scaled = do * jnp.asarray(1.0 / math.sqrt(HS), BF)
            log_total = l_ref[head, 0:1, at_q]
            inner = jnp.zeros((1, TILE), F32)
            for key in range(query + 1):
                at_k = pl.ds(tile_at(key), TILE)
                at_s = pl.ds(key * TILE, TILE)
                softmax = jnp.exp(masked(dot(k[at_k, :], q), key, query) - log_total)
                prob_grad = dot(v[at_k, :], scaled)
                s_ref[at_s, :] = softmax
                d_ref[at_s, :] = prob_grad
                inner = inner + jnp.sum(softmax * prob_grad, 0, keepdims=True)
            query_grad = jnp.zeros((HS, TILE), F32)
            for key in range(query + 1):
                at_k = pl.ds(tile_at(key), TILE)
                at_s = pl.ds(key * TILE, TILE)
                softmax = s_ref[at_s, :]
                score_grad = (softmax * (d_ref[at_s, :] - inner)).astype(BF)
                query_grad = query_grad + dot(kt[:, at_k], score_grad)
                dk[at_k, :] += dot_nt(score_grad, q)
                dv[at_k, :] += dot_nt(softmax.astype(BF), do)
            table = pl.ds(query * TILE, TILE)
            dqt[own, at_q] = rotate(query_grad, cos_ref[:, table], -sin_ref[:, table]).astype(BF)
        return carry

    lax.fori_loop(0, heads, backward_head, 0)
    for event in later[heads * (tiles - 6) :]:
        event()
    for slot in range(4):
        block = at_slot(slot, rank)
        table = pl.ds(pl.multiple_of(block * local, local), local)
        tokens = pl.ds(slot * local, local)
        key_grad = dk[tokens, :].T * math.sqrt(HS)
        pair_grad[0:HS, tokens] = rotate(key_grad, cos_ref[:, table], -sin_ref[:, table])
        pair_grad[HS:, tokens] = dv[tokens, :].T

    @pl.when(place.is_swapped)
    def _():
        for copy in homes:
            copy.wait_send()
            copy.wait_recv()
        if shares:
            big_own[...] = big_land[...].astype(F32)

    copies.finish()


def first_pass(dp_size, x, c, entry, leave, shared, ids, vector, cosine, sine):
    local = x.shape[0]
    length = 4 * local
    rows, part = entry.shape
    query_width = HEADS * HS // 4
    width = 2 * query_width
    wide = 2 * (part - query_width)
    heads = query_width // HS
    gathers_pair = shared.shape[0] != D
    shares = dp_size == 2 and rows % 128 == 0
    held = (rows if shares else 128, wide)
    tokens = ((4, local, D), BF)
    hidden = ((4, local, wide // 2), BF)
    outs = [
        tokens,
        tokens,
        tokens,
        hidden,
        hidden,
        ((D, wide), BF),
        ((D, width), BF),
        ((dp_size, 4, shared.shape[0], 2 * HS) if gathers_pair else (D, 2 * HS), BF),
        ((query_width, length), BF),
        ((query_width, length), BF),
        ((2 * HS, length), F32),
        ((8, D), F32),
        ((8, wide // 2), F32),
        ((rows if shares else D, wide), F32),
    ]
    vmem = pl.BlockSpec(memory_space=pltpu.VMEM)
    copies = 48 + 12 * dp_size
    work = query_width * length * length
    return pl.pallas_call(
        functools.partial(first_kernel, dp_size),
        out_shape=[jax.ShapeDtypeStruct(shape, kind) for shape, kind in outs],
        in_specs=[vmem] * 9,
        out_specs=[vmem] * len(outs),
        scratch_shapes=[
            pltpu.VMEM((rows, width), BF),
            pltpu.VMEM((rows, wide), BF),
            pltpu.VMEM((shared.shape[0] if gathers_pair else 16, 2 * HS), BF),
            pltpu.VMEM(vector.shape, F32),
            pltpu.VMEM((query_width, 1), F32),
            pltpu.VMEM((2 * HS, 1), F32),
            pltpu.VMEM(held, BF),
            pltpu.VMEM((4, local, D), BF),
            pltpu.VMEM((width, D), BF),
            pltpu.VMEM((2 * HS, D), BF),
            pltpu.VMEM((query_width, length), BF),
            pltpu.VMEM((query_width, length), BF),
            pltpu.VMEM((HS, length), BF),
            pltpu.VMEM((HS, length), BF),
            pltpu.VMEM((length, HS), BF),
            pltpu.VMEM((length, HS), BF),
            pltpu.VMEM((length, HS), F32),
            pltpu.VMEM((length, HS), F32),
            pltpu.VMEM((length, TILE), F32),
            pltpu.VMEM((length, TILE), F32),
            pltpu.VMEM((heads, 8, length), F32),
            pltpu.VMEM((1, length), jnp.int32),
            pltpu.VMEM(held, BF),
            pltpu.VMEM(held, BF),
            pltpu.VMEM(held, BF),
            pltpu.SemaphoreType.DMA((copies,)),
            pltpu.SemaphoreType.DMA((copies,)),
        ],
        compiler_params=pltpu.CompilerParams(
            collective_id=0, has_side_effects=True, vmem_limit_bytes=59 << 20
        ),
        cost_estimate=pl.CostEstimate(
            flops=60 * work, bytes_accessed=30 << 20, transcendentals=work // HS
        ),
        name="gather_attend",
    )(x, c, entry, leave, shared, ids, vector, cosine, sine)


def second_kernel(
    dp_size, sums_pair, x_ref, c_ref, bias_ref, xg, cg, a1, h, dh, big, small, kvw, ot, dqt, pair_grad,
    norm_ref, ub_grad,
    out_ref, grad_ref, small_own, vector_home, shared_home, pair_parts,
    y_land, u_land, small_land, stats, v_next, v_core, v_dp, s_core, s_next, s_dp,
    y_core, y_from, y_next, y_got, y_keep, y_home, u_core, u_from, u_next, u_got, u_keep, u_home,
    p_from, p_next, p_got, full, g_send, g_recv, g_swap, send, receive,
):
    place = Place(dp_size)
    copies = Copies(send, receive)
    local = xg.shape[1]
    wide = dh.shape[2]
    rows = small_own.shape[0]
    query_width = ot.shape[0]
    place.meet()
    pair_core = copies.remote(pair_grad.at[:, pl.ds(2 * local, 2 * local)], p_from, place.core)
    stats[...] = jnp.zeros_like(stats)

    def normal_of(slot):
        inputs = xg[slot].astype(F32)
        centered = inputs - jnp.mean(inputs, -1, keepdims=True)
        return centered * lax.rsqrt(jnp.mean(centered * centered, -1, keepdims=True) + NORM_EPS)

    def column_sum(rows_of):
        return jnp.sum(rows_of, 0, keepdims=True)

    def row_of(column):
        size = column.shape[0]
        down = lax.broadcasted_iota(jnp.int32, (size, size), 0)
        along = lax.broadcasted_iota(jnp.int32, (size, size), 1)
        return column_sum(jnp.where(down == along, column, 0.0))

    stats[4:5, :D] = column_sum(cg[0].astype(F32))
    tail = pl.ds(8 + place.rank, 1)
    stats[tail, :query_width] = row_of(jnp.sum(dqt[...].astype(F32), 1, keepdims=True))
    stats[tail, query_width : query_width + dh.shape[2]] = ub_grad[0:1, :]

    def both(slot):
        tokens = pl.ds(slot * local, local)
        branch = dot_nt(h[slot], big[:, wide:])
        branch = branch + dot_nt(ot[:, tokens].T, small[:, query_width:])
        first = dot_nt(dqt[:, tokens].T, small[:, :query_width])
        second = dot_nt(dh[slot], big[:, :wide])
        normal = normal_of(slot)
        stats[0:1, :D] += column_sum(first * normal)
        stats[1:2, :D] += column_sum(first)
        stats[2:3, :D] += column_sum(second * normal)
        stats[3:4, :D] += column_sum(second)
        return (branch, first * norm_ref[0:1, :] + second * norm_ref[2:3, :])

    step = local // 2
    spans = [pl.ds(at * step, step) for at in range(2)]
    y_cores, u_cores = ({}, {})
    for slot in (3, 2):
        branch, joined = both(slot)
        at = slot - 2
        u_core[at] = joined.astype(BF)
        u_cores[at] = copies.remote(u_core.at[at], u_from.at[at], place.core)
        y_core[at] = branch.astype(BF)
        y_cores[at] = copies.remote(y_core.at[at], y_from.at[at], place.core)
    pair_core.wait_recv()
    p_next[...] = pair_grad[:, local : 2 * local] + p_from[:, local:]
    pair_next = copies.remote(p_next, p_got, place.next)
    branch, joined = both(1)
    u_cores[1].wait_recv()
    u_next[...] = (joined + u_from[1].astype(F32)).astype(BF)
    u_nexts = [copies.remote(u_next.at[s], u_got.at[s], place.next) for s in spans]
    y_cores[1].wait_recv()
    y_next[...] = (branch + y_from[1].astype(F32)).astype(BF)

    turned = 0.0
    turned_out = 0.0
    for slot in range(4):
        tokens = pl.ds(slot * local, local)
        turned = turned + dot(dqt[:, tokens], a1[slot])
        turned_out = turned_out + dot(ot[:, tokens], cg[slot])
    full[:, :query_width] = turned.T
    full[:, query_width:] = turned_out.T
    shares = dp_size == 2 and rows < D
    if shares:
        g_send[...] = full[pl.ds(pl.multiple_of((1 - place.dp) * rows, 128), rows), :].astype(BF)
        small_sum = copies.remote(g_send, g_recv, place.dp_peers[0])
        small_home = copies.homeward(g_swap, small_land, place.swap)
        small_own[...] = full[pl.ds(pl.multiple_of(place.dp * rows, 128), rows), :]
    else:
        small_own[...] = full[...]

    branch, joined = both(0)
    u_cores[0].wait_recv()
    y_cores[0].wait_recv()
    y_keep[...] = branch + y_from[0].astype(F32)
    pair_next.wait_recv()
    pair_sum = (pair_grad[:, :local] + p_from[:, :local] + p_got[...]).astype(BF)
    stats[5:6, : 2 * HS] = row_of(jnp.sum(pair_sum.astype(F32), 1, keepdims=True))
    through_pair = dot_nt(pair_sum.T, kvw[...])
    stats[0:1, :D] += column_sum(through_pair * normal_of(0))
    stats[1:2, :D] += column_sum(through_pair)
    u_keep[...] = joined + u_from[0].astype(F32) + through_pair * norm_ref[0:1, :]
    pair_parts[...] = dot(pair_sum, a1[0]).T.reshape(pair_parts.shape)
    vector_core = copies.remote(stats, v_core, place.core)
    if sums_pair:
        shared_core = copies.remote(pair_parts, s_core, place.core)

    def sent_home(source, target):
        return copies.swapped(source, target, place.is_swapped, place.swap)

    homes = []
    if shares:
        small_sum.wait_recv()
        total = small_own[...] + g_recv[...].astype(F32)
        small_own[...] = total

        @pl.when(place.is_swapped)
        def _():
            g_swap[...] = total.astype(BF)
            small_home.start()

    vector_core.wait_recv()
    copies.sent(vector_core)
    stats[...] = stats[...] + v_core[...]
    vector_next = copies.remote(stats, v_next, place.next)
    if sums_pair:
        shared_core.wait_recv()
        copies.sent(shared_core)
        pair_parts[...] = pair_parts[...] + s_core[...]
        shared_next = [
            copies.remote(pair_parts.at[at * 4 + flip_one(place.rank)], s_next.at[at], place.next)
            for at in range(dp_size)
        ]
    vector_next.wait_recv()
    copies.sent(vector_next)
    stats[...] = stats[...] + v_next[...]
    vector_dp = [
        copies.remote(stats, v_dp.at[at], peer) for at, peer in enumerate(place.dp_peers)
    ]
    if sums_pair:
        for at, copy in enumerate(shared_next):
            copy.wait_recv()
            s_next[at] = s_next[at] + pair_parts[at * 4 + place.rank]
        shared_dp = [
            copies.remote(s_next.at[(place.dp + at + 1) % dp_size], s_dp.at[at], peer)
            for at, peer in enumerate(place.dp_peers)
        ]
    for copy in vector_dp:
        copy.wait_recv()
        copies.sent(copy)
    total = stats[...]
    for at in range(dp_size - 1):
        total = total + v_dp[at]
    stats[...] = total
    small_homes = [sent_home(stats, vector_home)]
    if sums_pair:
        for copy in shared_dp:
            copy.wait_recv()
        total = s_next[place.dp]
        for at in range(dp_size - 1):
            total = total + s_dp[at]
        s_core[0] = total
        small_homes.append(sent_home(s_core.at[0], shared_home))
    for start, _ in small_homes:
        start()
    y_nexts = []
    for span, copy in zip(spans, u_nexts):
        copy.wait_recv()
        y_nexts.append(copies.remote(y_next.at[span], y_got.at[span], place.next))
        u_home[span, :] = (u_keep[span, :] + u_got[span, :].astype(F32)).astype(BF)
        homes.append(sent_home(u_home.at[span], u_land.at[span]))
        homes[-1][0]()
    for span, copy in zip(spans, y_nexts):
        copy.wait_recv()
        y_home[span, :] = (y_keep[span, :] + y_got[span, :].astype(F32)).astype(BF)
        homes.append(sent_home(y_home.at[span], y_land.at[span]))
        homes[-1][0]()
    for span, (_, wait) in zip(spans, homes):
        wait()
        inputs = x_ref[span, :].astype(F32)
        centered = inputs - jnp.mean(inputs, -1, keepdims=True)
        scale = lax.rsqrt(jnp.mean(centered * centered, -1, keepdims=True) + NORM_EPS)
        normal = centered * scale
        joined = u_land[span, :].astype(F32)
        grad_ref[span, :] = c_ref[span, :].astype(F32) + scale * (
            joined
            - jnp.mean(joined, -1, keepdims=True)
            - normal * jnp.mean(joined * normal, -1, keepdims=True)
        )
    bias = bias_ref[:, 4 * D : 5 * D] + bias_ref[:, 5 * D : 6 * D]
    for span, (_, wait) in zip(spans, homes[2:]):
        wait()
        out_ref[span, :] = x_ref[span, :].astype(F32) + y_land[span, :].astype(F32) + bias
    for _, wait in small_homes:
        wait()
    if shares:

        @pl.when(place.is_swapped)
        def _():
            small_home.wait_send()
            small_home.wait_recv()
            small_own[...] = small_land[...].astype(F32)

    copies.finish()


def second_pass(
    dp_size, x, c, vector, xg, cg, a1, h, dh, big, small, kvw, ot, dqt, pair_grad, norms, ub_grad, piece
):
    local = xg.shape[1]
    length = 4 * local
    width = small.shape[1]
    rows = D // dp_size
    shares = dp_size == 2 and rows % 128 == 0
    sums_pair = piece % 16 == 0
    held = (rows if shares else 8, width)
    parts = (4 * dp_size, piece, 2 * HS) if sums_pair else (1, D, 2 * HS)
    own = (piece if sums_pair else 8, 2 * HS)
    outs = [
        (local, D),
        (local, D),
        (rows if shares else D, width),
        (16, 1024),
        own,
        parts,
    ]
    vmem = pl.BlockSpec(memory_space=pltpu.VMEM)
    branch = [
        pltpu.VMEM((2, local, D), BF),
        pltpu.VMEM((2, local, D), BF),
        pltpu.VMEM((local, D), BF),
        pltpu.VMEM((local, D), BF),
        pltpu.VMEM((local, D), F32),
        pltpu.VMEM((local, D), BF),
    ]
    work = length * D * D
    return pl.pallas_call(
        functools.partial(second_kernel, dp_size, sums_pair),
        out_shape=[jax.ShapeDtypeStruct(shape, F32) for shape in outs],
        in_specs=[vmem] * 16,
        out_specs=[vmem] * len(outs),
        scratch_shapes=[
            pltpu.VMEM((local, D), BF),
            pltpu.VMEM((local, D), BF),
            pltpu.VMEM(held, BF),
            pltpu.VMEM((16, 1024), F32),
            pltpu.VMEM((16, 1024), F32),
            pltpu.VMEM((16, 1024), F32),
            pltpu.VMEM((dp_size - 1, 16, 1024), F32),
            pltpu.VMEM(parts, F32),
            pltpu.VMEM((dp_size,) + own, F32),
            pltpu.VMEM((dp_size - 1,) + own, F32),
        ]
        + branch
        + branch
        + [
            pltpu.VMEM((2 * HS, 2 * local), F32),
            pltpu.VMEM((2 * HS, local), F32),
            pltpu.VMEM((2 * HS, local), F32),
            pltpu.VMEM((D, width), F32),
            pltpu.VMEM(held, BF),
            pltpu.VMEM(held, BF),
            pltpu.VMEM(held, BF),
            pltpu.SemaphoreType.DMA((32 + 3 * dp_size,)),
            pltpu.SemaphoreType.DMA((32 + 3 * dp_size,)),
        ],
        compiler_params=pltpu.CompilerParams(
            collective_id=1, has_side_effects=True, vmem_limit_bytes=59 << 20
        ),
        cost_estimate=pl.CostEstimate(flops=8 * work, bytes_accessed=30 << 20, transcendentals=0),
        name="sum_branches",
    )(x, c, vector, xg, cg, a1, h, dh, big, small, kvw, ot, dqt, pair_grad, norms, ub_grad)


def outer_step(total, groups, anchor, velocity):
    change = total / groups
    momentum = OUTER_BETA * velocity + change
    return (change, momentum, anchor - OUTER_RATE * (change + OUTER_BETA * momentum))


def third_kernel(
    groups, big_grad, small_grad, vector_grad, shared_grad,
    ew, em, ev, ea, eu, xw, xm, xv, xa, xu, sw, sm, sv, sa, su, vw, vm, vv, va, vu,
    em2, ev2, ew2, ec, ep, eg, xm2, xv2, xw2, xc, xp, xg, sm2, sv2, sw2, sc, sp, sg, vm2, vv2, vw2, vc, vp, vg,
    entry_grad, exit_grad, e_send, e_from, e_low, e_got, e_sum, e_back,
    x_send, x_from, x_low, x_got, x_sum, x_back, s_gap, s_core, s_part, s_half, v_gap, v_core, v_part, v_half,
    send, receive,
):
    group = lax.axis_index("group")
    core = group % 2
    mate, across = ({"group": flip_one(group)}, {"group": flip_two(group)})
    copies = Copies(send, receive)
    barrier = pltpu.get_barrier_semaphore()
    for peer in (mate, across):
        pl.semaphore_signal(barrier, inc=1, device_id=peer, device_id_type=pl.DeviceIdType.MESH)
    pl.semaphore_wait(barrier, 2)
    query_width = small_grad.shape[1] // 2
    wide = big_grad.shape[1] // 2

    def halves(ref):
        size = ref.shape[0] // 2
        return [pl.ds(pl.multiple_of(at * size, 8), size) for at in (core, 1 - core)]

    def update(span, grad, olds, news, rate, decay):
        weight, first, second, anchor = (ref[span, :] for ref in olds)
        first, second, new = adamw_update(weight, first, second, grad, rate, decay)
        news[0][span, :] = first
        news[1][span, :] = second
        news[2][span, :] = new
        return anchor - new

    entry_grad[:, :query_width] = small_grad[:, :query_width]
    entry_grad[:, query_width:] = big_grad[:, :wide]
    entry = ((ew, em, ev, ea), (em2, ev2, ew2))
    leave = ((xw, xm, xv, xa), (xm2, xv2, xw2))
    e_own, e_other = halves(ew)
    x_own, x_other = halves(xw)
    e_send[...] = update(e_other, entry_grad[e_other, :], *entry, MATRIX_RATE, MATRIX_DECAY)
    e_core = copies.remote(e_send, e_from, mate)
    e_sum[...] = update(e_own, entry_grad[e_own, :], *entry, MATRIX_RATE, MATRIX_DECAY)
    e_core.wait_recv()
    e_low[...] = (e_sum[...] + e_from[...]).astype(BF)
    e_across = copies.remote(e_low, e_got, across)
    exit_grad[:query_width, :] = small_grad[:, query_width:].T
    exit_grad[query_width:, :] = big_grad[:, wide:].T
    x_send[...] = update(x_other, exit_grad[x_other, :], *leave, MATRIX_RATE, MATRIX_DECAY)
    x_core = copies.remote(x_send, x_from, mate)
    x_sum[...] = update(x_own, exit_grad[x_own, :], *leave, MATRIX_RATE, MATRIX_DECAY)
    x_core.wait_recv()
    x_low[...] = (x_sum[...] + x_from[...]).astype(BF)
    x_across = copies.remote(x_low, x_got, across)
    every = slice(None)
    s_gap[...] = update(
        every, shared_grad[...], (sw, sm, sv, sa), (sm2, sv2, sw2), MATRIX_RATE, MATRIX_DECAY
    )
    shared_core = copies.remote(s_gap, s_core, mate)
    part = query_width + wide
    rows = [vector_grad[at : at + 1, :D] for at in (0, 1, 2, 3, 4, 4)]
    rows.append(vector_grad[5:6, : 2 * HS])
    rows += [vector_grad[8 + at : 9 + at, :part] for at in range(4)]
    v_gap[...] = update(
        every, jnp.concatenate(rows, 1), (vw, vm, vv, va), (vm2, vv2, vw2), VECTOR_RATE, 0.0
    )
    vector_core = copies.remote(v_gap, v_core, mate)
    shared_core.wait_recv()
    s_part[...] = s_gap[...] + s_core[...]
    shared_across = copies.remote(s_part, s_half, across)
    vector_core.wait_recv()
    v_part[...] = v_gap[...] + v_core[...]
    vector_across = copies.remote(v_part, v_half, across)

    def finish(span, total, anchor, velocity, outs):
        for ref, value in zip(outs, outer_step(total, groups, anchor[span, :], velocity[span, :])):
            ref[span, :] = value

    backs = []
    for across_copy, low, got, total, back, own, anchor, velocity, outs in (
        (e_across, e_low, e_got, e_sum, e_back, e_own, ea, eu, (ec, ep, eg)),
        (x_across, x_low, x_got, x_sum, x_back, x_own, xa, xu, (xc, xp, xg)),
    ):
        across_copy.wait_recv()
        total[...] = low[...].astype(F32) + got[...].astype(F32)
        backs.append(copies.remote(total, back, mate))
        finish(own, total[...], anchor, velocity, outs)
    shared_across.wait_recv()
    finish(every, s_part[...] + s_half[...], sa, su, (sc, sp, sg))
    vector_across.wait_recv()
    finish(every, v_part[...] + v_half[...], va, vu, (vc, vp, vg))
    backs[0].wait_recv()
    finish(e_other, e_back[...], ea, eu, (ec, ep, eg))
    backs[1].wait_recv()
    finish(x_other, x_back[...], xa, xu, (xc, xp, xg))
    copies.finish()


def third_pass(groups, grads, entry, leave, shared, vector):
    vmem = pl.BlockSpec(memory_space=pltpu.VMEM)
    outs = [array[0] for array in (entry, leave, shared, vector) for _ in range(6)]

    def half(array, kind):
        return pltpu.VMEM((array.shape[0] // 2, array.shape[1]), kind)

    def whole(array):
        return [pltpu.VMEM(array.shape, F32)] * 4

    def sums(array):
        return [half(array, kind) for kind in (F32, F32, BF, BF, F32, F32)]

    arrays = list(grads) + [array for arrays in (entry, leave, shared, vector) for array in arrays]
    return pl.pallas_call(
        functools.partial(third_kernel, groups),
        out_shape=[jax.ShapeDtypeStruct(array.shape, F32) for array in outs],
        in_specs=[vmem] * len(arrays),
        out_specs=[vmem] * len(outs),
        scratch_shapes=[pltpu.VMEM(entry[0].shape, F32), pltpu.VMEM(leave[0].shape, F32)]
        + sums(entry[0])
        + sums(leave[0])
        + whole(shared[0])
        + whole(vector[0])
        + [pltpu.SemaphoreType.DMA((16,)), pltpu.SemaphoreType.DMA((16,))],
        compiler_params=pltpu.CompilerParams(
            collective_id=2, has_side_effects=True, vmem_limit_bytes=59 << 20
        ),
        cost_estimate=pl.CostEstimate(flops=1 << 26, bytes_accessed=40 << 20, transcendentals=1 << 20),
        name="update_weights",
    )(*arrays)

def shards(
    hidden_in,
    doc_ids,
    out_cotangent,
    entry_weight,
    entry_first,
    entry_second,
    entry_anchor,
    entry_velocity,
    exit_weight,
    exit_first,
    exit_second,
    exit_anchor,
    exit_velocity,
    shared_weight,
    shared_first,
    shared_second,
    shared_anchor,
    shared_velocity,
    vector_weight,
    vector_first,
    vector_second,
    vector_anchor,
    vector_velocity,
):
    batch, local_len = hidden_in.shape[:2]
    parts = lax.axis_size("mp")
    group, rank = (lax.axis_index("group"), lax.axis_index("mp"))
    is_swapped = (group % 2) != (rank // 2)
    rank = jnp.where(is_swapped, jnp.bitwise_xor(rank, 2), rank)
    length = local_len * parts
    part_width = entry_weight.shape[2]
    query_width = HEADS * HS // parts
    heads = query_width // HS

    dp_size = lax.axis_size("dp")
    order = jnp.bitwise_xor(jnp.arange(parts), rank)
    piece = shared_weight.shape[1]
    shared_piece = shared_weight[0]
    if piece % 16:
        pieces = gather_square(swapped_parts(shared_piece.astype(BF)))
        pieces = jnp.take(pieces, order, axis=0)
        shared_piece = gather_dp(pieces.reshape(-1, 2 * HS), 0)
    half = ROT // 2
    frequency = 10000.0 ** (-(np.arange(half) * 2.0 / ROT))
    angles = frequency.astype(np.float32)[:, None] * np.arange(length, dtype=np.float32)[None, :]
    cosine_table = jnp.asarray(np.cos(angles.astype(np.float64)).astype(np.float32))
    sine_table = jnp.asarray(np.sin(angles.astype(np.float64)).astype(np.float32))
    (
        inputs, cots, attn_input, hidden, hidden_grad, big, small, pair_weight, attended, query_grad,
        pair_rows, norms, up_bias_rows, big_grad,
    ) = first_pass(
        dp_size,
        hidden_in[0],
        out_cotangent[0],
        entry_weight[0],
        exit_weight[0],
        shared_piece,
        doc_ids,
        vector_weight,
        cosine_table,
        sine_table,
    )
    block_output, input_grad, small_grad, vector_grad, shared_grad, pair_parts = second_pass(
        dp_size, hidden_in[0], out_cotangent[0], vector_weight, inputs, cots, attn_input, hidden,
        hidden_grad, big, small, pair_weight.reshape(D, 2 * HS), attended, query_grad, pair_rows, norms,
        up_bias_rows, piece,
    )
    if big_grad.shape[0] == D:
        big_grad, small_grad = (scatter_dp(array, 0, F32) for array in (big_grad, small_grad))
        big_grad, small_grad = (swapped_parts(array) for array in (big_grad, small_grad))
    if piece % 16:
        grad_pieces = pair_parts.reshape(dp_size, parts, -1, 2 * HS)
        grad_pieces = jnp.take(grad_pieces, order, axis=1).swapaxes(0, 1)
        shared_grad = scatter_dp(scatter_square(grad_pieces, F32), 0, F32)
        shared_grad = swapped_parts(shared_grad.reshape(-1, 2 * HS))
    updated = third_pass(
        lax.axis_size("group"),
        (big_grad, small_grad, vector_grad, shared_grad),
        (entry_weight[0], entry_first[0], entry_second[0], entry_anchor, entry_velocity),
        (exit_weight[0], exit_first[0], exit_second[0], exit_anchor, exit_velocity),
        (shared_weight[0], shared_first[0], shared_second[0], shared_anchor, shared_velocity),
        (vector_weight, vector_first, vector_second, vector_anchor[None], vector_velocity[None]),
    )
    updated = list(updated)
    results = [block_output[None], input_grad[None]]
    for at in range(3):
        results += [array[None] for array in updated[6 * at : 6 * at + 3]]
        results += updated[6 * at + 3 : 6 * at + 6]
    results += updated[18:21] + [array[0] for array in updated[21:24]]
    return tuple(results)


def solution(mesh):
    in_specs = (
        P(("group", "dp"), "mp", None),
        P(("group", "dp"), "mp"),
        P(("group", "dp"), "mp", None),
        P("group", "dp", "mp"),
        P("group", "dp", "mp"),
        P("group", "dp", "mp"),
        P("dp", "mp"),
        P("dp", "mp"),
        P("group", "mp", "dp"),
        P("group", "mp", "dp"),
        P("group", "mp", "dp"),
        P("mp", "dp"),
        P("mp", "dp"),
        P("group", ("dp", "mp"), None),
        P("group", ("dp", "mp"), None),
        P("group", ("dp", "mp"), None),
        P(("dp", "mp"), None),
        P(("dp", "mp"), None),
        P("group", None),
        P("group", None),
        P("group", None),
        P(),
        P(),
    )
    out_specs = (
        P(("group", "dp"), "mp", None),
        P(("group", "dp"), "mp", None),
        P("group", "dp", "mp"),
        P("group", "dp", "mp"),
        P("group", "dp", "mp"),
        P("dp", "mp"),
        P("dp", "mp"),
        P("dp", "mp"),
        P("group", "mp", "dp"),
        P("group", "mp", "dp"),
        P("group", "mp", "dp"),
        P("mp", "dp"),
        P("mp", "dp"),
        P("mp", "dp"),
        P("group", ("dp", "mp"), None),
        P("group", ("dp", "mp"), None),
        P("group", ("dp", "mp"), None),
        P(("dp", "mp"), None),
        P(("dp", "mp"), None),
        P(("dp", "mp"), None),
        P("group", None),
        P("group", None),
        P("group", None),
        P(),
        P(),
        P(),
    )
    return jax.shard_map(shards, mesh=mesh, in_specs=in_specs, out_specs=out_specs, check_vma=False)
```

time: 408 us -> 324 us (0.79)
  Pallas kernels: 161 us -> 275 us
  waiting for transfers between devices: 60.7 us -> 0 us
  starting transfers between devices: 52.7 us -> 0 us
  other arithmetic: 49 us -> 2.09 us
  matrix products: 45 us -> 0 us
  local copies, waits for them, and re-layouts: 31.1 us -> 41.9 us
    pallas_call x0 -> x2, Pallas kernels: none -> 126 us  [the longest x1 87.4 us: second_pass(): pl.pallas_call(functools.partial(second_kernel, dp_size, sums_pair), out_...]
    ppermute x32 -> x0, waiting for transfers between devices: 60.7 us -> none  [the longest x6 47.2 us: swapped_parts(): return lax.ppermute(array, ('group', 'mp'), pairs)]
    ppermute x32 -> x0, starting transfers between devices: 52.7 us -> none  [the longest x6 24.1 us: swapped_parts(): return lax.ppermute(array, ('group', 'mp'), pairs)]
    dot_general x12 -> x0, matrix products: 45 us -> none  [the longest x4 16.2 us: dot(): return jnp.dot(left, right, preferred_element_type=F32)]
    unnamed x143 -> x90, local copies, waits for them, and re-layouts: 8.16 us -> 40.6 us
    sub x8 -> x0, other arithmetic: 15.9 us -> none  [the longest x4 6.35 us: shards(): anchors[position] - OUTER_RATE * (change + OUTER_BETA * momentum)]
    pallas_call x1, Pallas kernels: 161 us -> 150 us  [first_pass(): pl.pallas_call(functools.partial(first_kernel, dp_size), out_shape=[jax.S...]
    convert_element_type x8 -> x0, other arithmetic: 9.13 us -> none  [the longest x2 3.03 us: sum_groups(): part = (kept + over_core(sent)).astype(send_type)]
  transfers between devices with their start and end apart: 32 -> 0, of which waited for: 10 -> 0; matrix products, arithmetic and copies ran while one was open for 22% -> 0% of each run, Pallas kernels for 0% -> 0%
where the time goes in v3:
time: 324 us; the launch traced here: 320 us
  Pallas kernels  275 us (85%)
  local copies, waits for them, and re-layouts  41.9 us (13%)
    pallas_call x1, Pallas kernels, first_pass(): pl.pallas_call(functools.partial(first_kernel, dp_size), out_shape=[jax.S...  150 us
    pallas_call x1, Pallas kernels, second_pass(): pl.pallas_call(functools.partial(second_kernel, dp_size, sums_pair), out_...  87.4 us
    unnamed x90, local copies, waits for them, and re-layouts  40.6 us
    pallas_call x1, Pallas kernels, third_pass(): pl.pallas_call(functools.partial(third_kernel, groups), out_shape=[jax.Sh...  38.2 us

profile of v3, /device:TPU:1, one launch (start us, length us, event | category | flops | bytes accessed | tf_op | source)
XLA Modules:
  0.0 320.5 jit_solution(10552144930506187315)
XLA Ops:
  0.7 3.0 copy.51
  3.7 149.8 %gather_attend.1 = (bf16[4,512,768]{2,1,0:T(8,128)(2,1)}, bf16[4,512,768]{2,1,0:T(8,128)(2,1)}, bf16[4,512,768]{2,1,0:T(8,128)(2,1)}, bf16[4,512,768]{2,1,0:T(8,...) custom-call(bf16[512,768]{1,0:T(8,128)(2,1)} %bitcast.46, ...), custom_call_target="tpu_custom_call" | custom-call | flops 48318382080 | bytes 31457280 | tf_op jit(solution)/shard_map/gather_attend/pallas_call | solution.py:678
  153.5 0.0 copy-start.7
  153.5 87.4 %sum_branches.1 = (f32[512,768]{1,0:T(8,128)}, f32[512,768]{1,0:T(8,128)}, f32[384,384]{1,0:T(8,128)}, f32[16,1024]{1,0:T(8,128)}, f32[96,128]{1,0:T(8,128)}, /*index=5*/f32[8,96,128]{2,1,0:T(8,128)}) custom-call(bf16[512,768]{1,0:T(8,128)(2,1)} %bitcast.47, bf16[512,768]{1,0:T(8,128)(2,1)} %bitcast.49, f32[1,8576]{1,0:T(1,128)} %vw.1, ...), custom_call_target="tpu_custom_call" | custom-call | flops 9663676416 | bytes 31457280 | tf_op jit(solution)/shard_map/sum_branches/pallas_call | solution.py:954
  241.0 0.0 copy-start.8
  241.0 1.6 copy.52
  242.6 1.6 copy.53
  244.2 1.6 copy.54.ea
  245.9 1.6 copy.55.eu
  247.5 0.6 broadcast_in_dim.41.va
  248.1 0.0 copy-done.24
  248.1 0.6 broadcast_in_dim.42.vu
  248.8 38.2 %update_weights.1 = (f32[384,960]{1,0:T(8,128)}, f32[384,960]{1,0:T(8,128)}, f32[384,960]{1,0:T(8,128)}, f32[384,960]{1,0:T(8,128)}, f32[384,960]{1,0:T(8,128)},...) custom-call(f32[384,1536]{1,0:T(8,128)} %get-tuple-element.84.big_gr, ...), custom_call_target="tpu_custom_call" | custom-call | flops 67108864 | bytes 41943040 | tf_op jit(solution)/shard_map/update_weights/pallas_call | solution.py:1107
  287.0 3.1 copy.56
  290.1 0.0 copy-done.6
  290.1 1.6 copy.57
  291.7 1.6 copy.58
  293.2 1.6 copy.59
  294.8 1.6 copy.60
  296.4 1.6 copy.61
  297.9 0.7 reduce
  298.6 0.7 reduce.1
  299.3 0.0 copy-done.28
  299.3 0.7 reduce.2
  300.1 1.1 copy.79
  301.2 0.8 copy-done
  302.0 1.1 copy.80
  303.2 0.8 copy-done.16
  304.0 1.1 copy.81
  305.1 0.8 copy-done.15
  305.9 1.1 copy.82
  307.0 0.8 copy-done.14
  307.8 1.1 copy.83
  308.9 0.8 copy-done.13
  309.7 1.1 copy.84
  310.8 0.8 copy-done.12
  311.6 1.1 copy.85
  312.7 0.8 copy-done.11
  313.6 1.1 copy.86
  314.7 0.6 copy.87
  315.3 0.6 copy.88
  315.9 0.6 copy.89
  316.5 0.6 copy.90
  317.2 0.6 copy.91
  317.8 0.6 copy.92
  318.4 0.6 copy.93
  319.0 0.6 copy.94
  319.7 0.6 copy.95
  (50 shorter events, 0.1 us)
Async XLA Ops:
  153.5 87.4 %copy-start.7 = (f32[1,384,960]{1,2,0:T(8,128)S(1)}, f32[1,384,960]{1,2,0:T(8,128)}, u32[]{:S(2)}) copy-start(f32[1,384,960]{1,2,0:T(8,128)} %param.29) | copy-start | bytes 4423684
  241.0 1.6 copy-start.8
  242.6 1.6 copy-start.9
  244.2 1.6 copy-start.10
  245.8 1.7 copy-start.23
  245.9 2.3 copy-start.24
  287.0 3.1 copy-start.6
  290.1 1.6 copy-start.5
  291.7 1.6 copy-start.4
  293.2 1.6 copy-start.3
  294.8 1.6 copy-start.2
  296.4 1.6 copy-start.30
  296.4 2.3 copy-start.29
  296.4 3.0 copy-start.28
  296.4 3.7 %copy-start.1 = (f32[512,768]{1,0:T(8,128)S(1)}, f32[512,768]{1,0:T(8,128)}, u32[]{:S(2)}) copy-start(f32[512,768]{1,0:T(8,128)} %get-tuple-element.82) | copy-start | bytes 4718596
  300.0 2.0 copy-start
  302.0 1.9 copy-start.16
  304.0 1.9 copy-start.15
  305.9 1.9 copy-start.14
  307.8 1.9 copy-start.13
  309.7 1.9 copy-start.12
  311.6 1.9 copy-start.11
  313.5 1.2 copy-start.22
  313.5 1.8 copy-start.21
  313.5 2.4 copy-start.20
  313.5 3.0 copy-start.19
  313.5 3.7 %copy-start.18 = (f32[96,128]{1,0:T(8,128)S(1)}, f32[96,128]{1,0:T(8,128)}, u32[]{:S(2)}) copy-start(f32[96,128]{1,0:T(8,128)} %get-tuple-element.182) | copy-start | bytes 147460
  313.5 4.3 %copy-start.17 = (f32[96,128]{1,0:T(8,128)S(1)}, f32[96,128]{1,0:T(8,128)}, u32[]{:S(2)}) copy-start(f32[96,128]{1,0:T(8,128)} %get-tuple-element.183) | copy-start | bytes 147460
  313.5 4.9 %copy-start.27 = (f32[1,8576]{1,0:T(1,128)S(1)}, f32[1,8576]{1,0:T(1,128)}, u32[]{:S(2)}) copy-start(f32[1,8576]{1,0:T(1,128)} %get-tuple-element.184) | copy-start | bytes 102916
  313.5 5.5 %copy-start.26 = (f32[1,8576]{1,0:T(1,128)S(1)}, f32[1,8576]{1,0:T(1,128)}, u32[]{:S(2)}) copy-start(f32[1,8576]{1,0:T(1,128)} %get-tuple-element.185) | copy-start | bytes 102916
  313.6 6.1 %copy-start.25 = (f32[1,8576]{1,0:T(1,128)S(1)}, f32[1,8576]{1,0:T(1,128)}, u32[]{:S(2)}) copy-start(f32[1,8576]{1,0:T(1,128)} %get-tuple-element.186) | copy-start | bytes 102916

commit v4 on v3

v4 whole, which is shorter than its diff:
```python
import functools
import math

import jax
import jax.numpy as jnp
import numpy as np
from jax import lax
from jax.experimental import pallas as pl
from jax.experimental.pallas import tpu as pltpu
from jax.sharding import PartitionSpec as P

D = 768
HEADS = 12
HS = 64
ROT = 16
STEP = 5
IN_COLS = 3840


NORM_EPS = 1e-05
BETA_ONE = 0.9
BETA_TWO = 0.95
ADAM_EPS = 1e-08
MATRIX_RATE = 0.03
MATRIX_DECAY = 0.1
VECTOR_RATE = 0.3
OUTER_RATE = 0.7
OUTER_BETA = 0.9

TILE = 256
F32 = jnp.float32
BF = jnp.bfloat16


def dot(left, right):
    return jnp.dot(left, right, preferred_element_type=F32)


def dot_nt(left, right):
    return lax.dot_general(left, right, (((1,), (1,)), ((), ())), preferred_element_type=F32)


def dot_tn(left, right):
    return lax.dot_general(left, right, (((0,), (0,)), ((), ())), preferred_element_type=F32)


def adamw_update(weight, first, second, gradient, step_rate, decay):
    first_new = BETA_ONE * first + (1.0 - BETA_ONE) * gradient
    second_new = BETA_TWO * second + (1.0 - BETA_TWO) * gradient * gradient
    fix_first = 1.0 - BETA_ONE**STEP
    fix_second = 1.0 - BETA_TWO**STEP
    update = first_new / fix_first / (jnp.sqrt(second_new / fix_second) + ADAM_EPS)
    return (first_new, second_new, weight - step_rate * (update + decay * weight))


def pairs_of(size, bit):
    return [(at, at ^ bit) for at in range(size)]


def over_core(array):
    return lax.ppermute(array, "group", pairs_of(lax.axis_size("group"), 1))


def over_next(array):
    return lax.ppermute(array, "mp", pairs_of(lax.axis_size("mp"), 1))


def over_dp(array):
    return lax.ppermute(array, "dp", pairs_of(2, 1))


def swapped_parts(array):
    parts = lax.axis_size("mp")
    pairs = []
    for group in range(lax.axis_size("group")):
        for rank in range(parts):
            here = group * parts + rank
            there = (group ^ 1) * parts + (rank ^ 2)
            pairs.append((here, there if group % 2 != rank // 2 else here))
    return lax.ppermute(array, ("group", "mp"), pairs)


def gather_square(own):
    pair = jnp.stack([own, over_next(own)])
    return jnp.concatenate([pair, over_core(pair)], 0)


def scatter_square(slots, send_type):
    pair = slots[:2] + over_core(slots[2:].astype(send_type)).astype(F32)
    return pair[0] + over_next(pair[1].astype(send_type)).astype(F32)


def gather_dp(own, axis):
    if lax.axis_size("dp") == 2:
        other = over_dp(own)
        first = lax.axis_index("dp") == 0
        return jnp.concatenate(
            [jnp.where(first, own, other), jnp.where(first, other, own)], axis
        )
    return lax.all_gather(own, "dp", axis=axis, tiled=True)


def scatter_dp(array, axis, send_type):
    if lax.axis_size("dp") == 2:
        size = array.shape[axis] // 2
        mine = lax.axis_index("dp")
        kept = lax.dynamic_slice_in_dim(array, mine * size, size, axis)
        sent = lax.dynamic_slice_in_dim(array, (1 - mine) * size, size, axis)
        return kept + over_dp(sent.astype(send_type)).astype(F32)
    return lax.psum_scatter(array, "dp", scatter_dimension=axis, tiled=True)


def flip_one(index):
    return index + 1 - 2 * (index % 2)


def flip_two(index):
    return index + 2 - 4 * ((index // 2) % 2)


def at_slot(slot, rank):
    rank = flip_one(rank) if slot % 2 else rank
    return flip_two(rank) if slot // 2 else rank


class Copies:
    def __init__(self, send, receive):
        self.send, self.receive, self.used, self.sends = (send, receive, 0, [])

    def remote(self, source, target, device, starts=True):
        at = self.used
        self.used += 1
        copy = pltpu.make_async_remote_copy(
            src_ref=source,
            dst_ref=target,
            send_sem=self.send.at[at],
            recv_sem=self.receive.at[at],
            device_id=device,
            device_id_type=pl.DeviceIdType.MESH,
        )
        if starts:
            copy.start()
        self.sends.append(copy)
        return copy

    def swapped(self, source, target, is_swapped, device):
        at = self.used
        self.used += 1
        far = pltpu.make_async_remote_copy(
            src_ref=source,
            dst_ref=target,
            send_sem=self.send.at[at],
            recv_sem=self.receive.at[at],
            device_id=device,
            device_id_type=pl.DeviceIdType.MESH,
        )
        near = pltpu.make_async_copy(source, target, self.receive.at[at])

        def start():
            @pl.when(is_swapped)
            def _():
                far.start()

            @pl.when(jnp.logical_not(is_swapped))
            def _():
                near.start()

        def wait():
            @pl.when(is_swapped)
            def _():
                far.wait_send()
                far.wait_recv()

            @pl.when(jnp.logical_not(is_swapped))
            def _():
                near.wait()

        return (start, wait)

    def homeward(self, source, target, device):
        at = self.used
        self.used += 1
        return pltpu.make_async_remote_copy(
            src_ref=source,
            dst_ref=target,
            send_sem=self.send.at[at],
            recv_sem=self.receive.at[at],
            device_id=device,
            device_id_type=pl.DeviceIdType.MESH,
        )

    def local(self, source, target):
        at = self.used
        self.used += 1
        copy = pltpu.make_async_copy(source, target, self.receive.at[at])
        copy.start()
        return copy

    def sent(self, copy):
        copy.wait_send()
        self.sends = [other for other in self.sends if other is not copy]

    def finish(self):
        for copy in self.sends:
            copy.wait_send()


class Place:
    def __init__(self, dp_size):
        group, self.dp, home = (lax.axis_index("group"), lax.axis_index("dp"), lax.axis_index("mp"))
        core, upper = (group % 2, home // 2)
        self.is_swapped = core != upper
        self.home = home
        self.rank = jnp.where(self.is_swapped, flip_two(home), home)
        self.swap = {"group": flip_one(group), "mp": flip_two(home)}
        self.core = {"group": flip_one(group)}
        self.across = {"group": flip_two(group)}
        self.half = core
        self.next = {"mp": flip_one(home)}
        self.dp_peers = [{"dp": (self.dp + step) % dp_size} for step in range(1, dp_size)]

    def meet(self, others=()):
        barrier = pltpu.get_barrier_semaphore()
        peers = [self.core, self.next, self.swap] + self.dp_peers + list(others)
        for peer in peers:
            pl.semaphore_signal(
                barrier, inc=1, device_id=peer, device_id_type=pl.DeviceIdType.MESH
            )
        pl.semaphore_wait(barrier, len(peers))


def column_of(row):
    size = row.shape[1]
    down = lax.broadcasted_iota(jnp.int32, (size, size), 0)
    along = lax.broadcasted_iota(jnp.int32, (size, size), 1)
    return jnp.sum(jnp.where(down == along, row, 0.0), 1, keepdims=True)


def rotate(rows, cosine, sine):
    half = ROT // 2
    one, two = (rows[:half], rows[half:ROT])
    return jnp.concatenate(
        [one * cosine - two * sine, two * cosine + one * sine, rows[ROT:]], 0
    )


def first_kernel(
    dp_size, x_ref, c_ref, entry_ref, exit_ref, shared_ref, ids_ref, vector_ref, cos_ref, sin_ref,
    xg_out, cg_out, a1_out, dh_out, up_out, small_out, kvw_out, ot_out,
    dqt, pair_grad, norm_ref, ub_grad, big_own, y_land,
    xg, cg, a1, dh, up_w, small, kvw, ot, h, down_w, small_ref, up_ref, down_ref, pair_ref, vector_other, qb_ref, kvb_ref, big_land, a2,
    kvt, qt, dot_rows, kt, vt, k, v, dk, dv, s_ref, d_ref, l_ref, idr, tmp,
    y_from, y_got, y_keep, g_send, g_recv, send, receive,
):
    place = Place(dp_size)
    rank, dp = (place.rank, place.dp)
    copies = Copies(send, receive)
    local = x_ref.shape[0]
    length = 4 * local
    columns = entry_ref.shape[1]
    shares = columns != D
    query_width = small.shape[0] // 2
    wide = up_w.shape[0]
    heads = query_width // HS
    gathers_pair = shared_ref.shape[0] != D
    kept = (xg, cg, a1, dh, up_w, small, kvw, ot)
    kept_outs = (xg_out, cg_out, a1_out, dh_out, up_out, small_out, kvw_out, ot_out)
    place.meet()
    vector_core = copies.remote(vector_ref, vector_other, place.core)

    def swapped(source, target):
        return copies.swapped(source, target, place.is_swapped, place.swap)

    def dp_part(ref, start, size):
        return ref.at[pl.ds(start, size), pl.ds(pl.multiple_of(dp * columns, 128), columns)]

    step = local // 2
    spans = [pl.ds(at * step, step) for at in range(2)]
    x_swaps = [swapped(x_ref.at[s], xg.at[0, s]) for s in spans]
    c_swaps = [swapped(c_ref.at[s], cg.at[0, s]) for s in spans]
    ids_swap = swapped(ids_ref, idr.at[:, pl.ds(0, local)])
    small_swaps, big_swaps, big_parts = ([], [], [])
    if shares:
        small_part = dp_part(small, 0, 2 * query_width)
        small_swaps = [swapped(small_ref, small_part)]
        for at in range(0, wide, TILE):
            for source, target in ((up_ref, up_w), (down_ref, down_w)):
                big_parts.append(dp_part(target, at, TILE))
                big_swaps.append(swapped(source.at[pl.ds(at, TILE)], big_parts[-1]))
    first = [ids_swap]
    if gathers_pair:
        pair_swap = swapped(pair_ref, kvw.at[dp, place.home])
        first.append(pair_swap)
    queue = iter([start for start, _ in x_swaps + small_swaps + c_swaps])

    def start_next():
        start = next(queue, None)
        if start is not None:
            start()

    start_next()
    start_next()
    if gathers_pair:
        pair_ref[...] = shared_ref[...].astype(BF)
    for start, _ in first:
        start()
    if shares:
        small_ref[:query_width, :] = entry_ref[:query_width, :].astype(BF)
        small_ref[query_width:, :] = exit_ref[:query_width, :].astype(BF)
        up_ref[...] = entry_ref[query_width:, :].astype(BF)
        down_ref[...] = exit_ref[query_width:, :].astype(BF)
    else:
        small[:query_width, :] = entry_ref[:query_width, :]
        small[query_width:, :] = exit_ref[:query_width, :]
        up_w[...] = entry_ref[query_width:, :]
        down_w[...] = exit_ref[query_width:, :]
    vector_core.wait_recv()

    def role_vector(start, size):
        span = slice(start, start + size)
        return jnp.where(place.is_swapped, vector_other[:, span], vector_ref[:, span])

    for at in range(4):
        norm_ref[at : at + 1, :] = role_vector(at * D, D)
    kvb_ref[...] = column_of(role_vector(6 * D, 2 * HS))
    part = query_width + wide
    tail = 6 * D + 2 * HS
    in_bias = role_vector(tail, part)
    for at in range(1, 4):
        in_bias = jnp.where(rank == at, role_vector(tail + at * part, part), in_bias)
    qb_ref[...] = column_of(in_bias[:, :query_width])
    norm_ref[4:5, :] = in_bias[:, query_width:]

    def normalise(slot):
        def body(at, carry):
            span = pl.ds(pl.multiple_of(at * 128, 128), 128)
            wide = xg[slot, span, :].astype(F32)
            centered = wide - jnp.mean(wide, -1, keepdims=True)
            normal = centered * lax.rsqrt(
                jnp.mean(centered * centered, -1, keepdims=True) + NORM_EPS
            )
            a1[slot, span, :] = (normal * norm_ref[0:1, :] + norm_ref[1:2, :]).astype(BF)
            a2[slot, span, :] = (normal * norm_ref[2:3, :] + norm_ref[3:4, :]).astype(BF)
            return carry

        lax.fori_loop(0, local // 128, body, 0)

    def lanes(ref, slot):
        return ref.at[:, pl.ds(slot * local, local)]

    x_next, x_core, x_far = ([], [], [])
    for span, (_, wait) in zip(spans, x_swaps):
        wait()
        start_next()
        x_next.append(copies.remote(xg.at[0, span], xg.at[1, span], place.next))
        x_core.append(copies.remote(xg.at[0, span], xg.at[2, span], place.core))
    small_dp = []
    for _, wait in small_swaps:
        wait()
        start_next()
        small_dp += [copies.remote(small_part, small_part, peer) for peer in place.dp_peers]
    ids_swap[1]()
    ids_next = copies.remote(lanes(idr, 0), lanes(idr, 1), place.next)
    ids_core = copies.remote(lanes(idr, 0), lanes(idr, 2), place.core)
    if gathers_pair:
        pair_swap[1]()
        own_pair = kvw.at[dp, rank]
        pair_next = copies.remote(own_pair, own_pair, place.next)
        pair_core = copies.remote(own_pair, own_pair, place.core)
    c_next, c_core, c_far, big_dp = ([], [], [], [])
    for span in spans:
        c_next.append(copies.remote(cg.at[0, span], cg.at[1, span], place.next, starts=False))
        c_core.append(copies.remote(cg.at[0, span], cg.at[2, span], place.core, starts=False))
        c_far.append(copies.remote(cg.at[1, span], cg.at[3, span], place.core, starts=False))
    for part in big_parts:
        big_dp.append([copies.remote(part, part, peer, starts=False) for peer in place.dp_peers])

    def c_sends(at):
        c_next[at].start()
        c_core[at].start()

    def c_arrives(at):
        @pl.when(place.is_swapped)
        def _():
            c_swaps[at][1]()
            c_sends(at)

        if at < len(big_swaps):
            big_swaps[at][0]()

    def c_passes(at):
        c_next[at].wait_recv()
        c_far[at].start()

    def big_arrives(at):
        big_swaps[at][1]()
        if at + 2 < len(big_swaps):
            big_swaps[at + 2][0]()
        for copy in big_dp[at]:
            copy.start()

    normalise(0)
    for span, copy in zip(spans, x_next):
        copy.wait_recv()
        x_far.append(copies.remote(xg.at[1, span], xg.at[3, span], place.core))
    for at in range(2):

        @pl.when(jnp.logical_not(place.is_swapped))
        def _():
            c_swaps[at][1]()
            c_sends(at)

    ids_next.wait_recv()
    ids_far = copies.remote(lanes(idr, 1), lanes(idr, 3), place.core)
    if gathers_pair:
        pair_next.wait_recv()
        next_pair = kvw.at[dp, flip_one(rank)]
        pair_far = copies.remote(next_pair, next_pair, place.core)
        pair_core.wait_recv()
        pair_far.wait_recv()
        pair_dp = [copies.remote(kvw.at[dp], kvw.at[dp], peer) for peer in place.dp_peers]
    events = [((0, 6), c_passes, 0), ((1, 5), c_passes, 1)]
    if shares:
        places = ((0, 5), (0, 7), (1, 6), (2, 3))
        events += [(place, big_arrives, at) for at, place in enumerate(places)]
    for copy in x_core:
        copy.wait_recv()
    normalise(2)
    normalise(1)
    for copy in x_far:
        copy.wait_recv()
    normalise(3)
    for copy in small_dp:
        copy.wait_recv()
    if gathers_pair:
        for copy in pair_dp:
            copy.wait_recv()
        kvt[...] = kvw[...].reshape(D, 2 * HS).T
    else:
        kvw[...] = shared_ref[...]
        kvt[...] = shared_ref[...].T
    c_arrives(0)
    for slot in range(4):
        block = at_slot(slot, rank)
        table = pl.ds(pl.multiple_of(block * local, local), local)
        cosine, sine = (cos_ref[:, table], sin_ref[:, table])
        tokens = pl.ds(slot * local, local)
        queries = dot_nt(small[0:query_width, :], a1[slot]) + qb_ref[...]
        for head in range(heads):
            turned = rotate(queries[head * HS : (head + 1) * HS], cosine, sine).astype(BF)
            qt[head * HS : (head + 1) * HS, tokens] = turned * jnp.asarray(1.0 / math.sqrt(HS), BF)
        pairs = dot_nt(kvt[...], a1[slot]) + kvb_ref[...]
        turned = rotate(pairs[:HS], cosine, sine).astype(BF)
        kt[:, tokens] = turned
        k[tokens, :] = turned.T
        value = pairs[HS:].astype(BF)
        vt[:, tokens] = value
        v[tokens, :] = value.T
    c_arrives(1)
    for copy in (ids_core, ids_far):
        copy.wait_recv()
    ids = idr[...].astype(F32)
    first_end = jnp.sum(jnp.where(ids < 0.5, 1.0, 0.0), 1, keepdims=True)
    second_end = jnp.sum(jnp.where(ids < 1.5, 1.0, 0.0), 1, keepdims=True)

    def document(position):
        position = position.astype(F32)
        return jnp.where(position < first_end, 0.0, jnp.where(position < second_end, 1.0, 2.0))

    tiles = length // TILE
    per = tiles // 4

    def tile_at(tile):
        return pl.multiple_of(at_slot(tile // per, rank) * local + (tile % per) * TILE, TILE)

    def masked(scores, key, query):
        edge = key == 0 or query == tiles - 1
        allowed = None
        if key == query:
            down = lax.broadcasted_iota(jnp.int32, (TILE, TILE), 0)
            allowed = down <= lax.broadcasted_iota(jnp.int32, (TILE, TILE), 1)
        if edge:
            down = document(lax.broadcasted_iota(jnp.int32, (TILE, 1), 0) + key * TILE)
            along = document(lax.broadcasted_iota(jnp.int32, (1, TILE), 1) + query * TILE)
            same = down == along
            allowed = same if allowed is None else allowed & same
        return scores if allowed is None else jnp.where(allowed, scores, -1e9)

    def hooks(head, query, todo):
        for (at_head, at_query), event, at in todo:
            if query == at_query:

                @pl.when(head == at_head)
                def _():
                    event(at)

    def forward_head(head, carry):
        own = pl.ds(pl.multiple_of(head * HS, HS), HS)
        for query in range(tiles):
            hooks(head, query, events)
            at_q = pl.ds(tile_at(query), TILE)
            q = qt[own, at_q]
            highest = jnp.full((1, TILE), -jnp.inf, F32)
            for key in range(query + 1):
                scores = masked(dot(k[pl.ds(tile_at(key), TILE), :], q), key, query)
                s_ref[pl.ds(key * TILE, TILE), :] = scores
                highest = jnp.maximum(highest, jnp.max(scores, 0, keepdims=True))
            total = jnp.zeros((1, TILE), F32)
            for key in range(query + 1):
                exponent = jnp.exp(s_ref[pl.ds(key * TILE, TILE), :] - highest)
                s_ref[pl.ds(key * TILE, TILE), :] = exponent
                total = total + jnp.sum(exponent, 0, keepdims=True)
            inverse = 1.0 / total
            mixed = jnp.zeros((HS, TILE), F32)
            for key in range(query + 1):
                softmax = (s_ref[pl.ds(key * TILE, TILE), :] * inverse).astype(BF)
                mixed = mixed + dot(vt[:, pl.ds(tile_at(key), TILE)], softmax)
            ot[own, at_q] = mixed.astype(BF)
            l_ref[head, :, at_q] = jnp.broadcast_to(highest + jnp.log(total), (8, TILE))
        return carry

    lax.fori_loop(0, heads, forward_head, 0)
    for copy in c_core + c_far:
        copy.wait_recv()
    ub_grad[...] = jnp.zeros_like(ub_grad)

    def attention_grad(slot, carry):
        tokens = pl.ds(pl.multiple_of(slot * local, local), local)
        dot_rows[:, tokens] = dot_nt(small[query_width:, :], cg[slot]).astype(BF)
        return carry

    lax.fori_loop(0, 4, attention_grad, 0)
    other = pl.ds(pl.multiple_of((1 - dp) * columns, 128), columns) if shares else None
    own_part = pl.ds(pl.multiple_of(dp * columns, 128), columns) if shares else None
    sums, homes = ({}, {})

    def sum_arrives(at):
        span = pl.ds(at * TILE, TILE)
        sums[at].wait_recv()
        sums[at].wait_send()
        total = big_own[span, :] + g_recv[span, :].astype(F32)
        big_own[span, :] = total

        @pl.when(place.is_swapped)
        def _():
            g_send[span, :] = total.astype(BF)
            homes[at].start()

    pieces = wide // TILE
    for piece in range(pieces):
        units = slice(piece * TILE, (piece + 1) * TILE)
        if shares:
            for copy in big_dp[2 * piece] + big_dp[2 * piece + 1]:
                copy.wait_recv()

        def perceptron(slot, carry):
            pre = dot_nt(a2[slot], up_w[units, :]) + norm_ref[4:5, units]
            below = 0.5 * (1.0 + lax.erf(pre * math.sqrt(0.5)))
            h[slot, :, units] = (pre * below).astype(BF)
            density = jnp.exp(-0.5 * pre * pre) * (1.0 / math.sqrt(2.0 * math.pi))
            grad = dot_nt(cg[slot], down_w[units, :]) * (below + pre * density)
            grad = grad.astype(BF)
            dh[slot, :, units] = grad
            ub_grad[0:1, units] += jnp.sum(grad.astype(F32), 0, keepdims=True)
            return carry

        lax.fori_loop(0, 4, perceptron, 0)
        if piece == 0:
            for at in range(4, len(big_swaps)):
                big_arrives(at)
        if shares and piece >= 2:
            sum_arrives(piece - 2)
            sum_arrives(pieces + piece - 2)
        for at, left, right in ((piece, dh, a2), (pieces + piece, h, cg)):
            span = pl.ds(at * TILE, TILE)
            total = 0.0
            for slot in range(4):
                total = total + dot_tn(left[slot, :, units], right[slot])
            if shares:
                tmp[...] = total
                g_send[span, :] = tmp[:, other].astype(BF)
                sums[at] = copies.remote(g_send.at[span], g_recv.at[span], place.dp_peers[0])
                big_own[span, :] = tmp[:, own_part]
                homes[at] = copies.homeward(g_send.at[span], big_land.at[span], place.swap)
            else:
                big_own[span, :] = total
    copies.sends = [
        copy for copy in copies.sends if not any(copy is other for other in sums.values())
    ]
    leaving = [copies.local(held, out) for held, out in zip(kept, kept_outs)]

    def branches(slot):
        tokens = pl.ds(slot * local, local)
        return dot(h[slot], down_w[...]) + dot_tn(ot[:, tokens], small[query_width:, :])

    y_cores = {}
    for slot in (3, 2):
        at = slot - 2
        a2[at] = branches(slot).astype(BF)
        y_cores[at] = copies.remote(a2.at[at], y_from.at[at], place.core)
    if shares:
        sum_arrives(pieces - 2)
        sum_arrives(2 * pieces - 2)
    branch = branches(1)
    y_cores[1].wait_recv()
    a2[2] = (branch + y_from[1].astype(F32)).astype(BF)
    y_nexts = [
        copies.remote(a2.at[2, span], y_got.at[span], place.next)
        for at, span in enumerate(spans)
    ]
    branch = branches(0)
    y_cores[0].wait_recv()
    y_keep[...] = branch + y_from[0].astype(F32)
    y_homes = [swapped(a2.at[3, span], y_land.at[span]) for span in spans]

    def y_arrives(at):
        y_nexts[at].wait_recv()
        span = spans[at]
        a2[3, span, :] = (y_keep[span, :] + y_got[span, :].astype(F32)).astype(BF)
        y_homes[at][0]()

    later = [((0, 7), y_arrives, 0), ((1, 7), y_arrives, 1)]
    if shares:
        later += [((0, 5), sum_arrives, at) for at in (pieces - 1, 2 * pieces - 1)]

    dk[...] = jnp.zeros_like(dk)
    dv[...] = jnp.zeros_like(dv)

    def backward_head(head, carry):
        own = pl.ds(pl.multiple_of(head * HS, HS), HS)
        for query in range(tiles):
            hooks(head, query, later)
            at_q = pl.ds(tile_at(query), TILE)
            q, do = (qt[own, at_q], dot_rows[own, at_q])
            scaled = do * jnp.asarray(1.0 / math.sqrt(HS), BF)
            log_total = l_ref[head, 0:1, at_q]
            inner = jnp.zeros((1, TILE), F32)
            for key in range(query + 1):
                at_k = pl.ds(tile_at(key), TILE)
                at_s = pl.ds(key * TILE, TILE)
                softmax = jnp.exp(masked(dot(k[at_k, :], q), key, query) - log_total)
                prob_grad = dot(v[at_k, :], scaled)
                s_ref[at_s, :] = softmax
                d_ref[at_s, :] = prob_grad
                inner = inner + jnp.sum(softmax * prob_grad, 0, keepdims=True)
            query_grad = jnp.zeros((HS, TILE), F32)
            for key in range(query + 1):
                at_k = pl.ds(tile_at(key), TILE)
                at_s = pl.ds(key * TILE, TILE)
                softmax = s_ref[at_s, :]
                score_grad = (softmax * (d_ref[at_s, :] - inner)).astype(BF)
                query_grad = query_grad + dot(kt[:, at_k], score_grad)
                dk[at_k, :] += dot_nt(score_grad, q)
                dv[at_k, :] += dot_nt(softmax.astype(BF), do)
            table = pl.ds(query * TILE, TILE)
            dqt[own, at_q] = rotate(query_grad, cos_ref[:, table], -sin_ref[:, table]).astype(BF)
        return carry

    lax.fori_loop(0, heads, backward_head, 0)
    for slot in range(4):
        block = at_slot(slot, rank)
        table = pl.ds(pl.multiple_of(block * local, local), local)
        tokens = pl.ds(slot * local, local)
        key_grad = dk[tokens, :].T * math.sqrt(HS)
        pair_grad[0:HS, tokens] = rotate(key_grad, cos_ref[:, table], -sin_ref[:, table])
        pair_grad[HS:, tokens] = dv[tokens, :].T

    for _, wait in y_homes:
        wait()
    for copy in leaving:
        copy.wait()

    @pl.when(place.is_swapped)
    def _():
        for at, copy in homes.items():
            copy.wait_send()
            copy.wait_recv()
            span = pl.ds(at * TILE, TILE)
            big_own[span, :] = big_land[span, :].astype(F32)

    copies.finish()


def first_pass(dp_size, x, c, entry, leave, shared, ids, vector, cosine, sine):
    local = x.shape[0]
    length = 4 * local
    part, columns = entry.shape
    query_width = HEADS * HS // 4
    width = 2 * query_width
    wide = part - query_width
    heads = query_width // HS
    gathers_pair = shared.shape[0] != D
    shares = columns != D
    held = (2 * wide if shares else 16, columns)
    tokens = ((4, local, D), BF)
    hidden = ((4, local, wide), BF)
    outs = [
        tokens,
        tokens,
        tokens,
        hidden,
        ((wide, D), BF),
        ((width, D), BF),
        ((dp_size, 4, shared.shape[0], 2 * HS) if gathers_pair else (D, 2 * HS), BF),
        ((query_width, length), BF),
        ((query_width, length), BF),
        ((2 * HS, length), F32),
        ((8, D), F32),
        ((8, wide), F32),
        ((2 * wide, columns), F32),
        ((local, D), BF),
    ]
    vmem = pl.BlockSpec(memory_space=pltpu.VMEM)
    copies = 64 + 12 * dp_size
    work = query_width * length * length
    return pl.pallas_call(
        functools.partial(first_kernel, dp_size),
        out_shape=[jax.ShapeDtypeStruct(shape, kind) for shape, kind in outs],
        in_specs=[vmem] * 9,
        out_specs=[pl.BlockSpec(memory_space=pl.ANY)] * 8 + [vmem] * (len(outs) - 8),
        scratch_shapes=[pltpu.VMEM(shape, kind) for shape, kind in outs[:8]]
        + [
            pltpu.VMEM(hidden[0], BF),
            pltpu.VMEM((wide, D), BF),
            pltpu.VMEM((width, columns), BF),
            pltpu.VMEM((wide, columns), BF),
            pltpu.VMEM((wide, columns), BF),
            pltpu.VMEM((shared.shape[0] if gathers_pair else 16, 2 * HS), BF),
            pltpu.VMEM(vector.shape, F32),
            pltpu.VMEM((query_width, 1), F32),
            pltpu.VMEM((2 * HS, 1), F32),
            pltpu.VMEM(held, BF),
            pltpu.VMEM((4, local, D), BF),
            pltpu.VMEM((2 * HS, D), BF),
            pltpu.VMEM((query_width, length), BF),
            pltpu.VMEM((query_width, length), BF),
            pltpu.VMEM((HS, length), BF),
            pltpu.VMEM((HS, length), BF),
            pltpu.VMEM((length, HS), BF),
            pltpu.VMEM((length, HS), BF),
            pltpu.VMEM((length, HS), F32),
            pltpu.VMEM((length, HS), F32),
            pltpu.VMEM((length, TILE), F32),
            pltpu.VMEM((length, TILE), F32),
            pltpu.VMEM((heads, 8, length), F32),
            pltpu.VMEM((1, length), jnp.int32),
            pltpu.VMEM((TILE, D), F32),
            pltpu.VMEM((2, local, D), BF),
            pltpu.VMEM((local, D), BF),
            pltpu.VMEM((local, D), F32),
            pltpu.VMEM(held, BF),
            pltpu.VMEM(held, BF),
            pltpu.SemaphoreType.DMA((copies,)),
            pltpu.SemaphoreType.DMA((copies,)),
        ],
        compiler_params=pltpu.CompilerParams(
            collective_id=0, has_side_effects=True, vmem_limit_bytes=59 << 20
        ),
        cost_estimate=pl.CostEstimate(
            flops=60 * work, bytes_accessed=30 << 20, transcendentals=work // HS
        ),
        name="gather_attend",
    )(x, c, entry, leave, shared, ids, vector, cosine, sine)


def column_sum(rows):
    return jnp.sum(rows, 0, keepdims=True)


def row_of(column):
    size = column.shape[0]
    down = lax.broadcasted_iota(jnp.int32, (size, size), 0)
    along = lax.broadcasted_iota(jnp.int32, (size, size), 1)
    return column_sum(jnp.where(down == along, column, 0.0))


def gap_of(grad, weight, first, second, anchor, rate, decay):
    return anchor - adamw_update(weight, first, second, grad, rate, decay)[2]


def second_kernel(dp_size, sums_pair, shares, *refs):
    refs = iter(refs)

    def take(number):
        return [next(refs) for _ in range(number)]

    late = take(5 + (8 if shares else 0))
    xg, dh, up_w, small, kvw, ot, dqt, pair_grad, norm_ref, ub_grad = take(10)
    if shares:
        shared, vector = (take(4) for _ in range(2))
    grad_ref, small_own, vector_row, shared_home, pair_parts = take(5)
    if shares:
        entry_sum, exit_sum, shared_sum, vector_sum = take(4)
    u_land, small_land, vector_home, stats, v_next, v_core, v_dp, s_core, s_next, s_dp = take(10)
    u_core, u_from, u_next, u_got, u_keep, u_home, p_from, p_next, p_got, full, g_send, g_recv = take(12)
    if shares:
        wide_buffers = [take(4), take(4)]
        small_buffers = [take(4), take(4)]
        shared_buffers, vector_buffers = (take(4), take(4))
    held = take(len(late))
    x_ref, c_ref, cg, a1, big_g = held[:5]
    entry, leave = (held[5:9], held[9:])
    send, receive = take(2)

    place = Place(dp_size)
    copies = Copies(send, receive)
    local = xg.shape[1]
    wide = dh.shape[2]
    columns = small_own.shape[1]
    query_width = ot.shape[0]
    place.meet([place.across])
    loads = [copies.local(source, target) for source, target in zip(late, held)]
    pair_core = copies.remote(pair_grad.at[:, pl.ds(2 * local, 2 * local)], p_from, place.core)
    stats[...] = jnp.zeros_like(stats)

    def normal_of(slot):
        inputs = xg[slot].astype(F32)
        centered = inputs - jnp.mean(inputs, -1, keepdims=True)
        return centered * lax.rsqrt(jnp.mean(centered * centered, -1, keepdims=True) + NORM_EPS)

    def joined_of(slot):
        tokens = pl.ds(slot * local, local)
        first = dot_tn(dqt[:, tokens], small[:query_width, :])
        second = dot(dh[slot], up_w[...])
        normal = normal_of(slot)
        stats[0:1, :D] += column_sum(first * normal)
        stats[1:2, :D] += column_sum(first)
        stats[2:3, :D] += column_sum(second * normal)
        stats[3:4, :D] += column_sum(second)
        return first * norm_ref[0:1, :] + second * norm_ref[2:3, :]

    def sent_home(source, target):
        return copies.swapped(source, target, place.is_swapped, place.swap)

    class GroupSum:
        def __init__(self, olds, grads, total, start, grad_start, size, buffers):
            self.olds, self.grads, self.total, self.buffers = (olds, grads, total, buffers)
            self.own, self.other = (
                pl.ds(pl.multiple_of(start + at * size, 8), size) for at in (place.half, 1 - place.half)
            )
            self.grad_own, self.grad_other = (
                pl.ds(pl.multiple_of(grad_start + at * size, 8), size)
                for at in (place.half, 1 - place.half)
            )

        def gap(self, span, grad_span):
            olds = (ref[span, :] for ref in self.olds)
            return gap_of(self.grads[grad_span, :], *olds, MATRIX_RATE, MATRIX_DECAY)

        def to_core(self):
            sent, got = self.buffers[:2]
            sent[...] = self.gap(self.other, self.grad_other)
            self.copy = copies.remote(sent, got, place.core)
            self.total[self.own, :] = self.gap(self.own, self.grad_own)

        def to_chip(self):
            self.copy.wait_recv()
            low, far = self.buffers[2:]
            low[...] = (self.total[self.own, :] + self.buffers[1][...]).astype(BF)
            self.copy = copies.remote(low, far, place.across)

        def back(self):
            self.copy.wait_recv()
            low, far = self.buffers[2:]
            self.total[self.own, :] = low[...].astype(F32) + far[...].astype(F32)
            part = self.total.at[self.own]
            self.copy = copies.remote(part, part, place.core)

    step = local // 2
    spans = [pl.ds(at * step, step) for at in range(2)]
    u_cores = {}
    for slot in (3, 2):
        at = slot - 2
        u_core[at] = joined_of(slot).astype(BF)
        u_cores[at] = copies.remote(u_core.at[at], u_from.at[at], place.core)
    pair_core.wait_recv()
    p_next[...] = pair_grad[:, local : 2 * local] + p_from[:, local:]
    pair_next = copies.remote(p_next, p_got, place.next)
    joined = joined_of(1)
    u_cores[1].wait_recv()
    u_next[...] = (joined + u_from[1].astype(F32)).astype(BF)
    u_nexts = [
        copies.remote(u_next.at[span], u_got.at[span], place.next, starts=at == 0)
        for at, span in enumerate(spans)
    ]
    wide_sums, small_sums = ([], [])
    if shares:
        half = wide // 2
        for copy in loads[4:]:
            copy.wait()
        for olds, start, total, buffers in (
            (entry, 0, entry_sum, wide_buffers[0]),
            (leave, wide, exit_sum, wide_buffers[1]),
        ):
            wide_sums.append(GroupSum(olds, big_g, total, query_width, start, half, buffers))
            wide_sums[-1].to_core()

    if not shares:
        loads[4].wait()
    loads[2].wait()
    loads[3].wait()
    turned = 0.0
    turned_out = 0.0
    for slot in range(4):
        tokens = pl.ds(slot * local, local)
        turned = turned + dot(dqt[:, tokens], a1[slot])
        turned_out = turned_out + dot(ot[:, tokens], cg[slot])
    if shares:
        full[:query_width, :] = turned
        full[query_width:, :] = turned_out
        other = pl.ds(pl.multiple_of((1 - place.dp) * columns, 128), columns)
        g_send[...] = full[:, other].astype(BF)
        small_sum = copies.remote(g_send, g_recv, place.dp_peers[0])
        small_home = copies.homeward(g_send, small_land, place.swap)
        small_own[...] = full[:, pl.ds(pl.multiple_of(place.dp * columns, 128), columns)]
        for part in wide_sums:
            part.to_chip()
    else:
        small_own[:query_width, :] = turned
        small_own[query_width:, :] = turned_out

    joined = joined_of(0)
    u_cores[0].wait_recv()
    pair_next.wait_recv()
    pair_sum = (pair_grad[:, :local] + p_from[:, :local] + p_got[...]).astype(BF)
    through_pair = dot_nt(pair_sum.T, kvw[...])
    u_keep[...] = joined + u_from[0].astype(F32) + through_pair * norm_ref[0:1, :]
    u_homes = [sent_home(u_home.at[span], u_land.at[span]) for span in spans]

    def u_arrives(at):
        u_nexts[at].wait_recv()
        if at == 0:
            u_nexts[1].start()
        span = spans[at]
        u_home[span, :] = (u_keep[span, :] + u_got[span, :].astype(F32)).astype(BF)
        u_homes[at][0]()

    stats[0:1, :D] += column_sum(through_pair * normal_of(0))
    stats[1:2, :D] += column_sum(through_pair)
    stats[4:5, :D] = column_sum(cg[0].astype(F32))
    stats[5:6, : 2 * HS] = row_of(jnp.sum(pair_sum.astype(F32), 1, keepdims=True))
    tail = pl.ds(8 + place.rank, 1)
    stats[tail, :query_width] = row_of(jnp.sum(dqt[...].astype(F32), 1, keepdims=True))
    stats[tail, query_width : query_width + wide] = ub_grad[0:1, :]
    vector_core = copies.remote(stats, v_core, place.core)
    pair_parts[...] = dot(pair_sum, a1[0]).T.reshape(pair_parts.shape)
    if sums_pair:
        shared_core = copies.remote(pair_parts, s_core, place.core)
    u_arrives(0)
    if shares:
        small_sum.wait_recv()
        copies.sent(small_sum)
        total = small_own[...] + g_recv[...].astype(F32)
        small_own[...] = total

        @pl.when(place.is_swapped)
        def _():
            g_send[...] = total.astype(BF)
            small_home.start()

    vector_core.wait_recv()
    copies.sent(vector_core)
    stats[...] = stats[...] + v_core[...]
    vector_next = copies.remote(stats, v_next, place.next)
    if sums_pair:
        shared_core.wait_recv()
        copies.sent(shared_core)
        pair_parts[...] = pair_parts[...] + s_core[...]
        shared_next = [
            copies.remote(pair_parts.at[at * 4 + flip_one(place.rank)], s_next.at[at], place.next)
            for at in range(dp_size)
        ]
    for part in wide_sums:
        part.back()
    u_arrives(1)
    vector_next.wait_recv()
    copies.sent(vector_next)
    stats[...] = stats[...] + v_next[...]
    vector_dp = [
        copies.remote(stats, v_dp.at[at], peer) for at, peer in enumerate(place.dp_peers)
    ]
    if sums_pair:
        for at, copy in enumerate(shared_next):
            copy.wait_recv()
            s_next[at] = s_next[at] + pair_parts[at * 4 + place.rank]
        shared_dp = [
            copies.remote(s_next.at[(place.dp + at + 1) % dp_size], s_dp.at[at], peer)
            for at, peer in enumerate(place.dp_peers)
        ]
    for copy in vector_dp:
        copy.wait_recv()
        copies.sent(copy)
    total = stats[...]
    for at in range(dp_size - 1):
        total = total + v_dp[at]
    stats[...] = total
    late_homes = [sent_home(stats, vector_home)]
    if sums_pair:
        for copy in shared_dp:
            copy.wait_recv()
        total = s_next[place.dp]
        for at in range(dp_size - 1):
            total = total + s_dp[at]
        s_core[0] = total
        late_homes.append(sent_home(s_core.at[0], shared_home))
    for start, _ in late_homes:
        start()

    if shares:

        @pl.when(place.is_swapped)
        def _():
            small_home.wait_send()
            small_home.wait_recv()
            small_own[...] = small_land[...].astype(F32)

        size = query_width // 2
        for olds, start, total, buffers in (
            (entry, 0, entry_sum, small_buffers[0]),
            (leave, query_width, exit_sum, small_buffers[1]),
        ):
            small_sums.append(GroupSum(olds, small_own, total, 0, start, size, buffers))
            small_sums[-1].to_core()
        for part in small_sums:
            part.to_chip()

    loads[0].wait()
    loads[1].wait()

    def end_rows(at):
        u_homes[at][1]()
        span = spans[at]
        inputs = x_ref[span, :].astype(F32)
        centered = inputs - jnp.mean(inputs, -1, keepdims=True)
        scale = lax.rsqrt(jnp.mean(centered * centered, -1, keepdims=True) + NORM_EPS)
        normal = centered * scale
        joined = u_land[span, :].astype(F32)
        grad_ref[span, :] = c_ref[span, :].astype(F32) + scale * (
            joined
            - jnp.mean(joined, -1, keepdims=True)
            - normal * jnp.mean(joined * normal, -1, keepdims=True)
        )

    end_rows(0)
    for _, wait in late_homes:
        wait()
    part = query_width + wide
    rows = [vector_home[at : at + 1, :D] for at in (0, 1, 2, 3, 4, 4)]
    rows.append(vector_home[5:6, : 2 * HS])
    rows += [vector_home[8 + at : 9 + at, :part] for at in range(4)]
    vector_row[...] = jnp.concatenate(rows, 1)
    if shares:
        whole_sums = []
        for olds, grads, buffers, rate, decay in (
            (vector, vector_row, vector_buffers, VECTOR_RATE, 0.0),
            (shared, shared_home, shared_buffers, MATRIX_RATE, MATRIX_DECAY),
        ):
            buffers[0][...] = gap_of(grads[...], *(ref[...] for ref in olds), rate, decay)
            whole_sums.append(copies.remote(buffers[0], buffers[1], place.core))
        for at, buffers in enumerate((vector_buffers, shared_buffers)):
            whole_sums[at].wait_recv()
            buffers[2][...] = buffers[0][...] + buffers[1][...]
            whole_sums[at] = copies.remote(buffers[2], buffers[3], place.across)
    end_rows(1)
    if shares:
        for part in small_sums:
            part.back()
        for copy, buffers, total in (
            (whole_sums[0], vector_buffers, vector_sum),
            (whole_sums[1], shared_buffers, shared_sum),
        ):
            copy.wait_recv()
            total[...] = buffers[2][...] + buffers[3][...]
        for part in wide_sums + small_sums:
            part.copy.wait_recv()
    copies.finish()


def second_pass(dp_size, late, arrays, olds, piece):
    x = late[0]
    up_w, small = arrays[2:4]
    local = x.shape[0]
    width = small.shape[0]
    query_width = width // 2
    wide = up_w.shape[0]
    shares = len(olds) > 0
    columns = olds[0].shape[1] if shares else D
    sums_pair = piece % 16 == 0
    held = (width if shares else 16, columns)
    parts = (4 * dp_size, piece, 2 * HS) if sums_pair else (1, D, 2 * HS)
    own = (piece if sums_pair else 8, 2 * HS)
    vector = (1, 6 * D + 2 * HS + 4 * (query_width + wide))
    outs = [(local, D), (width, columns), vector, own, parts]
    scratch = [
        ((local, D), BF),
        (held, BF),
        ((16, 1024), F32),
        ((16, 1024), F32),
        ((16, 1024), F32),
        ((16, 1024), F32),
        ((dp_size - 1, 16, 1024), F32),
        (parts, F32),
        ((dp_size,) + own, F32),
        ((dp_size - 1,) + own, F32),
        ((2, local, D), BF),
        ((2, local, D), BF),
        ((local, D), BF),
        ((local, D), BF),
        ((local, D), F32),
        ((local, D), BF),
        ((2 * HS, 2 * local), F32),
        ((2 * HS, local), F32),
        ((2 * HS, local), F32),
        ((width, D), F32),
        (held, BF),
        (held, BF),
    ]
    if shares:
        outs += [olds[0].shape, olds[4].shape, own, vector]
        for size in (wide // 2, wide // 2, query_width // 2, query_width // 2):
            scratch += [((size, columns), kind) for kind in (F32, F32, BF, BF)]
        scratch += [(own, F32)] * 4 + [(vector, F32)] * 4
    late = list(late) + list(olds[:8])
    scratch += [(array.shape, array.dtype) for array in late]
    arrays = late + list(arrays) + list(olds[8:])
    vmem = pl.BlockSpec(memory_space=pltpu.VMEM)
    work = 4 * local * D * D
    semaphores = pltpu.SemaphoreType.DMA((72 + 3 * dp_size,))
    return pl.pallas_call(
        functools.partial(second_kernel, dp_size, sums_pair, shares),
        out_shape=[jax.ShapeDtypeStruct(shape, F32) for shape in outs],
        in_specs=[pl.BlockSpec(memory_space=pl.ANY)] * len(late) + [vmem] * (len(arrays) - len(late)),
        out_specs=[vmem] * len(outs),
        scratch_shapes=[pltpu.VMEM(shape, kind) for shape, kind in scratch] + [semaphores] * 2,
        compiler_params=pltpu.CompilerParams(
            collective_id=1, has_side_effects=True, vmem_limit_bytes=60 << 20
        ),
        cost_estimate=pl.CostEstimate(flops=8 * work, bytes_accessed=30 << 20, transcendentals=0),
        name="sum_branches",
    )(*arrays)


def third_kernel(groups, *refs):
    refs = iter(refs)

    def take(number):
        return [next(refs) for _ in range(number)]

    grads = [take(2), take(2), take(1), take(1)]
    olds = [take(6) for _ in range(4)]
    news = [take(6) for _ in range(4)]
    step = pl.program_id(0)

    def update(at, grad, rate, decay):
        weight, first, second, anchor, velocity, total = (ref[...] for ref in olds[at])
        first, second, weight = adamw_update(weight, first, second, grad, rate, decay)
        change = total / groups
        momentum = OUTER_BETA * velocity + change
        outer = anchor - OUTER_RATE * (change + OUTER_BETA * momentum)
        for ref, value in zip(news[at], (first, second, weight, change, momentum, outer)):
            ref[...] = value

    for at in range(2):
        head, rest = grads[at]
        update(at, jnp.where(step == 0, head[...], rest[...]), MATRIX_RATE, MATRIX_DECAY)

    @pl.when(step == 0)
    def _():
        update(2, grads[2][0][...], MATRIX_RATE, MATRIX_DECAY)
        update(3, grads[3][0][...], VECTOR_RATE, 0.0)


def third_pass(groups, big, small, shared_grad, vector_grad, entry, leave, shared, vector):
    rows, columns = entry[0].shape
    size = small.shape[0] // 2
    wide = rows // size - 1

    def block(index):
        return pl.BlockSpec((size, columns), index)

    def all_of(array):
        return pl.BlockSpec(array.shape, lambda i: (0, 0))

    here = block(lambda i: (i, 0))
    grad_specs = [
        block(lambda i: (0, 0)),
        block(lambda i: (jnp.maximum(i - 1, 0), 0)),
        block(lambda i: (1, 0)),
        block(lambda i: (wide + jnp.maximum(i - 1, 0), 0)),
        all_of(shared_grad),
        all_of(vector_grad),
    ]
    specs = [here] * 12 + [all_of(array) for array in shared + vector]
    out_specs = [here] * 12 + [all_of(shared[0])] * 6 + [all_of(vector[0])] * 6
    outs = [array for array in (entry[0], leave[0], shared[0], vector[0]) for _ in range(6)]
    return pl.pallas_call(
        functools.partial(third_kernel, groups),
        grid=(rows // size,),
        out_shape=[jax.ShapeDtypeStruct(array.shape, F32) for array in outs],
        in_specs=grad_specs + specs,
        out_specs=out_specs,
        compiler_params=pltpu.CompilerParams(vmem_limit_bytes=60 << 20),
        cost_estimate=pl.CostEstimate(flops=1 << 26, bytes_accessed=40 << 20, transcendentals=1 << 20),
        name="update_weights",
    )(small, big, small, big, shared_grad, vector_grad, *entry, *leave, *shared, *vector)


def shards(
    hidden_in,
    doc_ids,
    out_cotangent,
    entry_weight,
    entry_first,
    entry_second,
    entry_anchor,
    entry_velocity,
    exit_weight,
    exit_first,
    exit_second,
    exit_anchor,
    exit_velocity,
    shared_weight,
    shared_first,
    shared_second,
    shared_anchor,
    shared_velocity,
    vector_weight,
    vector_first,
    vector_second,
    vector_anchor,
    vector_velocity,
):
    batch, local_len = hidden_in.shape[:2]
    parts = lax.axis_size("mp")
    group, rank = (lax.axis_index("group"), lax.axis_index("mp"))
    is_swapped = (group % 2) != (rank // 2)
    rank = jnp.where(is_swapped, jnp.bitwise_xor(rank, 2), rank)
    length = local_len * parts
    part_width = entry_weight.shape[2]
    query_width = HEADS * HS // parts
    heads = query_width // HS

    dp_size = lax.axis_size("dp")
    groups = lax.axis_size("group")
    order = jnp.bitwise_xor(jnp.arange(parts), rank)
    piece = shared_weight.shape[1]
    shared_piece = shared_weight[0]
    if piece % 16:
        pieces = gather_square(swapped_parts(shared_piece.astype(BF)))
        pieces = jnp.take(pieces, order, axis=0)
        shared_piece = gather_dp(pieces.reshape(-1, 2 * HS), 0)
    half = ROT // 2
    frequency = 10000.0 ** (-(np.arange(half) * 2.0 / ROT))
    angles = frequency.astype(np.float32)[:, None] * np.arange(length, dtype=np.float32)[None, :]
    cosine_table = jnp.asarray(np.cos(angles.astype(np.float64)).astype(np.float32))
    sine_table = jnp.asarray(np.sin(angles.astype(np.float64)).astype(np.float32))
    entry = [array[0].T for array in (entry_weight, entry_first, entry_second)]
    entry += [array.T for array in (entry_anchor, entry_velocity)]
    leave = [array[0] for array in (exit_weight, exit_first, exit_second)]
    leave += [exit_anchor, exit_velocity]
    shared = [array[0] for array in (shared_weight, shared_first, shared_second)]
    shared += [shared_anchor, shared_velocity]
    vector = [vector_weight, vector_first, vector_second, vector_anchor[None], vector_velocity[None]]
    shares = dp_size == 2 and leave[0].shape[1] % 128 == 0 and piece % 16 == 0
    weights = [entry[0], leave[0]]
    if not shares:
        weights = [gather_dp(swapped_parts(array.astype(BF)), 1) for array in weights]
    (
        inputs, cots, attn_input, hidden_grad, up_w, small, pair_weight, attended, query_grad,
        pair_rows, norms, up_bias_rows, big_grad, branch_home,
    ) = first_pass(
        dp_size,
        hidden_in[0],
        out_cotangent[0],
        *weights,
        shared_piece,
        doc_ids,
        vector_weight,
        cosine_table,
        sine_table,
    )
    home_bias = vector_weight[0, 4 * D : 5 * D] + vector_weight[0, 5 * D : 6 * D]
    block_output = hidden_in[0].astype(F32) + branch_home.astype(F32) + home_bias
    late = (hidden_in[0], out_cotangent[0], cots, attn_input, big_grad)
    arrays = (
        inputs, hidden_grad, up_w, small, pair_weight.reshape(D, 2 * HS), attended, query_grad,
        pair_rows, norms, up_bias_rows,
    )
    olds = [array for arrays in (entry, leave, shared, vector) for array in arrays[:4]]
    input_grad, small_grad, vector_grad, shared_grad, pair_parts, *totals = second_pass(
        dp_size, late, arrays, olds if shares else [], piece
    )
    if not shares:
        big_grad, small_grad = (
            swapped_parts(scatter_dp(array, 1, F32)) for array in (big_grad, small_grad)
        )
        if piece % 16:
            grad_pieces = pair_parts.reshape(dp_size, parts, -1, 2 * HS)
            grad_pieces = jnp.take(grad_pieces, order, axis=1).swapaxes(0, 1)
            shared_grad = scatter_dp(scatter_square(grad_pieces, F32), 0, F32)
            shared_grad = swapped_parts(shared_grad.reshape(-1, 2 * HS))
        size, wide = (small_grad.shape[0] // 2, big_grad.shape[0] // 2)
        gaps = (
            gap_of(
                jnp.concatenate([small_grad[:size], big_grad[:wide]]),
                *entry[:4], MATRIX_RATE, MATRIX_DECAY,
            ),
            gap_of(
                jnp.concatenate([small_grad[size:], big_grad[wide:]]),
                *leave[:4], MATRIX_RATE, MATRIX_DECAY,
            ),
            gap_of(shared_grad, *shared[:4], MATRIX_RATE, MATRIX_DECAY),
            gap_of(vector_grad, *vector[:4], VECTOR_RATE, 0.0),
        )
        totals = lax.psum(gaps, "group")
    updated = third_pass(
        groups, big_grad, small_grad, shared_grad, vector_grad,
        *(arrays + [total] for arrays, total in zip((entry, leave, shared, vector), totals)),
    )
    updated = list(updated)
    results = [block_output[None], input_grad[None]]
    for at in range(3):
        own = updated[6 * at : 6 * at + 6]
        if at == 0:
            own = [array.T for array in own]
        results += [array[None] for array in own[:3]] + own[3:]
    results += updated[18:21] + [array[0] for array in updated[21:24]]
    return tuple(results)


def solution(mesh):
    in_specs = (
        P(("group", "dp"), "mp", None),
        P(("group", "dp"), "mp"),
        P(("group", "dp"), "mp", None),
        P("group", "dp", "mp"),
        P("group", "dp", "mp"),
        P("group", "dp", "mp"),
        P("dp", "mp"),
        P("dp", "mp"),
        P("group", "mp", "dp"),
        P("group", "mp", "dp"),
        P("group", "mp", "dp"),
        P("mp", "dp"),
        P("mp", "dp"),
        P("group", ("dp", "mp"), None),
        P("group", ("dp", "mp"), None),
        P("group", ("dp", "mp"), None),
        P(("dp", "mp"), None),
        P(("dp", "mp"), None),
        P("group", None),
        P("group", None),
        P("group", None),
        P(),
        P(),
    )
    out_specs = (
        P(("group", "dp"), "mp", None),
        P(("group", "dp"), "mp", None),
        P("group", "dp", "mp"),
        P("group", "dp", "mp"),
        P("group", "dp", "mp"),
        P("dp", "mp"),
        P("dp", "mp"),
        P("dp", "mp"),
        P("group", "mp", "dp"),
        P("group", "mp", "dp"),
        P("group", "mp", "dp"),
        P("mp", "dp"),
        P("mp", "dp"),
        P("mp", "dp"),
        P("group", ("dp", "mp"), None),
        P("group", ("dp", "mp"), None),
        P("group", ("dp", "mp"), None),
        P(("dp", "mp"), None),
        P(("dp", "mp"), None),
        P(("dp", "mp"), None),
        P("group", None),
        P("group", None),
        P("group", None),
        P(),
        P(),
        P(),
    )
    return jax.shard_map(shards, mesh=mesh, in_specs=in_specs, out_specs=out_specs, check_vma=False)
```

time: 324 us -> 259 us (0.80)
  local copies, waits for them, and re-layouts: 41.9 us -> 3.06 us
  Pallas kernels: 275 us -> 245 us
  other arithmetic: 2.09 us -> 6.44 us
    pallas_call x2, Pallas kernels: 126 us -> 81 us  [the longest x1 64.4 us: second_pass(): pl.pallas_call(functools.partial(second_kernel, dp_size, sums_pair, share...]
    unnamed x90 -> x11, local copies, waits for them, and re-layouts: 40.6 us -> 1.78 us
    pallas_call x1, Pallas kernels: 150 us -> 164 us  [first_pass(): pl.pallas_call(functools.partial(first_kernel, dp_size), out_shape=[jax.S...]
where the time goes in v4:
time: 259 us; the launch traced here: 255 us
  Pallas kernels  245 us (95%)
  other arithmetic  6.44 us (2%)
  local copies, waits for them, and re-layouts  3.06 us (1%)
    pallas_call x1, Pallas kernels, first_pass(): pl.pallas_call(functools.partial(first_kernel, dp_size), out_shape=[jax.S...  164 us
    pallas_call x1, Pallas kernels, second_pass(): pl.pallas_call(functools.partial(second_kernel, dp_size, sums_pair, share...  64.4 us
    pallas_call x1, Pallas kernels, third_pass(): pl.pallas_call(functools.partial(third_kernel, groups), grid=(rows // siz...  16.6 us

profile of v4, /device:TPU:1, one launch (start us, length us, event | category | flops | bytes accessed | tf_op | source)
XLA Modules:
  0.0 255.1 jit_solution(124190709382788838)
XLA Ops:
  0.7 0.0 copy-start.3
  0.7 163.6 %gather_attend.1 = (bf16[4,512,768]{2,1,0:T(8,128)(2,1)}, bf16[4,512,768]{2,1,0:T(8,128)(2,1)}, bf16[4,512,768]{2,1,0:T(8,128)(2,1)}, bf16[4,512,768]{2,1,0:T(8,...) custom-call(bf16[512,768]{1,0:T(8,128)(2,1)} %bitcast.60, ...), custom_call_target="tpu_custom_call" | custom-call | flops 48318382080 | bytes 31457280 | tf_op jit(solution)/shard_map/gather_attend/pallas_call | solution.py:716
  164.3 0.0 copy-done.3
  164.3 0.6 broadcast_in_dim.41.refs_30_.refs_27_
  164.9 0.0 copy-start.4
  164.9 64.4 %sum_branches.1 = (f32[512,768]{1,0:T(8,128)}, f32[384,384]{1,0:T(8,128)}, f32[1,8576]{1,0:T(1,128)}, f32[96,128]{1,0:T(8,128)}, f32[8,96,128]{2,1,0:T(8,128)}, ...) custom-call(bf16[512,768]{1,0:T(8,128)(2,1)} %bitcast.61, ...), custom_call_target="tpu_custom_call" | custom-call | flops 9663676416 | bytes 31457280 | tf_op jit(solution)/shard_map/sum_branches/pallas_call | solution.py:1129
  229.4 0.0 copy-done.4
  229.4 0.6 broadcast_in_dim.43.refs_28_
  230.0 0.0 copy-start.1
  230.0 0.0 copy-start.2
  230.0 16.6 %update_weights.1 = (f32[960,384]{1,0:T(8,128)}, f32[960,384]{1,0:T(8,128)}, f32[960,384]{1,0:T(8,128)}, f32[960,384]{1,0:T(8,128)}, f32[960,384]{1,0:T(8,128)},...) custom-call(f32[384,384]{1,0:T(8,128)} %get-tuple-element.87.refs_0_, ...), custom_call_target="tpu_custom_call" | custom-call | flops 67108864 | bytes 41943040 | tf_op jit(solution)/shard_map/update_weights/pallas_call | solution.py:1196
  246.6 1.5 reduce.1
  248.1 1.5 reduce.2
  249.5 1.5 reduce.3
  251.0 0.7 add_reduce_fusion
  251.7 0.0 copy-done.1
  251.7 0.0 copy-done.2
  251.7 0.0 copy-start
  251.7 1.3 add_bitcast_fusion
  253.1 0.6 copy-done
  253.7 1.1 copy.52
Async XLA Ops:
  0.7 163.6 %copy-start.3 = (f32[8576]{0:T(1024)S(1)}, f32[8576]{0:T(1024)}, u32[]{:S(2)}) copy-start(f32[8576]{0:T(1024)} %param.46) | copy-start | bytes 102916
  164.9 64.4 %copy-start.4 = (f32[8576]{0:T(1024)S(1)}, f32[8576]{0:T(1024)}, u32[]{:S(2)}) copy-start(f32[8576]{0:T(1024)} %param.47) | copy-start | bytes 102916
  230.0 21.7 %copy-start.1 = (bf16[1,512,768]{2,1,0:T(8,128)(2,1)S(1)}, bf16[1,512,768]{2,1,0:T(8,128)(2,1)}, u32[]{:S(2)}) copy-start(bf16[1,512,768]{2,1,0:T(8,128)(2,1)} %param.25) | copy-start | bytes 2359300
  230.0 21.7 %copy-start.2 = (bf16[512,768]{1,0:T(8,128)(2,1)S(1)}, bf16[512,768]{1,0:T(8,128)(2,1)}, u32[]{:S(2)}) copy-start(bf16[512,768]{1,0:T(8,128)(2,1)} %get-tuple-element.72) | copy-start | bytes 2359300
  251.7 2.0 copy-start

commit v5 on v4

--- a/solution.py
+++ b/solution.py
@@ -245,12 +245,12 @@
 
 
 def first_kernel(
-    dp_size, x_ref, c_ref, entry_ref, exit_ref, shared_ref, ids_ref, vector_ref, cos_ref, sin_ref,
+    dp_size, x_ref, c_ref, entry_far, exit_far, shared_ref, ids_ref, vector_ref, cos_ref, sin_ref,
     xg_out, cg_out, a1_out, dh_out, up_out, small_out, kvw_out, ot_out,
-    dqt, pair_grad, norm_ref, ub_grad, big_own, y_land,
+    dqt, pair_grad, norm_ref, ub_grad, big_own, y_sum,
     xg, cg, a1, dh, up_w, small, kvw, ot, h, down_w, small_ref, up_ref, down_ref, pair_ref, vector_other, qb_ref, kvb_ref, big_land, a2,
     kvt, qt, dot_rows, kt, vt, k, v, dk, dv, s_ref, d_ref, l_ref, idr, tmp,
-    y_from, y_got, y_keep, g_send, g_recv, send, receive,
+    y_from, y_got, y_keep, g_send, g_recv, entry_ref, exit_ref, send, receive,
 ):
     place = Place(dp_size)
     rank, dp = (place.rank, place.dp)
@@ -267,6 +267,7 @@
     kept_outs = (xg_out, cg_out, a1_out, dh_out, up_out, small_out, kvw_out, ot_out)
     place.meet()
     vector_core = copies.remote(vector_ref, vector_other, place.core)
+    weight_loads = [copies.local(entry_far, entry_ref), copies.local(exit_far, exit_ref)]
 
     def swapped(source, target):
         return copies.swapped(source, target, place.is_swapped, place.swap)
@@ -304,6 +305,8 @@
         pair_ref[...] = shared_ref[...].astype(BF)
     for start, _ in first:
         start()
+    for copy in weight_loads:
+        copy.wait()
     if shares:
         small_ref[:query_width, :] = entry_ref[:query_width, :].astype(BF)
         small_ref[query_width:, :] = exit_ref[:query_width, :].astype(BF)
@@ -598,30 +601,17 @@
         at = slot - 2
         a2[at] = branches(slot).astype(BF)
         y_cores[at] = copies.remote(a2.at[at], y_from.at[at], place.core)
-    if shares:
-        sum_arrives(pieces - 2)
-        sum_arrives(2 * pieces - 2)
     branch = branches(1)
     y_cores[1].wait_recv()
     a2[2] = (branch + y_from[1].astype(F32)).astype(BF)
-    y_nexts = [
-        copies.remote(a2.at[2, span], y_got.at[span], place.next)
-        for at, span in enumerate(spans)
-    ]
+    y_next = copies.remote(a2.at[2], y_got, place.next)
     branch = branches(0)
     y_cores[0].wait_recv()
     y_keep[...] = branch + y_from[0].astype(F32)
-    y_homes = [swapped(a2.at[3, span], y_land.at[span]) for span in spans]
-
-    def y_arrives(at):
-        y_nexts[at].wait_recv()
-        span = spans[at]
-        a2[3, span, :] = (y_keep[span, :] + y_got[span, :].astype(F32)).astype(BF)
-        y_homes[at][0]()
-
-    later = [((0, 7), y_arrives, 0), ((1, 7), y_arrives, 1)]
-    if shares:
-        later += [((0, 5), sum_arrives, at) for at in (pieces - 1, 2 * pieces - 1)]
+    later = []
+    if shares:
+        for place_of, piece in (((0, 3), pieces - 2), ((0, 7), pieces - 1)):
+            later += [(place_of, sum_arrives, at) for at in (piece, pieces + piece)]
 
     dk[...] = jnp.zeros_like(dk)
     dv[...] = jnp.zeros_like(dv)
@@ -665,8 +655,8 @@
         pair_grad[0:HS, tokens] = rotate(key_grad, cos_ref[:, table], -sin_ref[:, table])
         pair_grad[HS:, tokens] = dv[tokens, :].T
 
-    for _, wait in y_homes:
-        wait()
+    y_next.wait_recv()
+    y_sum[...] = (y_keep[...] + y_got[...].astype(F32)).astype(BF)
     for copy in leaving:
         copy.wait()
 
@@ -716,7 +706,7 @@
     return pl.pallas_call(
         functools.partial(first_kernel, dp_size),
         out_shape=[jax.ShapeDtypeStruct(shape, kind) for shape, kind in outs],
-        in_specs=[vmem] * 9,
+        in_specs=[pl.BlockSpec(memory_space=pl.ANY)] * 4 + [vmem] * 5,
         out_specs=[pl.BlockSpec(memory_space=pl.ANY)] * 8 + [vmem] * (len(outs) - 8),
         scratch_shapes=[pltpu.VMEM(shape, kind) for shape, kind in outs[:8]]
         + [
@@ -750,6 +740,8 @@
             pltpu.VMEM((local, D), F32),
             pltpu.VMEM(held, BF),
             pltpu.VMEM(held, BF),
+            pltpu.VMEM(entry.shape, entry.dtype),
+            pltpu.VMEM(leave.shape, leave.dtype),
             pltpu.SemaphoreType.DMA((copies,)),
             pltpu.SemaphoreType.DMA((copies,)),
         ],
@@ -774,6 +766,10 @@
     return column_sum(jnp.where(down == along, column, 0.0))
 
 
+def as_row(array):
+    return array.reshape(1, -1) if array.ndim == 1 else array
+
+
 def gap_of(grad, weight, first, second, anchor, rate, decay):
     return anchor - adamw_update(weight, first, second, grad, rate, decay)[2]
 
@@ -784,22 +780,28 @@
     def take(number):
         return [next(refs) for _ in range(number)]
 
-    late = take(5 + (8 if shares else 0))
-    xg, dh, up_w, small, kvw, ot, dqt, pair_grad, norm_ref, ub_grad = take(10)
+    late = take(3)
+    xg_far, dh_far, ot_far = take(3)
+    if shares:
+        entry, leave = (take(4), take(4))
+    y_sum, up_w, small, kvw, dqt, pair_grad, norm_ref, ub_grad = take(8)
     if shares:
         shared, vector = (take(4) for _ in range(2))
-    grad_ref, small_own, vector_row, shared_home, pair_parts = take(5)
+    u_land, y_land, small_own, vector_row, shared_home, pair_parts = take(6)
     if shares:
         entry_sum, exit_sum, shared_sum, vector_sum = take(4)
-    u_land, small_land, vector_home, stats, v_next, v_core, v_dp, s_core, s_next, s_dp = take(10)
-    u_core, u_from, u_next, u_got, u_keep, u_home, p_from, p_next, p_got, full, g_send, g_recv = take(12)
+    small_land, vector_home, stats, v_next, v_core, v_dp, s_core, s_next, s_dp = take(9)
+    part_core, part_from = take(2)
+    u_next, u_got, u_keep, u_home = take(4)
+    p_from, p_next, p_got, full, g_send, g_recv = take(6)
     if shares:
         wide_buffers = [take(4), take(4)]
         small_buffers = [take(4), take(4)]
         shared_buffers, vector_buffers = (take(4), take(4))
-    held = take(len(late))
-    x_ref, c_ref, cg, a1, big_g = held[:5]
-    entry, leave = (held[5:9], held[9:])
+        wide_held = take(4)
+        small_held = [take(4), take(4)]
+    cg, a1, big_g = take(3)
+    xg, dh, ot = take(3)
     send, receive = take(2)
 
     place = Place(dp_size)
@@ -809,7 +811,28 @@
     columns = small_own.shape[1]
     query_width = ot.shape[0]
     place.meet([place.across])
-    loads = [copies.local(source, target) for source, target in zip(late, held)]
+    slot_loads = {
+        slot: [
+            copies.local(far.at[slot], near.at[slot]) for far, near in ((dh_far, dh), (xg_far, xg))
+        ]
+        for slot in (3, 2, 1, 0)
+    }
+    loads = [copies.local(source, target) for source, target in zip(late, (cg, a1, big_g))]
+    ot_load = copies.local(ot_far, ot)
+    if shares:
+        rest = pl.ds(query_width, wide)
+        first_rows = pl.ds(0, query_width)
+        wide_loads = [copies.local(ref.at[rest], to) for ref, to in zip(entry, wide_held)]
+        small_loads = [
+            copies.local(ref.at[first_rows], to)
+            for olds, tos in zip((entry, leave), small_held)
+            for ref, to in zip(olds, tos)
+        ]
+    def sent_home(source, target):
+        return copies.swapped(source, target, place.is_swapped, place.swap)
+
+    y_home = sent_home(y_sum, y_land)
+    y_home[0]()
     pair_core = copies.remote(pair_grad.at[:, pl.ds(2 * local, 2 * local)], p_from, place.core)
     stats[...] = jnp.zeros_like(stats)
 
@@ -819,6 +842,8 @@
         return centered * lax.rsqrt(jnp.mean(centered * centered, -1, keepdims=True) + NORM_EPS)
 
     def joined_of(slot):
+        for copy in slot_loads[slot]:
+            copy.wait()
         tokens = pl.ds(slot * local, local)
         first = dot_tn(dqt[:, tokens], small[:query_width, :])
         second = dot(dh[slot], up_w[...])
@@ -829,12 +854,10 @@
         stats[3:4, :D] += column_sum(second)
         return first * norm_ref[0:1, :] + second * norm_ref[2:3, :]
 
-    def sent_home(source, target):
-        return copies.swapped(source, target, place.is_swapped, place.swap)
-
     class GroupSum:
         def __init__(self, olds, grads, total, start, grad_start, size, buffers):
             self.olds, self.grads, self.total, self.buffers = (olds, grads, total, buffers)
+            self.held = [pl.ds(pl.multiple_of(at * size, 8), size) for at in (place.half, 1 - place.half)]
             self.own, self.other = (
                 pl.ds(pl.multiple_of(start + at * size, 8), size) for at in (place.half, 1 - place.half)
             )
@@ -843,15 +866,15 @@
                 for at in (place.half, 1 - place.half)
             )
 
-        def gap(self, span, grad_span):
-            olds = (ref[span, :] for ref in self.olds)
+        def gap(self, at, grad_span):
+            olds = (ref[self.held[at], :] for ref in self.olds)
             return gap_of(self.grads[grad_span, :], *olds, MATRIX_RATE, MATRIX_DECAY)
 
         def to_core(self):
             sent, got = self.buffers[:2]
-            sent[...] = self.gap(self.other, self.grad_other)
+            sent[...] = self.gap(1, self.grad_other)
             self.copy = copies.remote(sent, got, place.core)
-            self.total[self.own, :] = self.gap(self.own, self.grad_own)
+            self.total[self.own, :] = self.gap(0, self.grad_own)
 
         def to_chip(self):
             self.copy.wait_recv()
@@ -871,70 +894,32 @@
     u_cores = {}
     for slot in (3, 2):
         at = slot - 2
-        u_core[at] = joined_of(slot).astype(BF)
-        u_cores[at] = copies.remote(u_core.at[at], u_from.at[at], place.core)
+        part_core[at] = joined_of(slot).astype(BF)
+        u_cores[at] = copies.remote(part_core.at[at], part_from.at[at], place.core)
     pair_core.wait_recv()
     p_next[...] = pair_grad[:, local : 2 * local] + p_from[:, local:]
     pair_next = copies.remote(p_next, p_got, place.next)
     joined = joined_of(1)
     u_cores[1].wait_recv()
-    u_next[...] = (joined + u_from[1].astype(F32)).astype(BF)
-    u_nexts = [
-        copies.remote(u_next.at[span], u_got.at[span], place.next, starts=at == 0)
-        for at, span in enumerate(spans)
-    ]
-    wide_sums, small_sums = ([], [])
-    if shares:
-        half = wide // 2
-        for copy in loads[4:]:
-            copy.wait()
-        for olds, start, total, buffers in (
-            (entry, 0, entry_sum, wide_buffers[0]),
-            (leave, wide, exit_sum, wide_buffers[1]),
-        ):
-            wide_sums.append(GroupSum(olds, big_g, total, query_width, start, half, buffers))
-            wide_sums[-1].to_core()
-
-    if not shares:
-        loads[4].wait()
-    loads[2].wait()
-    loads[3].wait()
-    turned = 0.0
-    turned_out = 0.0
-    for slot in range(4):
-        tokens = pl.ds(slot * local, local)
-        turned = turned + dot(dqt[:, tokens], a1[slot])
-        turned_out = turned_out + dot(ot[:, tokens], cg[slot])
-    if shares:
-        full[:query_width, :] = turned
-        full[query_width:, :] = turned_out
-        other = pl.ds(pl.multiple_of((1 - place.dp) * columns, 128), columns)
-        g_send[...] = full[:, other].astype(BF)
-        small_sum = copies.remote(g_send, g_recv, place.dp_peers[0])
-        small_home = copies.homeward(g_send, small_land, place.swap)
-        small_own[...] = full[:, pl.ds(pl.multiple_of(place.dp * columns, 128), columns)]
-        for part in wide_sums:
-            part.to_chip()
-    else:
-        small_own[:query_width, :] = turned
-        small_own[query_width:, :] = turned_out
-
+    u_next[...] = (joined + part_from[1].astype(F32)).astype(BF)
+    u_nexts = [copies.remote(u_next.at[span], u_got.at[span], place.next) for span in spans]
     joined = joined_of(0)
     u_cores[0].wait_recv()
+    joined = joined + part_from[0].astype(F32)
     pair_next.wait_recv()
     pair_sum = (pair_grad[:, :local] + p_from[:, :local] + p_got[...]).astype(BF)
     through_pair = dot_nt(pair_sum.T, kvw[...])
-    u_keep[...] = joined + u_from[0].astype(F32) + through_pair * norm_ref[0:1, :]
+    u_keep[...] = joined + through_pair * norm_ref[0:1, :]
     u_homes = [sent_home(u_home.at[span], u_land.at[span]) for span in spans]
 
-    def u_arrives(at):
-        u_nexts[at].wait_recv()
-        if at == 0:
-            u_nexts[1].start()
+    def arrives(nexts, keep, got, home, homes, at):
+        nexts[at].wait_recv()
         span = spans[at]
-        u_home[span, :] = (u_keep[span, :] + u_got[span, :].astype(F32)).astype(BF)
-        u_homes[at][0]()
-
+        home[span, :] = (keep[span, :] + got[span, :].astype(F32)).astype(BF)
+        homes[at][0]()
+
+    loads[0].wait()
+    loads[1].wait()
     stats[0:1, :D] += column_sum(through_pair * normal_of(0))
     stats[1:2, :D] += column_sum(through_pair)
     stats[4:5, :D] = column_sum(cg[0].astype(F32))
@@ -946,17 +931,25 @@
     pair_parts[...] = dot(pair_sum, a1[0]).T.reshape(pair_parts.shape)
     if sums_pair:
         shared_core = copies.remote(pair_parts, s_core, place.core)
-    u_arrives(0)
-    if shares:
-        small_sum.wait_recv()
-        copies.sent(small_sum)
-        total = small_own[...] + g_recv[...].astype(F32)
-        small_own[...] = total
-
-        @pl.when(place.is_swapped)
-        def _():
-            g_send[...] = total.astype(BF)
-            small_home.start()
+
+    ot_load.wait()
+    turned = 0.0
+    turned_out = 0.0
+    for slot in range(4):
+        tokens = pl.ds(slot * local, local)
+        turned = turned + dot(dqt[:, tokens], a1[slot])
+        turned_out = turned_out + dot(ot[:, tokens], cg[slot])
+    if shares:
+        full[:query_width, :] = turned
+        full[query_width:, :] = turned_out
+        other = pl.ds(pl.multiple_of((1 - place.dp) * columns, 128), columns)
+        g_send[...] = full[:, other].astype(BF)
+        small_sum = copies.remote(g_send, g_recv, place.dp_peers[0])
+        small_home = copies.homeward(g_send, small_land, place.swap)
+        small_own[...] = full[:, pl.ds(pl.multiple_of(place.dp * columns, 128), columns)]
+    else:
+        small_own[:query_width, :] = turned
+        small_own[query_width:, :] = turned_out
 
     vector_core.wait_recv()
     copies.sent(vector_core)
@@ -970,9 +963,32 @@
             copies.remote(pair_parts.at[at * 4 + flip_one(place.rank)], s_next.at[at], place.next)
             for at in range(dp_size)
         ]
-    for part in wide_sums:
-        part.back()
-    u_arrives(1)
+    wide_sums, small_sums = ([], [])
+    loads[2].wait()
+    if shares:
+        half = wide // 2
+        for copy in wide_loads:
+            copy.wait()
+        wide_sums.append(
+            GroupSum(wide_held, big_g, entry_sum, query_width, 0, half, wide_buffers[0])
+        )
+        wide_sums[0].to_core()
+        wide_loads = [copies.local(ref.at[rest], to) for ref, to in zip(leave, wide_held)]
+
+    if shares:
+        wide_sums[0].to_chip()
+        small_sum.wait_recv()
+        copies.sent(small_sum)
+        total = small_own[...] + g_recv[...].astype(F32)
+        small_own[...] = total
+
+        @pl.when(place.is_swapped)
+        def _():
+            g_send[...] = total.astype(BF)
+            small_home.start()
+
+    u_move = functools.partial(arrives, u_nexts, u_keep, u_got, u_home, u_homes)
+    u_move(0)
     vector_next.wait_recv()
     copies.sent(vector_next)
     stats[...] = stats[...] + v_next[...]
@@ -987,6 +1003,7 @@
             copies.remote(s_next.at[(place.dp + at + 1) % dp_size], s_dp.at[at], peer)
             for at, peer in enumerate(place.dp_peers)
         ]
+    u_move(1)
     for copy in vector_dp:
         copy.wait_recv()
         copies.sent(copy)
@@ -1007,6 +1024,13 @@
         start()
 
     if shares:
+        for copy in wide_loads:
+            copy.wait()
+        wide_sums.append(
+            GroupSum(wide_held, big_g, exit_sum, query_width, wide, half, wide_buffers[1])
+        )
+        wide_sums[1].to_core()
+        wide_sums[0].back()
 
         @pl.when(place.is_swapped)
         def _():
@@ -1014,34 +1038,19 @@
             small_home.wait_recv()
             small_own[...] = small_land[...].astype(F32)
 
+        wide_sums[1].to_chip()
+        for copy in small_loads:
+            copy.wait()
         size = query_width // 2
         for olds, start, total, buffers in (
-            (entry, 0, entry_sum, small_buffers[0]),
-            (leave, query_width, exit_sum, small_buffers[1]),
+            (small_held[0], 0, entry_sum, small_buffers[0]),
+            (small_held[1], query_width, exit_sum, small_buffers[1]),
         ):
             small_sums.append(GroupSum(olds, small_own, total, 0, start, size, buffers))
             small_sums[-1].to_core()
         for part in small_sums:
             part.to_chip()
 
-    loads[0].wait()
-    loads[1].wait()
-
-    def end_rows(at):
-        u_homes[at][1]()
-        span = spans[at]
-        inputs = x_ref[span, :].astype(F32)
-        centered = inputs - jnp.mean(inputs, -1, keepdims=True)
-        scale = lax.rsqrt(jnp.mean(centered * centered, -1, keepdims=True) + NORM_EPS)
-        normal = centered * scale
-        joined = u_land[span, :].astype(F32)
-        grad_ref[span, :] = c_ref[span, :].astype(F32) + scale * (
-            joined
-            - jnp.mean(joined, -1, keepdims=True)
-            - normal * jnp.mean(joined * normal, -1, keepdims=True)
-        )
-
-    end_rows(0)
     for _, wait in late_homes:
         wait()
     part = query_width + wide
@@ -1055,15 +1064,14 @@
             (vector, vector_row, vector_buffers, VECTOR_RATE, 0.0),
             (shared, shared_home, shared_buffers, MATRIX_RATE, MATRIX_DECAY),
         ):
-            buffers[0][...] = gap_of(grads[...], *(ref[...] for ref in olds), rate, decay)
+            buffers[0][...] = gap_of(grads[...], *(as_row(ref[...]) for ref in olds), rate, decay)
             whole_sums.append(copies.remote(buffers[0], buffers[1], place.core))
         for at, buffers in enumerate((vector_buffers, shared_buffers)):
             whole_sums[at].wait_recv()
             buffers[2][...] = buffers[0][...] + buffers[1][...]
             whole_sums[at] = copies.remote(buffers[2], buffers[3], place.across)
-    end_rows(1)
-    if shares:
-        for part in small_sums:
+    if shares:
+        for part in wide_sums[1:] + small_sums:
             part.back()
         for copy, buffers, total in (
             (whole_sums[0], vector_buffers, vector_sum),
@@ -1073,13 +1081,14 @@
             total[...] = buffers[2][...] + buffers[3][...]
         for part in wide_sums + small_sums:
             part.copy.wait_recv()
+    for _, wait in u_homes + [y_home]:
+        wait()
     copies.finish()
 
 
 def second_pass(dp_size, late, arrays, olds, piece):
-    x = late[0]
-    up_w, small = arrays[2:4]
-    local = x.shape[0]
+    up_w, small = arrays[1:3]
+    local = arrays[0].shape[0]
     width = small.shape[0]
     query_width = width // 2
     wide = up_w.shape[0]
@@ -1090,9 +1099,9 @@
     parts = (4 * dp_size, piece, 2 * HS) if sums_pair else (1, D, 2 * HS)
     own = (piece if sums_pair else 8, 2 * HS)
     vector = (1, 6 * D + 2 * HS + 4 * (query_width + wide))
-    outs = [(local, D), (width, columns), vector, own, parts]
+    outs = [((local, D), BF)] * 2
+    outs += [(shape, F32) for shape in ((width, columns), vector, own, parts)]
     scratch = [
-        ((local, D), BF),
         (held, BF),
         ((16, 1024), F32),
         ((16, 1024), F32),
@@ -1116,22 +1125,24 @@
         (held, BF),
     ]
     if shares:
-        outs += [olds[0].shape, olds[4].shape, own, vector]
+        outs += [(shape, F32) for shape in (olds[0].shape, olds[4].shape, own, vector)]
         for size in (wide // 2, wide // 2, query_width // 2, query_width // 2):
             scratch += [((size, columns), kind) for kind in (F32, F32, BF, BF)]
         scratch += [(own, F32)] * 4 + [(vector, F32)] * 4
+        scratch += [((wide, columns), F32)] * 4 + [((query_width, columns), F32)] * 8
+    scratch += [(array.shape, array.dtype) for array in late]
     late = list(late) + list(olds[:8])
-    scratch += [(array.shape, array.dtype) for array in late]
     arrays = late + list(arrays) + list(olds[8:])
     vmem = pl.BlockSpec(memory_space=pltpu.VMEM)
     work = 4 * local * D * D
-    semaphores = pltpu.SemaphoreType.DMA((72 + 3 * dp_size,))
+    semaphores = pltpu.SemaphoreType.DMA((80 + 3 * dp_size,))
     return pl.pallas_call(
         functools.partial(second_kernel, dp_size, sums_pair, shares),
-        out_shape=[jax.ShapeDtypeStruct(shape, F32) for shape in outs],
+        out_shape=[jax.ShapeDtypeStruct(shape, kind) for shape, kind in outs],
         in_specs=[pl.BlockSpec(memory_space=pl.ANY)] * len(late) + [vmem] * (len(arrays) - len(late)),
         out_specs=[vmem] * len(outs),
-        scratch_shapes=[pltpu.VMEM(shape, kind) for shape, kind in scratch] + [semaphores] * 2,
+        scratch_shapes=[pltpu.VMEM(shape, kind) for shape, kind in scratch]
+        + [semaphores, semaphores],
         compiler_params=pltpu.CompilerParams(
             collective_id=1, has_side_effects=True, vmem_limit_bytes=60 << 20
         ),
@@ -1146,19 +1157,36 @@
     def take(number):
         return [next(refs) for _ in range(number)]
 
+    x_ref, c_ref, u_ref, y_ref, bias_ref = take(5)
     grads = [take(2), take(2), take(1), take(1)]
     olds = [take(6) for _ in range(4)]
+    out_ref, grad_ref = take(2)
     news = [take(6) for _ in range(4)]
     step = pl.program_id(0)
 
+    @pl.when(step < 4)
+    def _():
+        inputs = x_ref[...].astype(F32)
+        centered = inputs - jnp.mean(inputs, -1, keepdims=True)
+        scale = lax.rsqrt(jnp.mean(centered * centered, -1, keepdims=True) + NORM_EPS)
+        normal = centered * scale
+        joined = u_ref[...].astype(F32)
+        grad_ref[...] = c_ref[...].astype(F32) + scale * (
+            joined
+            - jnp.mean(joined, -1, keepdims=True)
+            - normal * jnp.mean(joined * normal, -1, keepdims=True)
+        )
+        bias = bias_ref[:, 4 * D : 5 * D] + bias_ref[:, 5 * D : 6 * D]
+        out_ref[...] = inputs + y_ref[...].astype(F32) + bias
+
     def update(at, grad, rate, decay):
-        weight, first, second, anchor, velocity, total = (ref[...] for ref in olds[at])
+        weight, first, second, anchor, velocity, total = (as_row(ref[...]) for ref in olds[at])
         first, second, weight = adamw_update(weight, first, second, grad, rate, decay)
         change = total / groups
         momentum = OUTER_BETA * velocity + change
         outer = anchor - OUTER_RATE * (change + OUTER_BETA * momentum)
         for ref, value in zip(news[at], (first, second, weight, change, momentum, outer)):
-            ref[...] = value
+            ref[...] = value.reshape(ref.shape)
 
     for at in range(2):
         head, rest = grads[at]
@@ -1170,7 +1198,7 @@
         update(3, grads[3][0][...], VECTOR_RATE, 0.0)
 
 
-def third_pass(groups, big, small, shared_grad, vector_grad, entry, leave, shared, vector):
+def third_pass(groups, x, c, u, y, big, small, shared_grad, vector_grad, entry, leave, shared, vector):
     rows, columns = entry[0].shape
     size = small.shape[0] // 2
     wide = rows // size - 1
@@ -1179,9 +1207,10 @@
         return pl.BlockSpec((size, columns), index)
 
     def all_of(array):
-        return pl.BlockSpec(array.shape, lambda i: (0, 0))
+        return pl.BlockSpec(array.shape, lambda i: (0,) * array.ndim)
 
     here = block(lambda i: (i, 0))
+    tokens = pl.BlockSpec((x.shape[0] // 4, D), lambda i: (jnp.minimum(i, 3), 0))
     grad_specs = [
         block(lambda i: (0, 0)),
         block(lambda i: (jnp.maximum(i - 1, 0), 0)),
@@ -1191,18 +1220,20 @@
         all_of(vector_grad),
     ]
     specs = [here] * 12 + [all_of(array) for array in shared + vector]
-    out_specs = [here] * 12 + [all_of(shared[0])] * 6 + [all_of(vector[0])] * 6
-    outs = [array for array in (entry[0], leave[0], shared[0], vector[0]) for _ in range(6)]
+    out_specs = [tokens] * 2 + [here] * 12 + [all_of(shared[0])] * 6 + [all_of(vector[0])] * 3
+    out_specs += [all_of(vector[3])] * 3
+    outs = [x, x] + [array for array in (entry[0], leave[0], shared[0]) for _ in range(6)]
+    outs += [vector[0]] * 3 + [vector[3]] * 3
     return pl.pallas_call(
         functools.partial(third_kernel, groups),
         grid=(rows // size,),
         out_shape=[jax.ShapeDtypeStruct(array.shape, F32) for array in outs],
-        in_specs=grad_specs + specs,
+        in_specs=[tokens] * 4 + [all_of(vector[0])] + grad_specs + specs,
         out_specs=out_specs,
         compiler_params=pltpu.CompilerParams(vmem_limit_bytes=60 << 20),
         cost_estimate=pl.CostEstimate(flops=1 << 26, bytes_accessed=40 << 20, transcendentals=1 << 20),
         name="update_weights",
-    )(small, big, small, big, shared_grad, vector_grad, *entry, *leave, *shared, *vector)
+    )(x, c, u, y, vector[0], small, big, small, big, shared_grad, vector_grad, *entry, *leave, *shared, *vector)
 
 
 def shards(
@@ -1260,14 +1291,14 @@
     leave += [exit_anchor, exit_velocity]
     shared = [array[0] for array in (shared_weight, shared_first, shared_second)]
     shared += [shared_anchor, shared_velocity]
-    vector = [vector_weight, vector_first, vector_second, vector_anchor[None], vector_velocity[None]]
+    vector = [vector_weight, vector_first, vector_second, vector_anchor, vector_velocity]
     shares = dp_size == 2 and leave[0].shape[1] % 128 == 0 and piece % 16 == 0
     weights = [entry[0], leave[0]]
     if not shares:
         weights = [gather_dp(swapped_parts(array.astype(BF)), 1) for array in weights]
     (
-        inputs, cots, attn_input, hidden_grad, up_w, small, pair_weight, attended, query_grad,
-        pair_rows, norms, up_bias_rows, big_grad, branch_home,
+        inputs, cots, attn_input, hidden_grad, up_w, small, pair_weight, attended,
+        query_grad, pair_rows, norms, up_bias_rows, big_grad, branch,
     ) = first_pass(
         dp_size,
         hidden_in[0],
@@ -1279,16 +1310,13 @@
         cosine_table,
         sine_table,
     )
-    home_bias = vector_weight[0, 4 * D : 5 * D] + vector_weight[0, 5 * D : 6 * D]
-    block_output = hidden_in[0].astype(F32) + branch_home.astype(F32) + home_bias
-    late = (hidden_in[0], out_cotangent[0], cots, attn_input, big_grad)
     arrays = (
-        inputs, hidden_grad, up_w, small, pair_weight.reshape(D, 2 * HS), attended, query_grad,
+        branch, up_w, small, pair_weight.reshape(D, 2 * HS), query_grad,
         pair_rows, norms, up_bias_rows,
     )
     olds = [array for arrays in (entry, leave, shared, vector) for array in arrays[:4]]
-    input_grad, small_grad, vector_grad, shared_grad, pair_parts, *totals = second_pass(
-        dp_size, late, arrays, olds if shares else [], piece
+    joined, branch, small_grad, vector_grad, shared_grad, pair_parts, *totals = second_pass(
+        dp_size, (cots, attn_input, big_grad, inputs, hidden_grad, attended), arrays, olds if shares else [], piece
     )
     if not shares:
         big_grad, small_grad = (
@@ -1310,21 +1338,20 @@
                 *leave[:4], MATRIX_RATE, MATRIX_DECAY,
             ),
             gap_of(shared_grad, *shared[:4], MATRIX_RATE, MATRIX_DECAY),
-            gap_of(vector_grad, *vector[:4], VECTOR_RATE, 0.0),
+            gap_of(vector_grad, *vector[:3], vector_anchor[None], VECTOR_RATE, 0.0),
         )
         totals = lax.psum(gaps, "group")
-    updated = third_pass(
-        groups, big_grad, small_grad, shared_grad, vector_grad,
+    block_output, input_grad, *updated = third_pass(
+        groups, hidden_in[0], out_cotangent[0], joined, branch, big_grad, small_grad, shared_grad, vector_grad,
         *(arrays + [total] for arrays, total in zip((entry, leave, shared, vector), totals)),
     )
-    updated = list(updated)
     results = [block_output[None], input_grad[None]]
     for at in range(3):
         own = updated[6 * at : 6 * at + 6]
         if at == 0:
             own = [array.T for array in own]
         results += [array[None] for array in own[:3]] + own[3:]
-    results += updated[18:21] + [array[0] for array in updated[21:24]]
+    results += updated[18:24]
     return tuple(results)
 
 

time: 259 us -> 248 us (0.958)
  other arithmetic: 6.44 us -> 0 us
  local copies, waits for them, and re-layouts: 3.06 us -> 0 us
    pallas_call x1, Pallas kernels: 164 us -> 148 us  [first_pass(): pl.pallas_call(functools.partial(first_kernel, dp_size), out_shape=[jax.S...]
    pallas_call x1, Pallas kernels: 64.4 us -> 74.7 us  [second_pass(): pl.pallas_call(functools.partial(second_kernel, dp_size, sums_pair, share...]
    pallas_call x3 -> x0, other arithmetic: 4.38 us -> none  [third_pass(): pl.pallas_call(functools.partial(third_kernel, groups), grid=(rows // siz...]
    pallas_call x1, Pallas kernels: 16.6 us -> 20 us  [third_pass(): pl.pallas_call(functools.partial(third_kernel, groups), grid=(rows // siz...]
where the time goes in v5:
time: 248 us; the launch traced here: 244 us
  Pallas kernels  243 us (98%)
    pallas_call x1, Pallas kernels, first_pass(): pl.pallas_call(functools.partial(first_kernel, dp_size), out_shape=[jax.S...  148 us
    pallas_call x1, Pallas kernels, second_pass(): pl.pallas_call(functools.partial(second_kernel, dp_size, sums_pair, share...  74.7 us
    pallas_call x1, Pallas kernels, third_pass(): pl.pallas_call(functools.partial(third_kernel, groups), grid=(rows // siz...  20 us

profile of v5, /device:TPU:1, one launch (start us, length us, event | category | flops | bytes accessed | tf_op | source)
XLA Modules:
  0.0 243.9 jit_solution(14557571915579935192)
XLA Ops:
  0.7 148.2 %gather_attend.1 = (bf16[4,512,768]{2,1,0:T(8,128)(2,1)}, bf16[4,512,768]{2,1,0:T(8,128)(2,1)}, bf16[4,512,768]{2,1,0:T(8,128)(2,1)}, bf16[4,512,768]{2,1,0:T(8,...) custom-call(bf16[512,768]{1,0:T(8,128)(2,1)} %bitcast.57, ...), custom_call_target="tpu_custom_call" | custom-call | flops 48318382080 | bytes 31457280 | tf_op jit(solution)/shard_map/gather_attend/pallas_call | solution.py:706
  148.9 74.7 %sum_branches.1 = (bf16[512,768]{1,0:T(8,128)(2,1)}, bf16[512,768]{1,0:T(8,128)(2,1)}, f32[384,384]{1,0:T(8,128)}, f32[1,8576]{1,0:T(1,128)}, f32[96,128]{1,0:T(...) custom-call(bf16[4,512,768]{2,1,0:T(8,128)(2,1)} %get-tuple-element., ...), custom_call_target="tpu_custom_call" | custom-call | flops 9663676416 | bytes 31457280 | tf_op jit(solution)/shard_map/sum_branches/pallas_call | solution.py:1139
  223.7 20.0 %update_weights.1 = (f32[512,768]{1,0:T(8,128)}, f32[512,768]{1,0:T(8,128)}, f32[960,384]{1,0:T(8,128)}, f32[960,384]{1,0:T(8,128)}, f32[960,384]{1,0:T(8,128)},...) custom-call(bf16[512,768]{1,0:T(8,128)(2,1)} %bitcast.58, ...), custom_call_target="tpu_custom_call" | custom-call | flops 67108864 | bytes 41943040 | tf_op jit(solution)/shard_map/update_weights/pallas_call | solution.py:1227

commit v6 on v5

--- a/solution.py
+++ b/solution.py
@@ -605,12 +605,15 @@
     y_cores[1].wait_recv()
     a2[2] = (branch + y_from[1].astype(F32)).astype(BF)
     y_next = copies.remote(a2.at[2], y_got, place.next)
+    if shares:
+        sum_arrives(pieces - 2)
+        sum_arrives(2 * pieces - 2)
     branch = branches(0)
     y_cores[0].wait_recv()
     y_keep[...] = branch + y_from[0].astype(F32)
     later = []
     if shares:
-        for place_of, piece in (((0, 3), pieces - 2), ((0, 7), pieces - 1)):
+        for place_of, piece in (((0, 6), pieces - 1),):
             later += [(place_of, sum_arrives, at) for at in (piece, pieces + piece)]
 
     dk[...] = jnp.zeros_like(dk)
@@ -902,8 +905,12 @@
     joined = joined_of(1)
     u_cores[1].wait_recv()
     u_next[...] = (joined + part_from[1].astype(F32)).astype(BF)
-    u_nexts = [copies.remote(u_next.at[span], u_got.at[span], place.next) for span in spans]
+    u_nexts = [
+        copies.remote(u_next.at[span], u_got.at[span], place.next, starts=at == 0)
+        for at, span in enumerate(spans)
+    ]
     joined = joined_of(0)
+    u_nexts[1].start()
     u_cores[0].wait_recv()
     joined = joined + part_from[0].astype(F32)
     pair_next.wait_recv()

time: 248 us -> 248 us (level)
  no operation moved by 1% of the time
where the time goes in v6:
time: 248 us; the launch traced here: 244 us
  Pallas kernels  243 us (98%)
    pallas_call x1, Pallas kernels, first_pass(): pl.pallas_call(functools.partial(first_kernel, dp_size), out_shape=[jax.S...  148 us
    pallas_call x1, Pallas kernels, second_pass(): pl.pallas_call(functools.partial(second_kernel, dp_size, sums_pair, share...  74.5 us
    pallas_call x1, Pallas kernels, third_pass(): pl.pallas_call(functools.partial(third_kernel, groups), grid=(rows // siz...  20 us

profile of v6, /device:TPU:1, one launch (start us, length us, event | category | flops | bytes accessed | tf_op | source)
XLA Modules:
  0.0 243.7 jit_solution(9120413916267038186)
XLA Ops:
  0.7 148.3 %gather_attend.1 = (bf16[4,512,768]{2,1,0:T(8,128)(2,1)}, bf16[4,512,768]{2,1,0:T(8,128)(2,1)}, bf16[4,512,768]{2,1,0:T(8,128)(2,1)}, bf16[4,512,768]{2,1,0:T(8,...) custom-call(bf16[512,768]{1,0:T(8,128)(2,1)} %bitcast.57, ...), custom_call_target="tpu_custom_call" | custom-call | flops 48318382080 | bytes 31457280 | tf_op jit(solution)/shard_map/gather_attend/pallas_call | solution.py:709
  148.9 74.5 %sum_branches.1 = (bf16[512,768]{1,0:T(8,128)(2,1)}, bf16[512,768]{1,0:T(8,128)(2,1)}, f32[384,384]{1,0:T(8,128)}, f32[1,8576]{1,0:T(1,128)}, f32[96,128]{1,0:T(...) custom-call(bf16[4,512,768]{2,1,0:T(8,128)(2,1)} %get-tuple-element., ...), custom_call_target="tpu_custom_call" | custom-call | flops 9663676416 | bytes 31457280 | tf_op jit(solution)/shard_map/sum_branches/pallas_call | solution.py:1146
  223.4 20.0 %update_weights.1 = (f32[512,768]{1,0:T(8,128)}, f32[512,768]{1,0:T(8,128)}, f32[960,384]{1,0:T(8,128)}, f32[960,384]{1,0:T(8,128)}, f32[960,384]{1,0:T(8,128)},...) custom-call(bf16[512,768]{1,0:T(8,128)(2,1)} %bitcast.58, ...), custom_call_target="tpu_custom_call" | custom-call | flops 67108864 | bytes 41943040 | tf_op jit(solution)/shard_map/update_weights/pallas_call | solution.py:1234
